TPU v7x, 512 devices: a whole 4x4x16 slice. The times are simulated.
512 devices in a mesh: blk: 32 (over x, z_lo), grp: 16 (over y, z_hi, core).
Axes of the slice: x: 4, y: 4, z: 16 (z_hi: 2, z_lo: 8; z = z_hi * 8 + z_lo), core: 2. Of those that a mesh axis runs over, the one named last changes fastest.
Arguments:
- fluid_vel: float32 [3, 1024, 16, 256], P(None, ('blk', 'grp')), may hold values from -6 to 6
- pressure: float32 [1024, 16, 256], P(('blk', 'grp')), may hold values from -6 to 6
- parcel_vel: float32 [3, 4194304], P(None, ('blk', 'grp')), may hold values from -6 to 6
- parcel_vol: float32 [4194304], P(('blk', 'grp')), may hold values from 0.02 to 0.2
- parcel_rate: float32 [4194304], P(('blk', 'grp')), may hold values from 0.2 to 5
- cell_local: int32 [4194304], P(('blk', 'grp')), may hold values from 0 to 2047
- tile_block: int32 [16384], P(('blk', 'grp')), may hold values from 0 to 63
- parcel_count: int32 [512], P(('blk', 'grp')), may hold values from 2048 to 8192, as said below
- leave_lists: int32 [2, 131072], P(None, ('blk', 'grp')), may hold values from 0 to 8191, as said below
- mig_counts: int32 [2, 512], P(None, ('blk', 'grp')), may hold values from 1 to 256, as said below
Outputs:
- fluid_next: float32 [3, 1024, 16, 256], P(None, ('blk', 'grp'))
- pressure_next: float32 [1024, 16, 256], P(('blk', 'grp'))
- parcel_next: float32 [3, 4194304], P(None, ('blk', 'grp'))
- arrivals: float32 [2, 5, 131072], P(None, None, ('blk', 'grp'))
Inputs may be any that keep to these rules, and one draw needn't show every extreme that they name: `parcel_count`: one device, drawn from the seed, holds 8192 live parcels. `leave_lists`: every listed slot is live on its device, and the 512 slots of one device are distinct; entries past the count are ignored. `mig_counts`: in each list, some device drawn from the seed uses all 256 entries.
All inputs are finite; a program needn't handle non-finite values.
Results may differ from a plain program's by a relative error of at most 0.0013.
Values may be sent and summed in bfloat16 or wider, within the bound.
No kernel may reach another device: no remote copies, remote signals or barrier semaphores. Data moves between devices by JAX's collectives and lax.ppermute only.
A program may use at most 64 MiB of HBM per device.

v0:
```python
import jax
import jax.numpy as jnp
from jax import lax
from jax.sharding import PartitionSpec as P

PCAP = 8192
TP = 256
BLOCK = 2048
RADIAL = 16
LINE = 256
PL_DEV = 2
SWEEPS = 2
MIG = 256


DT = 0.2
NU = 0.5
group_tiles = 8


def padded(cells, sides, width):
    for axis, dim in sides:
        count = lax.axis_size(axis)
        head = lax.slice_in_dim(cells, 0, width, axis=dim)
        tail = lax.slice_in_dim(cells, cells.shape[dim] - width, cells.shape[dim], axis=dim)
        cells = jnp.concatenate(
            [
                lax.ppermute(tail, axis, [(i, (i + 1) % count) for i in range(count)]),
                cells,
                lax.ppermute(head, axis, [((i + 1) % count, i) for i in range(count)]),
            ],
            axis=dim,
        )
    return cells


def passed_along(block, axis, distance):
    devices = range(lax.axis_size(axis))
    route = [((i - distance) % len(devices), i) for i in devices]
    return lax.ppermute(block, axis, route)


def rad_up(values):
    return jnp.concatenate([values[..., 1:, :], jnp.zeros_like(values[..., :1, :])], axis=-2)


def rad_down(values):
    return jnp.concatenate([jnp.zeros_like(values[..., :1, :]), values[..., :-1, :]], axis=-2)


def axial_up(values):
    return jnp.concatenate([values[..., 1:], jnp.zeros_like(values[..., :1])], axis=-1)


def axial_down(values):
    return jnp.concatenate([jnp.zeros_like(values[..., :1]), values[..., :-1]], axis=-1)


def laplace(extended):
    center = extended[..., 1:-1, :, :]
    return (
        extended[..., 2:, :, :]
        + extended[..., :-2, :, :]
        + rad_up(center)
        + rad_down(center)
        + axial_up(center)
        + axial_down(center)
        - 6.0 * center
    )


def gradient(extended):
    center = extended[..., 1:-1, :, :]
    return jnp.stack(
        [
            0.5 * (extended[..., 2:, :, :] - extended[..., :-2, :, :]),
            0.5 * (rad_up(center) - rad_down(center)),
            0.5 * (axial_up(center) - axial_down(center)),
        ]
    )


def divergence(extended):
    center = extended[:, 1:-1]
    return 0.5 * (
        extended[0, 2:]
        - extended[0, :-2]
        + rad_up(center[1])
        - rad_down(center[1])
        + axial_up(center[2])
        - axial_down(center[2])
    )


def jacobi(extended, source):
    center = extended[1:-1]
    return (
        extended[2:]
        + extended[:-2]
        + rad_up(center)
        + rad_down(center)
        + axial_up(center)
        + axial_down(center)
        - source / DT
    ) / 6.0


def predict(extended, deposits):
    porosity = 1.0 / (1.0 + deposits[0])
    velocity = extended[:3, 1:-1]
    momentum_rhs = NU * laplace(extended[:3]) - gradient(extended[3])
    u_star = (velocity + DT * momentum_rhs + DT * deposits[2:5] / porosity) / (
        1.0 + DT * deposits[1] / porosity
    )
    return (u_star, porosity)


def cycle_rims(values, width):
    return padded(values, ((("blk", "grp"), 1),), width)


def migrate(outgoing, offset):
    return passed_along(outgoing, "blk", offset)


def one_hot_tiles(local_ids):
    columns = lax.broadcasted_iota(jnp.int32, (1, 1, BLOCK), 2)
    return (local_ids[:, :, None] == columns).astype(jnp.bfloat16)


def per_device(
    fluid_vel,
    pressure,
    parcel_vel,
    parcel_vol,
    parcel_rate,
    cell_local,
    tile_block,
    parcel_count,
    leave_lists,
    mig_counts,
):
    members = lax.axis_size("grp")
    tile_count = PCAP // TP
    rounds = tile_count // group_tiles
    slab_planes = PL_DEV * members
    block_count = slab_planes * RADIAL * LINE // BLOCK
    slot_ids = jnp.arange(PCAP, dtype=jnp.int32)
    active = (slot_ids < parcel_count[0]).astype(jnp.float32)
    drag_coeff = parcel_vol * parcel_rate
    quantity = (
        jnp.concatenate([parcel_vol[None], drag_coeff[None], drag_coeff[None] * parcel_vel])
        * active[None]
    ).astype(jnp.bfloat16)
    local_rounds = cell_local.reshape(rounds, group_tiles, TP)
    quantity_rounds = quantity.reshape(5, rounds, group_tiles, TP).transpose(1, 0, 2, 3)

    def deposit_step(carry, inputs):
        local_ids, amounts = inputs
        onehot = one_hot_tiles(local_ids)
        return (
            carry,
            jnp.einsum("gtc,kgt->gkc", onehot, amounts, preferred_element_type=jnp.float32),
        )

    _, tile_sums = lax.scan(
        deposit_step, jnp.zeros((), jnp.float32), (local_rounds, quantity_rounds)
    )
    tile_sums = tile_sums.reshape(tile_count, 5, BLOCK)
    selector = (tile_block[:, None] == jnp.arange(block_count, dtype=jnp.int32)[None, :]).astype(
        jnp.float32
    )
    slab_sums = jnp.einsum("tb,tkc->kbc", selector, tile_sums, precision=lax.Precision.HIGHEST)
    slab_sums = slab_sums.reshape(5, slab_planes, RADIAL, LINE).transpose(1, 0, 2, 3)
    own_sums = lax.psum_scatter(slab_sums, "grp", scatter_dimension=0, tiled=True)
    deposits = own_sums.transpose(1, 0, 2, 3)
    extended = cycle_rims(jnp.concatenate([fluid_vel, pressure[None]]), 1)
    u_star, porosity = predict(extended, deposits)
    eps_flux = porosity * u_star
    source = divergence(cycle_rims(eps_flux, 1))
    pressure_now = pressure
    for sweep_index in range(SWEEPS):
        pressure_now = jacobi(cycle_rims(pressure_now[None], 1)[0], source)
    fluid_new = u_star - DT * gradient(cycle_rims(pressure_now[None], 1)[0])
    fields = lax.all_gather(
        jnp.concatenate([fluid_new, porosity[None]]).astype(jnp.bfloat16), "grp", axis=1, tiled=True
    )
    field_blocks = fields.reshape(4, block_count, BLOCK).transpose(1, 0, 2)
    tile_fields = field_blocks[tile_block].reshape(rounds, group_tiles, 4, BLOCK)

    def sample_step(carry, inputs):
        local_ids, block_values = inputs
        onehot = one_hot_tiles(local_ids)
        return (
            carry,
            jnp.einsum("gtc,gkc->kgt", onehot, block_values, preferred_element_type=jnp.float32),
        )

    _, sampled = lax.scan(sample_step, jnp.zeros((), jnp.float32), (local_rounds, tile_fields))
    sampled = sampled.transpose(1, 0, 2, 3).reshape(4, PCAP)
    coupling = parcel_rate / (sampled[3] * sampled[3])
    moved_vel = (parcel_vel + DT * coupling[None] * sampled[:3]) / (1.0 + DT * coupling[None])
    parcel_state = jnp.concatenate([moved_vel, parcel_vol[None], parcel_rate[None]]) * active[None]
    list_valid = (jnp.arange(MIG, dtype=jnp.int32)[None, :] < mig_counts).astype(jnp.float32)
    outgoing = jnp.take(parcel_state, leave_lists, axis=1).transpose(1, 0, 2) * list_valid[:, None]
    leaving = (
        jnp.zeros((PCAP,), jnp.float32).at[leave_lists.reshape(-1)].max(list_valid.reshape(-1))
    )
    from_above = migrate(outgoing[0], -1)
    from_below = migrate(outgoing[1], 1)
    parcel_next = moved_vel * active[None] * (1.0 - leaving)[None]
    return (fluid_new, pressure_now, parcel_next, jnp.stack([from_above, from_below]))


def solution(mesh):
    placed = (
        P(None, ("blk", "grp"), None, None),
        P(("blk", "grp"), None, None),
        P(None, ("blk", "grp")),
        P(("blk", "grp")),
        P(("blk", "grp")),
        P(("blk", "grp")),
        P(("blk", "grp")),
        P(("blk", "grp")),
        P(None, ("blk", "grp")),
        P(None, ("blk", "grp")),
    )
    return jax.shard_map(
        per_device,
        mesh=mesh,
        in_specs=placed,
        out_specs=(
            P(None, ("blk", "grp"), None, None),
            P(("blk", "grp"), None, None),
            P(None, ("blk", "grp")),
            P(None, None, ("blk", "grp")),
        ),
        check_vma=False,
    )
```

profile of v0, /device:TPU:1, one launch (start us, length us, event | category | flops | bytes accessed | tf_op | source)
XLA Modules:
  0.0 552.7 jit_solution(17676559459379361549)
XLA Ops:
  11.3 14.8 %while.20 = (s32[]{:T(128)}, f32[4,8,5,2048]{3,2,1,0:T(8,128)}, bf16[4,5,8,256]{3,1,2,0:T(8,128)(2,1)S(1)}, s32[4,8,256]{2,1,0:T(8,128)S(1)}, s32[]{:T(128)}) while((s32[]{:T(128)}, f32[4,8,5,2048]{3,2,1,0:T(8,128)}, bf16[4,5,8,256]{3,1,2,0:T(8,128)(2,1)S(1)}, s32[4,8,256]{2,1,0:T(8,128)S(1)}, s32[]{:T(128)}) %tuple.68), condition=%wide.region_1.2_spmd, body=%wide.region_0.1_spmd.sunk | while | flops 46137344 | bytes 582729 | solution.py:166
  11.3 3.7 fusion.95
  15.0 3.7 fusion.95
  18.7 3.7 fusion.95
  22.3 3.7 fusion.95
  26.0 3.7 convolution_bitcast_fusion
  32.4 16.8 %collective-permute-start.1 = (f32[4,1,16,256]{3,2,1,0:T(8,128)S(1)}, f32[4,1,16,256]{3,2,1,0:T(8,128)S(1)}, u32[]{:S(2)}, u32[]{:S(2)}) collective-permute-start(f32[4,1,16,256]{3,2,1,0:T(8,128)S(1)} %get-tuple-element.102), channel_id=1, source_target_pairs={{0,1},{1,2},{2,3},{3,4},{4,5},{5,6},{6,7},{7,8},{8,9},{9,10},{10,1... | collective-permute-start | bytes 196616 | tf_op jit(solution)/shard_map/ppermute | solution.py:28
  51.1 12.4 %collective-permute-start.3 = (f32[1,1,16,256]{3,2,1,0:T(8,128)S(1)}, f32[1,1,16,256]{3,2,1,0:T(8,128)S(1)}, u32[]{:S(2)}, u32[]{:S(2)}) collective-permute-start(f32[1,1,16,256]{3,2,1,0:T(8,128)S(1)} %get-tuple-element.128), channel_id=1, source_target_pairs={{0,1},{1,2},{2,3},{3,4},{4,5},{5,6},{6,7},{7,8},{8,9},{9,10},{10,1... | collective-permute-start | bytes 49160 | tf_op jit(solution)/shard_map/ppermute | solution.py:28
  67.7 295.6 %all-reduce.23.cloned.1.call-done = f32[32,5,16,256]{3,2,0,1:T(8,128)} async-done(((f32[32,5,16,256]{3,2,0,1:T(8,128)}), f32[32,5,16,256]{3,2,0,1:T(8,128)}) %all-reduce.23.cloned.1.call-update) | async-done | bytes 2621456
  364.5 7.8 %collective-permute-start.5 = (f32[3,1,16,256]{3,2,1,0:T(8,128)S(1)}, f32[3,1,16,256]{3,2,1,0:T(8,128)S(1)}, u32[]{:S(2)}, u32[]{:S(2)}) collective-permute-start(f32[3,1,16,256]{3,2,1,0:T(8,128)S(1)} %get-tuple-element.104), channel_id=1, source_target_pairs={{0,1},{1,2},{2,3},{3,4},{4,5},{5,6},{6,7},{7,8},{8,9},{9,10},{10,1... | collective-permute-start | bytes 147464 | tf_op jit(solution)/shard_map/ppermute | solution.py:28
  372.3 4.9 collective-permute-start.4
  377.2 9.2 %collective-permute-done.4 = f32[3,1,16,256]{3,2,1,0:T(8,128)S(1)} collective-permute-done((f32[3,1,16,256]{3,2,1,0:T(8,128)S(1)}, f32[3,1,16,256]{3,2,1,0:T(8,128)S(1)}, u32[]{:S(2)}, u32[]{:S(2)}) %collective-permute-start.4) | collective-permute-done | bytes 49184 | tf_op jit(solution)/shard_map/ppermute | solution.py:30
  390.9 11.3 %collective-permute-done.6 = f32[1,1,16,256]{3,2,1,0:T(8,128)S(1)} collective-permute-done((f32[1,1,16,256]{3,2,1,0:T(8,128)S(1)}, f32[1,1,16,256]{3,2,1,0:T(8,128)S(1)}, u32[]{:S(2)}, u32[]{:S(2)}) %collective-permute-start.6) | collective-permute-done | bytes 16416 | tf_op jit(solution)/shard_map/ppermute | solution.py:30
  406.9 11.3 %collective-permute-done.8 = f32[1,1,16,256]{3,2,1,0:T(8,128)S(1)} collective-permute-done((f32[1,1,16,256]{3,2,1,0:T(8,128)S(1)}, f32[1,1,16,256]{3,2,1,0:T(8,128)S(1)}, u32[]{:S(2)}, u32[]{:S(2)}) %collective-permute-start.8) | collective-permute-done | bytes 16416 | tf_op jit(solution)/shard_map/ppermute | solution.py:30
  419.6 3.3 scatter_custom_fusion
  423.0 84.0 %all-gather.2.cloned.1.call-done = bf16[4,32,16,256]{3,2,1,0:T(8,128)(2,1)} async-done(((bf16[4,2,16,256]{3,2,1,0:T(8,128)(2,1)}), bf16[4,32,16,256]{3,2,1,0:T(8,128)(2,1)}) %all-gather.2.cloned.1.call-update) | async-done | bytes 1048592 | tf_op jit(solution)/shard_map/all_gather | solution.py:185
  510.5 13.1 %while.21 = (s32[]{:T(128)}, f32[4,4,8,256]{3,1,2,0:T(4,128)S(1)}, bf16[4,8,4,2048]{3,2,1,0:T(4,128)(2,1)S(1)}, s32[4,8,256]{2,1,0:T(8,128)S(1)}, s32[]{:T(128)}) while((s32[]{:T(128)}, f32[4,4,8,256]{3,1,2,0:T(4,128)S(1)}, bf16[4,8,4,2048]{3,2,1,0:T(4,128)(2,1)S(1)}, s32[4,8,256]{2,1,0:T(8,128)S(1)}, s32[]{:T(128)}) %tuple.79), condition=%wide.region_4.5_spmd, body=%wide.region_3.4_spmd.sunk | while | flops 37748736 | bytes 189513 | solution.py:199
  510.5 3.3 fusion.97
  513.8 3.3 fusion.97
  517.0 3.3 fusion.97
  520.3 3.3 fusion.97
  524.5 2.7 copy.46
  527.1 3.2 gather_fusion.1
  532.4 12.1 %collective-permute-start.10 = (f32[5,256]{1,0:T(8,128)S(1)}, f32[5,256]{1,0:T(8,128)S(1)}, u32[]{:S(2)}, u32[]{:S(2)}) collective-permute-start(f32[5,256]{1,0:T(8,128)S(1)} %get-tuple-element.133), channel_id=1, source_target_pairs={{16,0},{32,16},{48,32},{64,48},{80,64},{96,80},{112,96},{128,112},... | collective-permute-start | bytes 15368 | tf_op jit(solution)/shard_map/ppermute | solution.py:40
  (107 shorter events, 30.9 us)
Async XLA Ops:
  7.2 356.2 %all-reduce.23.cloned.1.call-start = ((), (), s32[]{:S(2)}) async-start(), calls=%async_computation.1 | async-start | bytes 5242880
  11.2 14.8 %copy-start.7 = (s32[32]{0:T(128)S(1)}, s32[32]{0:T(128)}, u32[]{:S(2)}) copy-start(s32[32]{0:T(128)} %param.20) | copy-start | bytes 388
  31.4 0.9 copy-start
  31.5 0.9 copy-start.1
  31.5 475.6 %all-gather.2.cloned.1.call-start = ((), (), s32[]{:S(2)}) async-start(), calls=%async_computation | async-start | bytes 1114112 | tf_op jit(solution)/shard_map/all_gather | solution.py:185
  32.4 35.3 %collective-permute-start.1 = (f32[4,1,16,256]{3,2,1,0:T(8,128)S(1)}, f32[4,1,16,256]{3,2,1,0:T(8,128)S(1)}, u32[]{:S(2)}, u32[]{:S(2)}) collective-permute-start(f32[4,1,16,256]{3,2,1,0:T(8,128)S(1)} %get-tuple-element.102), channel_id=1, source_target_pairs={{0,1},{1,2},{2,3},{3,4},{4,5},{5,6},{6,7},{7,8},{8,9},{9,10},{10,1... | collective-permute-start | bytes 196616 | tf_op jit(solution)/shard_map/ppermute | solution.py:28
  49.2 18.4 %collective-permute-start = (f32[4,1,16,256]{3,2,1,0:T(8,128)S(1)}, f32[4,1,16,256]{3,2,1,0:T(8,128)S(1)}, u32[]{:S(2)}, u32[]{:S(2)}) collective-permute-start(f32[4,1,16,256]{3,2,1,0:T(8,128)S(1)} %get-tuple-element.101), channel_id=1, source_target_pairs={{1,0},{2,1},{3,2},{4,3},{5,4},{6,5},{7,6},{8,7},{9,8},{10,9},{11,1... | collective-permute-start | bytes 196616 | tf_op jit(solution)/shard_map/ppermute | solution.py:30
  51.1 326.0 %collective-permute-start.3 = (f32[1,1,16,256]{3,2,1,0:T(8,128)S(1)}, f32[1,1,16,256]{3,2,1,0:T(8,128)S(1)}, u32[]{:S(2)}, u32[]{:S(2)}) collective-permute-start(f32[1,1,16,256]{3,2,1,0:T(8,128)S(1)} %get-tuple-element.128), channel_id=1, source_target_pairs={{0,1},{1,2},{2,3},{3,4},{4,5},{5,6},{6,7},{7,8},{8,9},{9,10},{10,1... | collective-permute-start | bytes 49160 | tf_op jit(solution)/shard_map/ppermute | solution.py:28
  63.5 313.7 %collective-permute-start.2 = (f32[1,1,16,256]{3,2,1,0:T(8,128)S(1)}, f32[1,1,16,256]{3,2,1,0:T(8,128)S(1)}, u32[]{:S(2)}, u32[]{:S(2)}) collective-permute-start(f32[1,1,16,256]{3,2,1,0:T(8,128)S(1)} %get-tuple-element.127), channel_id=1, source_target_pairs={{1,0},{2,1},{3,2},{4,3},{5,4},{6,5},{7,6},{8,7},{9,8},{10,9},{11,1... | collective-permute-start | bytes 49160 | tf_op jit(solution)/shard_map/ppermute | solution.py:30
  67.7 351.8 %copy-start.6 = (s32[2,256]{1,0:T(2,128)S(1)}, s32[2,256]{1,0:T(2,128)}, u32[]{:S(2)}) copy-start(s32[2,256]{1,0:T(2,128)} %param.22) | copy-start | bytes 6148
  67.7 351.9 %copy-start.8 = (s32[2,1]{0,1:T(1,128)S(1)}, s32[2,1]{0,1:T(1,128)}, u32[]{:S(2)}) copy-start(s32[2,1]{0,1:T(1,128)} %param.23) | copy-start | bytes 28
  364.5 12.7 %collective-permute-start.5 = (f32[3,1,16,256]{3,2,1,0:T(8,128)S(1)}, f32[3,1,16,256]{3,2,1,0:T(8,128)S(1)}, u32[]{:S(2)}, u32[]{:S(2)}) collective-permute-start(f32[3,1,16,256]{3,2,1,0:T(8,128)S(1)} %get-tuple-element.104), channel_id=1, source_target_pairs={{0,1},{1,2},{2,3},{3,4},{4,5},{5,6},{6,7},{7,8},{8,9},{9,10},{10,1... | collective-permute-start | bytes 147464 | tf_op jit(solution)/shard_map/ppermute | solution.py:28
  372.3 14.1 %collective-permute-start.4 = (f32[3,1,16,256]{3,2,1,0:T(8,128)S(1)}, f32[3,1,16,256]{3,2,1,0:T(8,128)S(1)}, u32[]{:S(2)}, u32[]{:S(2)}) collective-permute-start(f32[3,1,16,256]{3,2,1,0:T(8,128)S(1)} %get-tuple-element.103), channel_id=1, source_target_pairs={{1,0},{2,1},{3,2},{4,3},{5,4},{6,5},{7,6},{8,7},{9,8},{10,9},{11,1... | collective-permute-start | bytes 147464 | tf_op jit(solution)/shard_map/ppermute | solution.py:30
  386.6 4.4 collective-permute-start.7
  388.5 13.8 %collective-permute-start.6 = (f32[1,1,16,256]{3,2,1,0:T(8,128)S(1)}, f32[1,1,16,256]{3,2,1,0:T(8,128)S(1)}, u32[]{:S(2)}, u32[]{:S(2)}) collective-permute-start(f32[1,1,16,256]{3,2,1,0:T(8,128)S(1)} %get-tuple-element.121), channel_id=1, source_target_pairs={{1,0},{2,1},{3,2},{4,3},{5,4},{6,5},{7,6},{8,7},{9,8},{10,9},{11,1... | collective-permute-start | bytes 49160 | tf_op jit(solution)/shard_map/ppermute | solution.py:30
  402.4 107.0 %copy-start.2 = (f32[2,16,256]{2,1,0:T(8,128)}, f32[2,16,256]{2,1,0:T(8,128)S(1)}, u32[]{:S(2)}) copy-start(f32[2,16,256]{2,1,0:T(8,128)S(1)} %fusion.40) | copy-start | bytes 98308
  402.5 4.4 collective-permute-start.9
  404.4 13.8 %collective-permute-start.8 = (f32[1,1,16,256]{3,2,1,0:T(8,128)S(1)}, f32[1,1,16,256]{3,2,1,0:T(8,128)S(1)}, u32[]{:S(2)}, u32[]{:S(2)}) collective-permute-start(f32[1,1,16,256]{3,2,1,0:T(8,128)S(1)} %get-tuple-element.111), channel_id=1, source_target_pairs={{1,0},{2,1},{3,2},{4,3},{5,4},{6,5},{7,6},{8,7},{9,8},{10,9},{11,1... | collective-permute-start | bytes 49160 | tf_op jit(solution)/shard_map/ppermute | solution.py:30
  510.4 13.1 %copy-start.4 = (f32[8192]{0:T(1024)S(1)}, f32[8192]{0:T(1024)}, u32[]{:S(2)}) copy-start(f32[8192]{0:T(1024)} %param.18) | copy-start | bytes 98308
  510.4 13.2 %copy-start.3 = (f32[3,8192]{1,0:T(4,128)S(1)}, f32[3,8192]{1,0:T(4,128)}, u32[]{:S(2)}) copy-start(f32[3,8192]{1,0:T(4,128)} %param.16) | copy-start | bytes 294916
  510.4 13.9 %copy-start.5 = (f32[8192]{0:T(1024)S(1)}, f32[8192]{0:T(1024)}, u32[]{:S(2)}) copy-start(f32[8192]{0:T(1024)} %param.17) | copy-start | bytes 98308
  530.5 14.0 %collective-permute-start.11 = (f32[5,256]{1,0:T(8,128)S(1)}, f32[5,256]{1,0:T(8,128)S(1)}, u32[]{:S(2)}, u32[]{:S(2)}) collective-permute-start(f32[5,256]{1,0:T(8,128)S(1)} %get-tuple-element.134), channel_id=1, source_target_pairs={{496,0},{0,16},{16,32},{32,48},{48,64},{64,80},{80,96},{96,112},{1... | collective-permute-start | bytes 15368 | tf_op jit(solution)/shard_map/ppermute | solution.py:40
  532.4 12.9 %collective-permute-start.10 = (f32[5,256]{1,0:T(8,128)S(1)}, f32[5,256]{1,0:T(8,128)S(1)}, u32[]{:S(2)}, u32[]{:S(2)}) collective-permute-start(f32[5,256]{1,0:T(8,128)S(1)} %get-tuple-element.133), channel_id=1, source_target_pairs={{16,0},{32,16},{48,32},{64,48},{80,64},{96,80},{112,96},{128,112},... | collective-permute-start | bytes 15368 | tf_op jit(solution)/shard_map/ppermute | solution.py:40
Sparse Core Ops, SparseCore 0:
  31.6 331.6 all-reduce.22
  419.6 87.3 all-gather.1
where the time goes:
time: 554 us; the launch traced here: 553 us
  waiting for transfers between devices  412 us (74%)
  starting transfers between devices  68.4 us (12%)
  matrix products  31.4 us (6%)
  local copies, waits for them, and re-layouts  16 us (3%)
  between operations  15.9 us (3%)
  other arithmetic  8.73 us (2%)
    unnamed x3, waiting for transfers between devices  296 us
    all_gather x1, waiting for transfers between devices, per_device(): lax.all_gather(jnp.concatenate([fluid_new, porosity[None]]).astype(jnp.bf...  84 us
    ppermute x5, starting transfers between devices, padded(): lax.ppermute(tail, axis, [(i, (i + 1) % count) for i in range(count)])  40.8 us
    ppermute x5, waiting for transfers between devices, padded(): lax.ppermute(head, axis, [((i + 1) % count, i) for i in range(count)])  31.8 us
    dot_general x4, matrix products, deposit_step(): jnp.einsum('gtc,kgt->gkc', onehot, amounts, preferred_element_type=jnp.fl...  14.7 us
    ppermute x2, starting transfers between devices, passed_along(): return lax.ppermute(block, axis, route)  14 us
    ppermute x5, starting transfers between devices, padded(): lax.ppermute(head, axis, [((i + 1) % count, i) for i in range(count)])  13.5 us
    dot_general x4, matrix products, sample_step(): jnp.einsum('gtc,gkc->kgt', onehot, block_values, preferred_element_type=j...  13 us
  transfers between devices with their start and end apart: 14, of which 6 were waited for; matrix products, arithmetic and copies ran while one was open for 1% of the time, Pallas kernels for 0%

commit v1 on v0

v1 whole, which is shorter than its diff:
```python
import jax
import jax.numpy as jnp
from jax import lax
from jax.experimental import pallas as pl
from jax.experimental.pallas import tpu as pltpu
from jax.sharding import Mesh, PartitionSpec as P

PCAP = 8192
TP = 256
TILES = PCAP // TP
ROWS = PCAP // 128
BLOCK = 2048
RADIAL = 16
LINE = 256
MIG = 256
N_BLK, N_Y, N_Z, N_C = 32, 4, 2, 2
Z_LO = 8
ALL = ("blk", "y", "z", "c")

DT = 0.2
NU = 0.5

PAY_ROWS = 6 * ROWS + 16
SCR_ROWS = 7 * ROWS
SOURCES = N_Y * N_Z * N_C
OWN_BLOCKS = 8
UNROLL = 4
LIST_CAP = SOURCES * TILES + UNROLL

F32 = jnp.float32
BF16 = jnp.bfloat16
I32 = jnp.int32


def flat(blk, y, z, c):
    return ((blk * N_Y + y) * N_Z + z) * N_C + c


def every_place():
    for blk in range(N_BLK):
        for y in range(N_Y):
            for z in range(N_Z):
                for c in range(N_C):
                    yield blk, y, z, c


def halo_route():
    pairs = []
    for blk, y, z, c in every_place():
        if c == 1:
            here = flat(blk, y, z, 1)
            if y < N_Y - 1:
                there = flat(blk, y + 1, z, 0)
            else:
                crossing = blk % Z_LO == Z_LO - 1
                there = flat((blk + 1) % N_BLK, 0, 1 - z if crossing else z, 0)
            pairs += [(here, there), (there, here)]
    return pairs


def leave_route(step):
    edge = 0 if step < 0 else Z_LO - 1
    pairs = []
    for blk, y, z, c in every_place():
        sender = flat(blk, y, 1 - z if blk % Z_LO == edge else z, c)
        pairs.append((sender, flat((blk + step) % N_BLK, y, z, c)))
    return pairs


def swap(values, axis):
    return lax.ppermute(values, axis, [(0, 1), (1, 0)])


def call(kernel, outs, ins, scratch=(), smem=(), limit=16 << 20):
    specs = [
        pl.BlockSpec(memory_space=pltpu.SMEM if i in smem else pltpu.VMEM) for i in range(len(ins))
    ]
    return pl.pallas_call(
        kernel,
        out_shape=[jax.ShapeDtypeStruct(shape, dtype) for shape, dtype in outs],
        in_specs=specs,
        out_specs=[pl.BlockSpec(memory_space=pltpu.VMEM) for _ in outs],
        scratch_shapes=list(scratch),
        compiler_params=pltpu.CompilerParams(vmem_limit_bytes=limit),
    )(*ins)


def rows_iota(rows, lanes):
    return lax.broadcasted_iota(I32, (rows, lanes), 0)


def dot_nt(a, b):
    return lax.dot_general(a, b, (((1,), (1,)), ((), ())), preferred_element_type=F32)


def dot_nn(a, b):
    return lax.dot_general(a, b, (((1,), (0,)), ((), ())), preferred_element_type=F32)


def hi_of(cell):
    return ((cell >> 7) & 1) * 8 + (cell >> 8)


def pack_kernel(
    vel, vol, rate, cell, tiles, count, lists, mig, fluid, press, pay, fpay, keep, vsc, tsc
):
    for r in range(ROWS):
        for k in range(3):
            vsc[k, r : r + 1, :] = vel[k : k + 1, r * 128 : (r + 1) * 128]
    slot = rows_iota(ROWS, 128) * 128 + lax.broadcasted_iota(I32, (ROWS, 128), 1)
    active = (slot < count[0]).astype(F32)
    drag = vol[...] * rate[...]
    pay[0:ROWS, :] = (vol[...] * active).astype(BF16)
    pay[ROWS : 2 * ROWS, :] = (drag * active).astype(BF16)
    for k in range(3):
        pay[(2 + k) * ROWS : (3 + k) * ROWS, :] = (drag * vsc[k] * active).astype(BF16)
    cells = cell[...]
    hi = hi_of(cells)
    code = ((cells & 127) + 128).astype(F32)
    for bit in range(4):
        code = code * jnp.where((hi >> bit) & 1 == 1, F32(2.0 ** (1 << bit)), F32(1.0))
    pay[5 * ROWS : 6 * ROWS, :] = code.astype(BF16)
    lane = lax.broadcasted_iota(I32, (1, TILES), 1)
    tsc[...] = jnp.zeros((16, 128), F32)
    tsc[0:1, 0:TILES] = tiles[...].astype(F32)
    raw_tiles = tsc[...].astype(BF16)
    tsc[0:1, 0:TILES] = jnp.where(lane * TP < count[0], tiles[...].astype(F32), 255.0)
    pay[6 * ROWS : 6 * ROWS + 16, :] = tsc[...].astype(BF16)
    for k in range(3):
        fpay[2 * k : 2 * k + 2] = fluid[k]
    fpay[6:8] = press[...]
    slots = jnp.concatenate([lists[0:1, :], lists[1:2, :]], axis=1)
    lane512 = lax.broadcasted_iota(I32, (1, 2 * MIG), 1)
    ends = jnp.where(lane512 < MIG, mig[0, 0], mig[1, 0] + MIG)
    valid = jnp.where(lane512 < ends, F32(1.0), F32(0.0))
    low = (rows_iota(128, 2 * MIG) == (slots & 127)).astype(F32).astype(BF16)
    row_mask = rows_iota(ROWS, 2 * MIG) == (slots >> 7)
    counts = dot_nt(jnp.where(row_mask, valid, 0.0).astype(BF16), low)
    keep[...] = active * jnp.where(counts > 0.5, 0.0, 1.0)

    def picked(values, parts):
        total = None
        for _ in range(parts):
            piece = values.astype(BF16)
            values = values - piece.astype(F32)
            term = dot_nn(piece, low)
            total = term if total is None else total + term
        return jnp.sum(jnp.where(row_mask, total, 0.0), axis=0, keepdims=True)

    def put(row, values):
        fpay[8, row : row + 1, :] = values[:, :MIG]
        fpay[8, 8 + row : 9 + row, :] = values[:, MIG:]

    for k in range(3):
        put(k, picked(vsc[k], 3))
    put(3, picked(vol[...], 3))
    put(4, picked(rate[...], 3))
    tile_hot = (rows_iota(128, 2 * MIG) == (slots >> 8)).astype(F32).astype(BF16)
    block = dot_nn(raw_tiles, tile_hot)[0:1, :]
    cell_hi = picked((cells >> 7).astype(F32), 1)
    cell_lo = picked((cells & 127).astype(F32), 1)
    put(5, block * BLOCK + cell_hi * 128.0 + cell_lo)
    put(6, valid)
    put(7, jnp.zeros_like(valid))


def planes_kernel(own, far, side, side_far, planes, send):
    z = lax.axis_index("z")
    c = lax.axis_index("c")
    for k in range(4):
        for i in range(2):
            planes[k, z * 4 + c * 2 + i] = own[2 * k + i]
            planes[k, (1 - z) * 4 + c * 2 + i] = far[2 * k + i]
            planes[k, z * 4 + (1 - c) * 2 + i] = side[2 * k + i]
            planes[k, (1 - z) * 4 + (1 - c) * 2 + i] = side_far[2 * k + i]
    for k in range(3):
        send[k] = planes[k, 7 * c]
        send[3 + k] = planes[3, 5 * c + k]


def at(values, axis, step):
    size = values.shape[axis]
    moved = pltpu.roll(values, (-step) % size, axis)
    place = lax.broadcasted_iota(I32, values.shape, axis)
    return jnp.where(place == (size - 1 if step > 0 else 0), 0.0, moved)


def rad_up(values):
    return at(values, values.ndim - 2, 1)


def rad_down(values):
    return at(values, values.ndim - 2, -1)


def axial_up(values):
    return at(values, values.ndim - 1, 1)


def axial_down(values):
    return at(values, values.ndim - 1, -1)


def deposit_kernel(
    pays, planes, halo, u_out, por_out, flux_y, flux_c, scr, acc, tile_v, tile_s, picks, wide, flux, sem
):
    y = lax.axis_index("y")
    c = lax.axis_index("c")
    first = y * 16 + c * OWN_BLOCKS
    for s in range(SOURCES):
        tile_v[s : s + 1, :] = pays[s, 6 * ROWS : 6 * ROWS + 16, :].astype(F32)[0:1, :].astype(I32)
    copy = pltpu.make_async_copy(tile_v, tile_s, sem)
    copy.start()

    def widen(s, carry):
        base = pl.multiple_of(s * SCR_ROWS, 8)
        scr[pl.ds(base, 5 * ROWS), :] = pays[s, 0 : 5 * ROWS, :].astype(F32)
        code = pays[s, 5 * ROWS : 6 * ROWS, :].astype(F32)
        hi = jnp.zeros_like(code)
        for step in (8, 4, 2, 1):
            large = code >= 2.0 ** (7 + step)
            code = jnp.where(large, code * 2.0**-step, code)
            hi = hi + jnp.where(large, F32(step), 0.0)
        scr[pl.ds(base + 5 * ROWS, ROWS), :] = hi
        scr[pl.ds(base + 6 * ROWS, ROWS), :] = code - 128.0
        return carry

    lax.fori_loop(0, SOURCES, widen, 0)
    acc[...] = jnp.zeros_like(acc)
    copy.wait()

    def choose(s, found):
        for t in range(TILES):
            block = tile_s[s, t] - first
            picks[found] = (s * SCR_ROWS + 2 * t) * 16 + block
            mine = jnp.logical_and(block >= 0, block < OWN_BLOCKS)
            found = found + mine.astype(I32)
        return found

    found = lax.fori_loop(0, SOURCES, choose, jnp.int32(0))
    for i in range(UNROLL):
        picks[found + i] = OWN_BLOCKS
    iota16 = lax.broadcasted_iota(I32, (16, 128), 0).astype(F32)
    iota128 = lax.broadcasted_iota(I32, (128, 128), 0).astype(F32)

    def one_tile(code):
        block = code & 15
        base = code >> 4
        left, right = [], []
        for h in range(2):
            hi = scr[pl.ds(base + 5 * ROWS + h, 1), :]
            lo = scr[pl.ds(base + 6 * ROWS + h, 1), :]
            mask = iota16 == hi
            parts = [
                jnp.where(mask, scr[pl.ds(base + k * ROWS + h, 1), :], 0.0).astype(BF16)
                for k in range(5)
            ]
            left.append(jnp.concatenate(parts, axis=0))
            right.append(jnp.where(iota128 == lo, F32(1.0), F32(0.0)).astype(BF16))
        sums = dot_nt(jnp.concatenate(left, axis=1), jnp.concatenate(right, axis=1))
        return block, sums

    def deposit(i, carry):
        done = [one_tile(picks[i * UNROLL + u]) for u in range(UNROLL)]
        for block, sums in done:
            acc[block] = acc[block] + sums
        return carry

    lax.fori_loop(0, (found + UNROLL - 1) // UNROLL, deposit, 0)

    def amount(k):
        halves = []
        for b in range(OWN_BLOCKS):
            halves.append(
                jnp.concatenate([acc[b, k * 16 : k * 16 + 8, :], acc[b, k * 16 + 8 : k * 16 + 16, :]], axis=1)
            )
        return jnp.stack(
            [jnp.concatenate([halves[2 * i], halves[2 * i + 1]], axis=0) for i in range(4)]
        )

    for k in range(4):
        wide[k, 1:5] = planes[k, pl.ds(c * 4, 4)]
        wide[k, 5 * (1 - c)] = planes[k, 4 - c]
        if k < 3:
            wide[k, 5 * c] = halo[k]
    wide[3, 5 * c] = halo[3 + 2 * (1 - c)]
    porosity = 1.0 / (1.0 + amount(0))
    por_out[...] = porosity
    below = 1.0 + DT * amount(1) / porosity
    centre = wide[3, 1:5]
    slopes = [
        0.5 * (wide[3, 2:6] - wide[3, 0:4]),
        0.5 * (rad_up(centre) - rad_down(centre)),
        0.5 * (axial_up(centre) - axial_down(centre)),
    ]
    for k in range(3):
        v = wide[k, 1:5]
        lap = (
            wide[k, 2:6] + wide[k, 0:4] + rad_up(v) + rad_down(v) + axial_up(v) + axial_down(v) - 6.0 * v
        )
        u = (v + DT * (NU * lap - slopes[k]) + DT * amount(2 + k) / porosity) / below
        u_out[k] = u
        flux[k] = porosity * u
    for k in range(3):
        for i in range(3):
            flux_y[3 * k + i] = flux[k, c + i]
            flux_c[3 * k + i] = flux[k, 1 - c + i]


def fluid_kernel(u_in, por_in, planes, halo, from_y, from_c, fields, kept, sent, flux, pres, out):
    c = lax.axis_index("c")
    for k in range(3):
        flux[k, 3:7] = por_in[...] * u_in[k]
        for i in range(3):
            flux[k, 7 * c + i] = from_y[3 * k + i]
            flux[k, 7 * (1 - c) + i] = from_c[3 * k + i]
    for i in range(3):
        pres[7 * c + i] = halo[3 + i]
    for j in range(7):
        pres[3 * (1 - c) + j] = planes[3, c + j]
    f1 = flux[1, 1:9]
    f2 = flux[2, 1:9]
    source = 0.5 * (
        flux[0, 2:10] - flux[0, 0:8] + rad_up(f1) - rad_down(f1) + axial_up(f2) - axial_down(f2)
    )

    def sweep(p, s):
        centre = p[1:-1]
        return (
            p[2:]
            + p[:-2]
            + rad_up(centre)
            + rad_down(centre)
            + axial_up(centre)
            + axial_down(centre)
            - s / DT
        ) / 6.0

    p1 = sweep(pres[...], source)
    p2 = sweep(p1, source[1:-1])
    centre = p2[1:-1]
    slopes = [
        0.5 * (p2[2:] - p2[:-2]),
        0.5 * (rad_up(centre) - rad_down(centre)),
        0.5 * (axial_up(centre) - axial_down(centre)),
    ]
    for k in range(3):
        out[k] = u_in[k] - DT * slopes[k]
    out[3] = centre
    for k in range(4):
        for i in range(4):
            plane = out[k, i] if k < 3 else por_in[i]
            for h in range(2):
                half = plane[8 * h : 8 * h + 8]
                both = jnp.concatenate([half[:, :128], half[:, 128:]], axis=0)
                fields[2 * i + h, 16 * k : 16 * k + 16, :] = both.astype(BF16)
    for k in range(4):
        for i in range(2):
            kept[k, i] = out[k, 2 * c + i]
            sent[k, i] = out[k, 2 * (1 - c) + i]


def step_parcel(vel, rate, sampled):
    coupling = rate / (sampled[3] * sampled[3])
    pull = DT * coupling
    below = 1.0 + pull
    return [(vel[k] + pull * sampled[k]) / below for k in range(3)]


def leave_kernel(fields, own, far, out0, out1):
    z_lo = lax.rem(lax.axis_index("blk"), Z_LO)
    list0 = jnp.where(z_lo == 0, far[8, 0:8, :], own[8, 0:8, :])
    list1 = jnp.where(z_lo == Z_LO - 1, far[8, 8:16, :], own[8, 8:16, :])
    both = jnp.concatenate([list0, list1], axis=1)
    place = both[5:6, :].astype(I32)
    block = place >> 11
    hi = hi_of(place & (BLOCK - 1))
    low = (rows_iota(128, 2 * MIG) == (place & 127)).astype(F32).astype(BF16)
    mask = rows_iota(16, 2 * MIG) == hi

    def gather(i, total):
        for u in range(8):
            picked = dot_nn(fields[i // 4, i % 4, u], low)
            wanted = (i % 4) * 16 + (i // 4) * OWN_BLOCKS + u
            total = total + jnp.where(block == wanted, picked, 0.0)
        return total

    total = lax.fori_loop(0, 8, gather, jnp.zeros((64, 2 * MIG), F32))
    sampled = [
        jnp.sum(jnp.where(mask, total[16 * k : 16 * k + 16], 0.0), axis=0, keepdims=True)
        for k in range(4)
    ]
    sampled[3] = jnp.where(both[6:7, :] > 0.5, sampled[3], 1.0)
    vol, rate, valid = both[3:4, :], both[4:5, :], both[6:7, :]
    moved = step_parcel([both[k : k + 1, :] for k in range(3)], rate, sampled)
    for k, values in enumerate(moved + [vol, rate]):
        values = values * valid
        out0[k : k + 1, :] = values[:, :MIG]
        out1[k : k + 1, :] = values[:, MIG:]


def move_kernel(fields, tiles, cell, keep, vel, rate, out):
    iota16 = rows_iota(16, TP)
    iota128 = rows_iota(128, TP)

    def pair(ref, t):
        return jnp.concatenate([ref[pl.ds(2 * t, 1), :], ref[pl.ds(2 * t + 1, 1), :]], axis=1)

    def one_tile(t):
        block = tiles[t]
        here = fields[(block >> 3) & 1, block >> 4, block & 7]
        cells = pair(cell, t)
        low = jnp.where(iota128 == (cells & 127), F32(1.0), F32(0.0)).astype(BF16)
        picked = dot_nn(here, low)
        mask = iota16 == hi_of(cells)
        sampled = [
            jnp.sum(jnp.where(mask, picked[16 * k : 16 * k + 16], 0.0), axis=0, keepdims=True)
            for k in range(4)
        ]
        lanes = pl.ds(pl.multiple_of(t * TP, TP), TP)
        moved = step_parcel([vel[k : k + 1, lanes] for k in range(3)], pair(rate, t), sampled)
        stays = pair(keep, t)
        for k in range(3):
            out[k : k + 1, lanes] = moved[k] * stays

    def some(i, carry):
        for u in range(4):
            one_tile(i * 4 + u)
        return carry

    lax.fori_loop(0, TILES // 4, some, 0)


def over_y(values):
    copies = jnp.broadcast_to(values[None], (N_Y,) + values.shape)
    return lax.all_to_all(copies, "y", 0, 0, tiled=False)


def per_device(
    fluid_vel,
    pressure,
    parcel_vel,
    parcel_vol,
    parcel_rate,
    cell_local,
    tile_block,
    parcel_count,
    leave_lists,
    mig_counts,
):
    vol = parcel_vol.reshape(ROWS, 128)
    rate = parcel_rate.reshape(ROWS, 128)
    cell = cell_local.reshape(ROWS, 128)
    tiles = tile_block.reshape(1, TILES)
    pay, fpay, keep = call(
        pack_kernel,
        [((PAY_ROWS, 128), BF16), ((9, RADIAL, LINE), F32), ((ROWS, 128), F32)],
        [parcel_vel, vol, rate, cell, tiles, parcel_count, leave_lists, mig_counts, fluid_vel, pressure],
        scratch=[pltpu.VMEM((3, ROWS, 128), F32), pltpu.VMEM((16, 128), F32)],
        smem=(5, 7),
    )
    fpay_far = swap(fpay, "z")
    pay_far = swap(pay, "z")
    fpay_side = swap(fpay, "c")
    fpay_side_far = swap(fpay_far, "c")
    planes, send = call(
        planes_kernel,
        [((4, 8, RADIAL, LINE), F32), ((6, RADIAL, LINE), F32)],
        [fpay, fpay_far, fpay_side, fpay_side_far],
    )
    route = halo_route()
    halo = lax.ppermute(send, ALL, route)
    pays = over_y(jnp.concatenate([pay, pay_far]))
    pays = lax.all_gather(pays, "c", axis=0).reshape(SOURCES, PAY_ROWS, 128)
    u_star, porosity, flux_y, flux_c = call(
        deposit_kernel,
        [
            ((3, 4, RADIAL, LINE), F32),
            ((4, RADIAL, LINE), F32),
            ((9, RADIAL, LINE), F32),
            ((9, RADIAL, LINE), F32),
        ],
        [pays, planes, halo],
        scratch=[
            pltpu.VMEM((SOURCES * SCR_ROWS, 128), F32),
            pltpu.VMEM((OWN_BLOCKS + 1, 80, 128), F32),
            pltpu.VMEM((SOURCES, 128), I32),
            pltpu.SMEM((SOURCES, 128), I32),
            pltpu.SMEM((LIST_CAP,), I32),
            pltpu.VMEM((4, 6, RADIAL, LINE), F32),
            pltpu.VMEM((3, 4, RADIAL, LINE), F32),
            pltpu.SemaphoreType.DMA,
        ],
    )
    from_y = lax.ppermute(flux_y, ALL, route)
    from_c = swap(flux_c, "c")
    fields, kept, sent = call(
        fluid_kernel,
        [
            ((OWN_BLOCKS, 64, 128), BF16),
            ((4, 2, RADIAL, LINE), F32),
            ((4, 2, RADIAL, LINE), F32),
        ],
        [u_star, porosity, planes, halo, from_y, from_c],
        scratch=[
            pltpu.VMEM((3, 10, RADIAL, LINE), F32),
            pltpu.VMEM((10, RADIAL, LINE), F32),
            pltpu.VMEM((4, 4, RADIAL, LINE), F32),
        ],
    )
    fields = lax.all_gather(over_y(fields), "c", axis=0)
    swapped = swap(sent, "c")
    mine = lax.axis_index("c") == lax.axis_index("z")
    out0, out1 = call(
        leave_kernel, [((5, MIG), F32), ((5, MIG), F32)], [fields, fpay, fpay_far]
    )
    arrive0 = lax.ppermute(out0, ALL, leave_route(-1))
    arrive1 = lax.ppermute(out1, ALL, leave_route(1))
    (parcel_next,) = call(
        move_kernel,
        [((3, PCAP), F32)],
        [fields, tile_block, cell, keep, parcel_vel, rate],
        smem=(1,),
    )
    fluid_next = jnp.where(mine, kept[:3], swapped[:3])
    pressure_next = jnp.where(mine, kept[3], swapped[3])
    return fluid_next, pressure_next, parcel_next, jnp.stack([arrive0, arrive1])


def solution(mesh):
    fine = Mesh(mesh.devices.reshape(N_BLK, N_Y, N_Z, N_C), ALL)
    placed = (
        P(None, ALL, None, None),
        P(ALL, None, None),
        P(None, ALL),
        P(ALL),
        P(ALL),
        P(ALL),
        P(ALL),
        P(ALL),
        P(None, ALL),
        P(None, ALL),
    )
    return jax.shard_map(
        per_device,
        mesh=fine,
        in_specs=placed,
        out_specs=(
            P(None, ALL, None, None),
            P(ALL, None, None),
            P(None, ALL),
            P(None, None, ALL),
        ),
        check_vma=False,
    )
```

time: 554 us -> 161 us (0.29)
  waiting for transfers between devices: 412 us -> 18.5 us
  matrix products: 31.4 us -> 0 us
  blocking collectives: 0 us -> 27 us
  Pallas kernels: 0 us -> 12.6 us
  other arithmetic: 8.73 us -> 1.3 us
  starting transfers between devices: 68.4 us -> 75.8 us
  local copies, waits for them, and re-layouts: 16 us -> 10.4 us
    unnamed x3 -> x2, waiting for transfers between devices: 296 us -> 0.03 us
    all_gather x1 -> x2, waiting for transfers between devices: 84 us -> 9.72 us  [the longest x1 9.72 us: per_device(): fields = lax.all_gather(over_y(fields), 'c', axis=0)]
    dot_general x9 -> x0, matrix products: 31.4 us -> none  [the longest x4 14.7 us: deposit_step(): jnp.einsum('gtc,kgt->gkc', onehot, amounts, preferred_element_type=jnp.fl...]
    all_to_all x0 -> x2, blocking collectives: none -> 27 us  [over_y(): return lax.all_to_all(copies, 'y', 0, 0, tiled=False)]
    ppermute x12 -> x10, waiting for transfers between devices: 32.6 us -> 8.74 us  [the longest x6 5.24 us: swap(): return lax.ppermute(values, axis, [(0, 1), (1, 0)])]
    pallas_call x0 -> x6, Pallas kernels: none -> 12.6 us  [call(): pl.pallas_call(kernel, out_shape=[jax.ShapeDtypeStruct(shape, dtype) for...]
    unnamed x23 -> x30, local copies, waits for them, and re-layouts: 2.75 us -> 10.2 us
    ppermute x12 -> x10, starting transfers between devices: 68.3 us -> 75.7 us  [the longest x6 62.6 us: swap(): return lax.ppermute(values, axis, [(0, 1), (1, 0)])]
  transfers between devices with their start and end apart: 14 -> 12, of which waited for: 6 -> 6; matrix products, arithmetic and copies ran while one was open for 1% -> 1% of each run, Pallas kernels for 0% -> 2%
where the time goes in v1:
time: 161 us; the launch traced here: 160 us
  starting transfers between devices  75.8 us (47%)
  blocking collectives  27 us (17%)
  waiting for transfers between devices  18.5 us (11%)
  between operations  14.9 us (9%)
  Pallas kernels  12.6 us (8%)
  local copies, waits for them, and re-layouts  10.4 us (6%)
    ppermute x6, starting transfers between devices, swap(): return lax.ppermute(values, axis, [(0, 1), (1, 0)])  62.6 us
    all_to_all x2, blocking collectives, over_y(): return lax.all_to_all(copies, 'y', 0, 0, tiled=False)  27 us
    pallas_call x6, Pallas kernels, call(): pl.pallas_call(kernel, out_shape=[jax.ShapeDtypeStruct(shape, dtype) for...  12.6 us
    unnamed x30, local copies, waits for them, and re-layouts  10.2 us
    all_gather x1, waiting for transfers between devices, per_device(): fields = lax.all_gather(over_y(fields), 'c', axis=0)  9.72 us
    ppermute x1, starting transfers between devices, per_device(): arrive0 = lax.ppermute(out0, ALL, leave_route(-1))  6.54 us
    ppermute x6, waiting for transfers between devices, swap(): return lax.ppermute(values, axis, [(0, 1), (1, 0)])  5.24 us
    ppermute x1, waiting for transfers between devices, per_device(): halo = lax.ppermute(send, ALL, route)  3.49 us
  transfers between devices with their start and end apart: 12, of which 6 were waited for; matrix products, arithmetic and copies ran while one was open for 1% of the time, Pallas kernels for 2%

profile of v1, /device:TPU:1, one launch (start us, length us, event | category | flops | bytes accessed | tf_op | source)
XLA Modules:
  0.0 160.5 jit_solution(3139285266412955710)
XLA Ops:
  14.8 1.1 shard_map.129
  15.9 16.3 %collective-permute-start = (bf16[400,128]{1,0:T(8,128)(2,1)S(1)}, bf16[400,128]{1,0:T(8,128)(2,1)S(1)}, u32[]{:S(2)}, u32[]{:S(2)}) collective-permute-start(bf16[400,128]{1,0:T(8,128)(2,1)S(1)} %get-tuple-element.18), channel_id=1, source_target_pairs={{0,2},{2,0},{1,3},{3,1},{4,6},{6,4},{5,7},{7,5},{8,10},{10,8},{9,1... | collective-permute-start | bytes 307208 | tf_op jit(solution)/shard_map/ppermute | solution.py:71
  32.2 2.3 %collective-permute-done = bf16[400,128]{1,0:T(8,128)(2,1)S(1)} collective-permute-done((bf16[400,128]{1,0:T(8,128)(2,1)S(1)}, bf16[400,128]{1,0:T(8,128)(2,1)S(1)}, u32[]{:S(2)}, u32[]{:S(2)}) %collective-permute-start) | collective-permute-done | bytes 102432 | tf_op jit(solution)/shard_map/ppermute | solution.py:71
  34.6 14.5 %all_to_all.10 = bf16[4,800,128]{2,1,0:T(8,128)(2,1)} all-to-all(bf16[4,800,128]{2,1,0:T(8,128)(2,1)S(1)} %broadcast_in_dim.4), channel_id=1, replica_groups=mesh['blk'=32,'y'=4,'z'=2,'c'=2] {'y'}, dimensions={0} | all-to-all | bytes 1638400 | tf_op jit(solution)/shard_map/all_to_all | solution.py:436
  49.3 11.5 %collective-permute-start.1 = (f32[9,16,256]{2,1,0:T(8,128)S(1)}, f32[9,16,256]{2,1,0:T(8,128)S(1)}, u32[]{:S(2)}, u32[]{:S(2)}) collective-permute-start(f32[9,16,256]{2,1,0:T(8,128)S(1)} %get-tuple-element.19.own), channel_id=1, source_target_pairs={{0,2},{2,0},{1,3},{3,1},{4,6},{6,4},{5,7},{7,5},{8,10},{10,8},{9,1... | collective-permute-start | bytes 442376 | tf_op jit(solution)/shard_map/ppermute | solution.py:71
  60.8 5.8 %collective-permute-start.2 = (f32[9,16,256]{2,1,0:T(8,128)S(1)}, f32[9,16,256]{2,1,0:T(8,128)S(1)}, u32[]{:S(2)}, u32[]{:S(2)}) collective-permute-start(f32[9,16,256]{2,1,0:T(8,128)S(1)} %get-tuple-element.19.own), channel_id=1, source_target_pairs={{0,1},{1,0},{2,3},{3,2},{4,5},{5,4},{6,7},{7,6},{8,9},{9,8},{10,11... | collective-permute-start | bytes 442376 | tf_op jit(solution)/shard_map/ppermute | solution.py:71
  66.7 5.4 %collective-permute-start.3 = (f32[9,16,256]{2,1,0:T(8,128)S(1)}, f32[9,16,256]{2,1,0:T(8,128)S(1)}, u32[]{:S(2)}, u32[]{:S(2)}) collective-permute-start(f32[9,16,256]{2,1,0:T(8,128)S(1)} %collective-permute-done.1.far), channel_id=1, source_target_pairs={{0,1},{1,0},{2,3},{3,2},{4,5},{5,4},{6,7},{7,6},{8,9},{9,8},{10,11... | collective-permute-start | bytes 442376 | tf_op jit(solution)/shard_map/ppermute | solution.py:71
  72.0 1.0 collective-permute-done.3.side_far
  73.1 2.4 %collective-permute-start.4 = (f32[6,16,256]{2,1,0:T(8,128)S(1)}, f32[6,16,256]{2,1,0:T(8,128)S(1)}, u32[]{:S(2)}, u32[]{:S(2)}) collective-permute-start(f32[6,16,256]{2,1,0:T(8,128)S(1)} %get-tuple-element.21), channel_id=1, source_target_pairs={{1,4},{4,1},{3,6},{6,3},{5,8},{8,5},{7,10},{10,7},{9,12},{12,9},{1... | collective-permute-start | bytes 294920 | tf_op jit(solution)/shard_map/ppermute | solution.py:472
  75.5 3.5 %collective-permute-done.4.halo = f32[6,16,256]{2,1,0:T(8,128)S(1)} collective-permute-done((f32[6,16,256]{2,1,0:T(8,128)S(1)}, f32[6,16,256]{2,1,0:T(8,128)S(1)}, u32[]{:S(2)}, u32[]{:S(2)}) %collective-permute-start.4) | collective-permute-done | bytes 98336 | tf_op jit(solution)/shard_map/ppermute | solution.py:472
  79.0 1.4 copy-done.1
  80.4 5.4 %shard_map.131 = (f32[3,4,16,256]{3,2,1,0:T(8,128)S(1)}, f32[4,16,256]{2,1,0:T(8,128)S(1)}, f32[9,16,256]{2,1,0:T(8,128)S(1)}, f32[9,16,256]{2,1,0:T(8,128)S(1)}) custom-call(bf16[16,400,128]{2,1,0:T(8,128)(2,1)S(1)} %bitcast.12, f32[4,8,16,256]{3,2,1,0:T(8,128)S(1)} %get-tuple-element.20.planes, f32[6,16,256]{2,1,0:T(8,128)S(1)} %collective-permute-done.4.halo), custom_call_target="tpu_custom_call" | custom-call | tf_op jit(solution)/shard_map/pallas_call | solution.py:78
  85.9 1.9 %collective-permute-start.5 = (f32[9,16,256]{2,1,0:T(8,128)S(1)}, f32[9,16,256]{2,1,0:T(8,128)S(1)}, u32[]{:S(2)}, u32[]{:S(2)}) collective-permute-start(f32[9,16,256]{2,1,0:T(8,128)S(1)} %get-tuple-element.24), channel_id=1, source_target_pairs={{1,4},{4,1},{3,6},{6,3},{5,8},{8,5},{7,10},{10,7},{9,12},{12,9},{1... | collective-permute-start | bytes 442376 | tf_op jit(solution)/shard_map/ppermute | solution.py:495
  87.8 20.5 %collective-permute-start.6 = (f32[9,16,256]{2,1,0:T(8,128)S(1)}, f32[9,16,256]{2,1,0:T(8,128)S(1)}, u32[]{:S(2)}, u32[]{:S(2)}) collective-permute-start(f32[9,16,256]{2,1,0:T(8,128)S(1)} %get-tuple-element.25), channel_id=1, source_target_pairs={{0,1},{1,0},{2,3},{3,2},{4,5},{5,4},{6,7},{7,6},{8,9},{9,8},{10,11... | collective-permute-start | bytes 442376 | tf_op jit(solution)/shard_map/ppermute | solution.py:71
  108.3 1.0 collective-permute-done.6.from_c
  110.0 12.5 %all_to_all.11 = bf16[4,8,64,128]{3,2,1,0:T(8,128)(2,1)} all-to-all(bf16[4,8,64,128]{3,2,1,0:T(8,128)(2,1)S(1)} %broadcast_in_dim.5), channel_id=1, replica_groups=mesh['blk'=32,'y'=4,'z'=2,'c'=2] {'y'}, dimensions={0} | all-to-all | bytes 1048576 | tf_op jit(solution)/shard_map/all_to_all | solution.py:436
  122.5 3.1 %collective-permute-start.7 = (f32[4,2,16,256]{3,2,1,0:T(8,128)S(1)}, f32[4,2,16,256]{3,2,1,0:T(8,128)S(1)}, u32[]{:S(2)}, u32[]{:S(2)}) collective-permute-start(f32[4,2,16,256]{3,2,1,0:T(8,128)S(1)} %get-tuple-element.27), channel_id=1, source_target_pairs={{0,1},{1,0},{2,3},{3,2},{4,5},{5,4},{6,7},{7,6},{8,9},{9,8},{10,11... | collective-permute-start | bytes 393224 | tf_op jit(solution)/shard_map/ppermute | solution.py:71
  125.6 1.0 collective-permute-done.7
  127.2 9.7 %all-gather.7.cloned.1.call-done = bf16[8,8,64,128]{3,2,1,0:T(8,128)(2,1)} async-done(((bf16[4,8,64,128]{3,2,1,0:T(8,128)(2,1)}), bf16[8,8,64,128]{3,2,1,0:T(8,128)(2,1)}) %all-gather.7.cloned.1.call-update) | async-done | bytes 1048592 | tf_op jit(solution)/shard_map/all_gather | solution.py:511
  136.9 1.2 copy-done
  138.1 2.5 %shard_map.134 = (f32[5,256]{1,0:T(8,128)S(1)}, f32[5,256]{1,0:T(8,128)S(1)}) custom-call(bf16[2,4,8,64,128]{4,3,2,1,0:T(8,128)(2,1)S(1)} %bitcast.10, f32[9,16,256]{2,1,0:T(8,128)S(1)} %get-tuple-element.19.own, f32[9,16,256]{2,1,0:T(8,128)S(1)} %collective-permute-done.1.far), custom_call_target="tpu_custom_call" | custom-call | tf_op jit(solution)/shard_map/pallas_call | solution.py:78
  140.7 2.2 %collective-permute-start.9 = (f32[5,256]{1,0:T(8,128)S(1)}, f32[5,256]{1,0:T(8,128)S(1)}, u32[]{:S(2)}, u32[]{:S(2)}) collective-permute-start(f32[5,256]{1,0:T(8,128)S(1)} %get-tuple-element.31), channel_id=1, source_target_pairs={{0,16},{1,17},{2,18},{3,19},{4,20},{5,21},{6,22},{7,23},{8,24},{9,... | collective-permute-start | bytes 15368 | tf_op jit(solution)/shard_map/ppermute | solution.py:518
  142.8 6.5 %collective-permute-start.8 = (f32[5,256]{1,0:T(8,128)S(1)}, f32[5,256]{1,0:T(8,128)S(1)}, u32[]{:S(2)}, u32[]{:S(2)}) collective-permute-start(f32[5,256]{1,0:T(8,128)S(1)} %get-tuple-element.30), channel_id=1, source_target_pairs={{2,496},{3,497},{0,498},{1,499},{6,500},{7,501},{4,502},{5,503},{1... | collective-permute-start | bytes 15368 | tf_op jit(solution)/shard_map/ppermute | solution.py:517
  150.0 3.0 %shard_map.133 = f32[3,8192]{1,0:T(4,128)} custom-call(bf16[2,4,8,64,128]{4,3,2,1,0:T(8,128)(2,1)S(1)} %bitcast.11, s32[32]{0:T(128)S(1)} %copy-done.12, s32[64,128]{1,0:T(8,128)S(1)} %bitcast.16, f32[64,128]{1,0:T(8,128)S(1)} %get-tuple-element.29.keep, f32[3,8192]{1,0:T(4,128)S(1)} %copy-done.3, f32[64,128]{1,0:T(8,128)S(1)} %bitcast.14), custom_call_target="tpu_custom_call" | custom-call | tf_op jit(solution)/shard_map/pallas_call | solution.py:78
  (46 shorter events, 9.7 us)
Async XLA Ops:
  7.2 71.8 %all-gather.5.cloned.1.call-start = ((), (), s32[]{:S(2)}) async-start(), calls=%async_computation.2 | async-start | bytes 2457600 | tf_op jit(solution)/shard_map/all_gather | solution.py:474
  8.6 0.9 copy-start.2
  9.5 0.8 copy-start.4
  10.3 0.8 copy-start.6
  11.0 0.9 copy-start.8
  11.9 0.8 copy-start.9
  12.7 0.8 copy-start.10
  15.9 18.6 %collective-permute-start = (bf16[400,128]{1,0:T(8,128)(2,1)S(1)}, bf16[400,128]{1,0:T(8,128)(2,1)S(1)}, u32[]{:S(2)}, u32[]{:S(2)}) collective-permute-start(bf16[400,128]{1,0:T(8,128)(2,1)S(1)} %get-tuple-element.18), channel_id=1, source_target_pairs={{0,2},{2,0},{1,3},{3,1},{4,6},{6,4},{5,7},{7,5},{8,10},{10,8},{9,1... | collective-permute-start | bytes 307208 | tf_op jit(solution)/shard_map/ppermute | solution.py:71
  49.2 87.7 %all-gather.7.cloned.1.call-start = ((), (), s32[]{:S(2)}) async-start(), calls=%async_computation.3 | async-start | bytes 1572864 | tf_op jit(solution)/shard_map/all_gather | solution.py:511
  49.3 17.4 %collective-permute-start.1 = (f32[9,16,256]{2,1,0:T(8,128)S(1)}, f32[9,16,256]{2,1,0:T(8,128)S(1)}, u32[]{:S(2)}, u32[]{:S(2)}) collective-permute-start(f32[9,16,256]{2,1,0:T(8,128)S(1)} %get-tuple-element.19.own), channel_id=1, source_target_pairs={{0,2},{2,0},{1,3},{3,1},{4,6},{6,4},{5,7},{7,5},{8,10},{10,8},{9,1... | collective-permute-start | bytes 442376 | tf_op jit(solution)/shard_map/ppermute | solution.py:71
  60.8 11.2 %collective-permute-start.2 = (f32[9,16,256]{2,1,0:T(8,128)S(1)}, f32[9,16,256]{2,1,0:T(8,128)S(1)}, u32[]{:S(2)}, u32[]{:S(2)}) collective-permute-start(f32[9,16,256]{2,1,0:T(8,128)S(1)} %get-tuple-element.19.own), channel_id=1, source_target_pairs={{0,1},{1,0},{2,3},{3,2},{4,5},{5,4},{6,7},{7,6},{8,9},{9,8},{10,11... | collective-permute-start | bytes 442376 | tf_op jit(solution)/shard_map/ppermute | solution.py:71
  66.7 6.4 %collective-permute-start.3 = (f32[9,16,256]{2,1,0:T(8,128)S(1)}, f32[9,16,256]{2,1,0:T(8,128)S(1)}, u32[]{:S(2)}, u32[]{:S(2)}) collective-permute-start(f32[9,16,256]{2,1,0:T(8,128)S(1)} %collective-permute-done.1.far), channel_id=1, source_target_pairs={{0,1},{1,0},{2,3},{3,2},{4,5},{5,4},{6,7},{7,6},{8,9},{9,8},{10,11... | collective-permute-start | bytes 442376 | tf_op jit(solution)/shard_map/ppermute | solution.py:71
  73.1 5.9 %collective-permute-start.4 = (f32[6,16,256]{2,1,0:T(8,128)S(1)}, f32[6,16,256]{2,1,0:T(8,128)S(1)}, u32[]{:S(2)}, u32[]{:S(2)}) collective-permute-start(f32[6,16,256]{2,1,0:T(8,128)S(1)} %get-tuple-element.21), channel_id=1, source_target_pairs={{1,4},{4,1},{3,6},{6,3},{5,8},{8,5},{7,10},{10,7},{9,12},{12,9},{1... | collective-permute-start | bytes 294920 | tf_op jit(solution)/shard_map/ppermute | solution.py:472
  79.0 1.4 copy-start.1
  85.9 22.4 %collective-permute-start.5 = (f32[9,16,256]{2,1,0:T(8,128)S(1)}, f32[9,16,256]{2,1,0:T(8,128)S(1)}, u32[]{:S(2)}, u32[]{:S(2)}) collective-permute-start(f32[9,16,256]{2,1,0:T(8,128)S(1)} %get-tuple-element.24), channel_id=1, source_target_pairs={{1,4},{4,1},{3,6},{6,3},{5,8},{8,5},{7,10},{10,7},{9,12},{12,9},{1... | collective-permute-start | bytes 442376 | tf_op jit(solution)/shard_map/ppermute | solution.py:495
  87.8 21.5 %collective-permute-start.6 = (f32[9,16,256]{2,1,0:T(8,128)S(1)}, f32[9,16,256]{2,1,0:T(8,128)S(1)}, u32[]{:S(2)}, u32[]{:S(2)}) collective-permute-start(f32[9,16,256]{2,1,0:T(8,128)S(1)} %get-tuple-element.25), channel_id=1, source_target_pairs={{0,1},{1,0},{2,3},{3,2},{4,5},{5,4},{6,7},{7,6},{8,9},{9,8},{10,11... | collective-permute-start | bytes 442376 | tf_op jit(solution)/shard_map/ppermute | solution.py:71
  109.9 40.1 %copy-start.3 = (f32[3,8192]{1,0:T(4,128)S(1)}, f32[3,8192]{1,0:T(4,128)}, u32[]{:S(2)}) copy-start(f32[3,8192]{1,0:T(4,128)} %vel.3) | copy-start | bytes 294916
  109.9 40.1 %copy-start.5 = (f32[8192]{0:T(1024)S(1)}, f32[8192]{0:T(1024)}, u32[]{:S(2)}) copy-start(f32[8192]{0:T(1024)} %param.14) | copy-start | bytes 98308
  110.0 40.1 %copy-start.7 = (s32[8192]{0:T(1024)S(1)}, s32[8192]{0:T(1024)}, u32[]{:S(2)}) copy-start(s32[8192]{0:T(1024)} %param.15) | copy-start | bytes 98308
  110.0 40.1 %copy-start.12 = (s32[32]{0:T(128)S(1)}, s32[32]{0:T(128)}, u32[]{:S(2)}) copy-start(s32[32]{0:T(128)} %tiles.1) | copy-start | bytes 388
  122.5 4.1 %collective-permute-start.7 = (f32[4,2,16,256]{3,2,1,0:T(8,128)S(1)}, f32[4,2,16,256]{3,2,1,0:T(8,128)S(1)}, u32[]{:S(2)}, u32[]{:S(2)}) collective-permute-start(f32[4,2,16,256]{3,2,1,0:T(8,128)S(1)} %get-tuple-element.27), channel_id=1, source_target_pairs={{0,1},{1,0},{2,3},{3,2},{4,5},{5,4},{6,7},{7,6},{8,9},{9,8},{10,11... | collective-permute-start | bytes 393224 | tf_op jit(solution)/shard_map/ppermute | solution.py:71
  136.9 1.2 copy-start
  140.7 12.4 %collective-permute-start.9 = (f32[5,256]{1,0:T(8,128)S(1)}, f32[5,256]{1,0:T(8,128)S(1)}, u32[]{:S(2)}, u32[]{:S(2)}) collective-permute-start(f32[5,256]{1,0:T(8,128)S(1)} %get-tuple-element.31), channel_id=1, source_target_pairs={{0,16},{1,17},{2,18},{3,19},{4,20},{5,21},{6,22},{7,23},{8,24},{9,... | collective-permute-start | bytes 15368 | tf_op jit(solution)/shard_map/ppermute | solution.py:518
  142.8 10.2 %collective-permute-start.8 = (f32[5,256]{1,0:T(8,128)S(1)}, f32[5,256]{1,0:T(8,128)S(1)}, u32[]{:S(2)}, u32[]{:S(2)}) collective-permute-start(f32[5,256]{1,0:T(8,128)S(1)} %get-tuple-element.30), channel_id=1, source_target_pairs={{2,496},{3,497},{0,498},{1,499},{6,500},{7,501},{4,502},{5,503},{1... | collective-permute-start | bytes 15368 | tf_op jit(solution)/shard_map/ppermute | solution.py:517
  (2 other events, 1.3 us)
Sparse Core Ops, SparseCore 0:
  49.3 27.3 all-gather.4
  122.6 14.2 all-gather.6

commit v2 on v1

--- a/solution.py
+++ b/solution.py
@@ -22,10 +22,12 @@
 
 PAY_ROWS = 6 * ROWS + 16
 SCR_ROWS = 7 * ROWS
-SOURCES = N_Y * N_Z * N_C
+SOURCES = N_Y * N_Z
 OWN_BLOCKS = 8
 UNROLL = 4
 LIST_CAP = SOURCES * TILES + UNROLL
+
+PACK_LIMIT = 56 << 20
 
 F32 = jnp.float32
 BF16 = jnp.bfloat16
@@ -71,10 +73,11 @@
     return lax.ppermute(values, axis, [(0, 1), (1, 0)])
 
 
-def call(kernel, outs, ins, scratch=(), smem=(), limit=16 << 20):
-    specs = [
-        pl.BlockSpec(memory_space=pltpu.SMEM if i in smem else pltpu.VMEM) for i in range(len(ins))
-    ]
+def call(kernel, outs, ins, scratch=(), smem=(), hbm=(), limit=16 << 20, flops=0):
+    def space(i):
+        return pltpu.SMEM if i in smem else pltpu.HBM if i in hbm else pltpu.VMEM
+
+    specs = [pl.BlockSpec(memory_space=space(i)) for i in range(len(ins))]
     return pl.pallas_call(
         kernel,
         out_shape=[jax.ShapeDtypeStruct(shape, dtype) for shape, dtype in outs],
@@ -82,6 +85,7 @@
         out_specs=[pl.BlockSpec(memory_space=pltpu.VMEM) for _ in outs],
         scratch_shapes=list(scratch),
         compiler_params=pltpu.CompilerParams(vmem_limit_bytes=limit),
+        cost_estimate=pl.CostEstimate(flops=flops, bytes_accessed=1 << 20, transcendentals=0),
     )(*ins)
 
 
@@ -101,9 +105,24 @@
     return ((cell >> 7) & 1) * 8 + (cell >> 8)
 
 
-def pack_kernel(
-    vel, vol, rate, cell, tiles, count, lists, mig, fluid, press, pay, fpay, keep, vsc, tsc
-):
+def pack_kernel(*refs):
+    sources, (pay, fpay, keep), (vel, vol, rate, cell, tiles, count, lists, mig, vsc, tsc, sems) = (
+        refs[:10],
+        refs[10:13],
+        refs[13:],
+    )
+    fluid, press = sources[8:]
+    targets = [vel, vol, rate, cell, tiles, count, lists, mig]
+    targets += [fpay.at[2 * k : 2 * k + 2] for k in range(3)] + [fpay.at[6:8]]
+    origins = list(sources[:8]) + [fluid.at[k] for k in range(3)] + [press]
+    copies = [
+        pltpu.make_async_copy(origin, target, sems.at[i])
+        for i, (origin, target) in enumerate(zip(origins, targets))
+    ]
+    for copy in copies:
+        copy.start()
+    for copy in copies:
+        copy.wait()
     for r in range(ROWS):
         for k in range(3):
             vsc[k, r : r + 1, :] = vel[k : k + 1, r * 128 : (r + 1) * 128]
@@ -126,12 +145,9 @@
     raw_tiles = tsc[...].astype(BF16)
     tsc[0:1, 0:TILES] = jnp.where(lane * TP < count[0], tiles[...].astype(F32), 255.0)
     pay[6 * ROWS : 6 * ROWS + 16, :] = tsc[...].astype(BF16)
-    for k in range(3):
-        fpay[2 * k : 2 * k + 2] = fluid[k]
-    fpay[6:8] = press[...]
     slots = jnp.concatenate([lists[0:1, :], lists[1:2, :]], axis=1)
     lane512 = lax.broadcasted_iota(I32, (1, 2 * MIG), 1)
-    ends = jnp.where(lane512 < MIG, mig[0, 0], mig[1, 0] + MIG)
+    ends = jnp.where(lane512 < MIG, mig[0:1, :], mig[1:2, :] + MIG)
     valid = jnp.where(lane512 < ends, F32(1.0), F32(0.0))
     low = (rows_iota(128, 2 * MIG) == (slots & 127)).astype(F32).astype(BF16)
     row_mask = rows_iota(ROWS, 2 * MIG) == (slots >> 7)
@@ -164,18 +180,14 @@
     put(7, jnp.zeros_like(valid))
 
 
-def planes_kernel(own, far, side, side_far, planes, send):
-    z = lax.axis_index("z")
+def edge_kernel(own, far, edge, side):
     c = lax.axis_index("c")
+    native = lax.axis_index("z") == c
     for k in range(4):
+        edge[k] = jnp.where(native, own[2 * k + c], far[2 * k + c])
         for i in range(2):
-            planes[k, z * 4 + c * 2 + i] = own[2 * k + i]
-            planes[k, (1 - z) * 4 + c * 2 + i] = far[2 * k + i]
-            planes[k, z * 4 + (1 - c) * 2 + i] = side[2 * k + i]
-            planes[k, (1 - z) * 4 + (1 - c) * 2 + i] = side_far[2 * k + i]
-    for k in range(3):
-        send[k] = planes[k, 7 * c]
-        send[3 + k] = planes[3, 5 * c + k]
+            side[2 * k + i] = jnp.where(native, far[2 * k + i], own[2 * k + i])
+    side[8] = jnp.where(native, own[7 - c], far[7 - c])
 
 
 def at(values, axis, step):
@@ -201,12 +213,8 @@
     return at(values, values.ndim - 1, -1)
 
 
-def deposit_kernel(
-    pays, planes, halo, u_out, por_out, flux_y, flux_c, scr, acc, tile_v, tile_s, picks, wide, flux, sem
-):
-    y = lax.axis_index("y")
-    c = lax.axis_index("c")
-    first = y * 16 + c * OWN_BLOCKS
+def add_deposits(pays, acc, scr, tile_v, tile_s, picks, sem):
+    first = lax.axis_index("y") * 16 + lax.axis_index("c") * OWN_BLOCKS
     for s in range(SOURCES):
         tile_v[s : s + 1, :] = pays[s, 6 * ROWS : 6 * ROWS + 16, :].astype(F32)[0:1, :].astype(I32)
     copy = pltpu.make_async_copy(tile_v, tile_s, sem)
@@ -226,7 +234,6 @@
         return carry
 
     lax.fori_loop(0, SOURCES, widen, 0)
-    acc[...] = jnp.zeros_like(acc)
     copy.wait()
 
     def choose(s, found):
@@ -268,6 +275,20 @@
 
     lax.fori_loop(0, (found + UNROLL - 1) // UNROLL, deposit, 0)
 
+
+def first_deposit_kernel(pays, acc, *scratch):
+    acc[...] = jnp.zeros_like(acc)
+    add_deposits(pays, acc, *scratch)
+
+
+def velocity_kernel(
+    pays, before, own, far, side, edge, u_out, por_out, flux_y, flux_c, wide, flux, acc, *scratch
+):
+    c = lax.axis_index("c")
+    native = lax.axis_index("z") == c
+    acc[...] = before[...]
+    add_deposits(pays, acc, *scratch)
+
     def amount(k):
         halves = []
         for b in range(OWN_BLOCKS):
@@ -279,11 +300,11 @@
         )
 
     for k in range(4):
-        wide[k, 1:5] = planes[k, pl.ds(c * 4, 4)]
-        wide[k, 5 * (1 - c)] = planes[k, 4 - c]
-        if k < 3:
-            wide[k, 5 * c] = halo[k]
-    wide[3, 5 * c] = halo[3 + 2 * (1 - c)]
+        wide[k, 5 * c] = edge[k]
+        for i in range(2):
+            wide[k, 1 + 2 * c + i] = jnp.where(native, own[2 * k + i], far[2 * k + i])
+            wide[k, 3 - 2 * c + i] = side[2 * k + i]
+        wide[k, 5 * (1 - c)] = jnp.where(native, far[2 * k + c], own[2 * k + c])
     porosity = 1.0 / (1.0 + amount(0))
     por_out[...] = porosity
     below = 1.0 + DT * amount(1) / porosity
@@ -301,23 +322,30 @@
         u = (v + DT * (NU * lap - slopes[k]) + DT * amount(2 + k) / porosity) / below
         u_out[k] = u
         flux[k] = porosity * u
-    for k in range(3):
-        for i in range(3):
+    for i in range(3):
+        for k in range(3):
             flux_y[3 * k + i] = flux[k, c + i]
             flux_c[3 * k + i] = flux[k, 1 - c + i]
-
-
-def fluid_kernel(u_in, por_in, planes, halo, from_y, from_c, fields, kept, sent, flux, pres, out):
+        flux_y[9 + i] = wide[3, 1 + c + i]
+
+
+def fluid_kernel(
+    u_in, por_in, own, far, side, from_y, from_c, fields, kept, sent, flux, pres, out
+):
     c = lax.axis_index("c")
+    native = lax.axis_index("z") == c
     for k in range(3):
         flux[k, 3:7] = por_in[...] * u_in[k]
         for i in range(3):
             flux[k, 7 * c + i] = from_y[3 * k + i]
             flux[k, 7 * (1 - c) + i] = from_c[3 * k + i]
     for i in range(3):
-        pres[7 * c + i] = halo[3 + i]
-    for j in range(7):
-        pres[3 * (1 - c) + j] = planes[3, c + j]
+        pres[7 * c + i] = from_y[9 + i]
+    for i in range(2):
+        pres[3 + 2 * c + i] = jnp.where(native, own[6 + i], far[6 + i])
+        pres[5 - 2 * c + i] = side[6 + i]
+        pres[7 - 6 * c + i] = jnp.where(native, far[6 + i], own[6 + i])
+    pres[9 * (1 - c)] = side[8]
     f1 = flux[1, 1:9]
     f2 = flux[2, 1:9]
     source = 0.5 * (
@@ -353,7 +381,8 @@
             for h in range(2):
                 half = plane[8 * h : 8 * h + 8]
                 both = jnp.concatenate([half[:, :128], half[:, 128:]], axis=0)
-                fields[2 * i + h, 16 * k : 16 * k + 16, :] = both.astype(BF16)
+                for copy in range(N_Y):
+                    fields[copy, 2 * i + h, 16 * k : 16 * k + 16, :] = both.astype(BF16)
     for k in range(4):
         for i in range(2):
             kept[k, i] = out[k, 2 * c + i]
@@ -367,7 +396,8 @@
     return [(vel[k] + pull * sampled[k]) / below for k in range(3)]
 
 
-def leave_kernel(fields, own, far, out0, out1):
+def leave_kernel(near, other, own, far, out0, out1):
+    c = lax.axis_index("c")
     z_lo = lax.rem(lax.axis_index("blk"), Z_LO)
     list0 = jnp.where(z_lo == 0, far[8, 0:8, :], own[8, 0:8, :])
     list1 = jnp.where(z_lo == Z_LO - 1, far[8, 8:16, :], own[8, 8:16, :])
@@ -379,13 +409,14 @@
     mask = rows_iota(16, 2 * MIG) == hi
 
     def gather(i, total):
-        for u in range(8):
-            picked = dot_nn(fields[i // 4, i % 4, u], low)
-            wanted = (i % 4) * 16 + (i // 4) * OWN_BLOCKS + u
-            total = total + jnp.where(block == wanted, picked, 0.0)
+        for u in range(OWN_BLOCKS):
+            for half, core in ((near, c), (other, 1 - c)):
+                picked = dot_nn(half[i, u], low)
+                wanted = i * 16 + core * OWN_BLOCKS + u
+                total = total + jnp.where(block == wanted, picked, 0.0)
         return total
 
-    total = lax.fori_loop(0, 8, gather, jnp.zeros((64, 2 * MIG), F32))
+    total = lax.fori_loop(0, N_Y, gather, jnp.zeros((64, 2 * MIG), F32))
     sampled = [
         jnp.sum(jnp.where(mask, total[16 * k : 16 * k + 16], 0.0), axis=0, keepdims=True)
         for k in range(4)
@@ -399,7 +430,14 @@
         out1[k : k + 1, :] = values[:, MIG:]
 
 
-def move_kernel(fields, tiles, cell, keep, vel, rate, out):
+def move_kernel(near, other, tiles_in, cell_in, keep, vel_in, rate_in, out, tiles, cell, vel, rate, sems):
+    moves = ((tiles_in, tiles), (cell_in, cell), (vel_in, vel), (rate_in, rate))
+    copies = [pltpu.make_async_copy(a, b, sems.at[i]) for i, (a, b) in enumerate(moves)]
+    for copy in copies:
+        copy.start()
+    for copy in copies:
+        copy.wait()
+    c = lax.axis_index("c")
     iota16 = rows_iota(16, TP)
     iota128 = rows_iota(128, TP)
 
@@ -408,7 +446,8 @@
 
     def one_tile(t):
         block = tiles[t]
-        here = fields[(block >> 3) & 1, block >> 4, block & 7]
+        row, col = block >> 4, block & 7
+        here = jnp.where((block >> 3) & 1 == c, near[row, col], other[row, col])
         cells = pair(cell, t)
         low = jnp.where(iota128 == (cells & 127), F32(1.0), F32(0.0)).astype(BF16)
         picked = dot_nn(here, low)
@@ -452,79 +491,107 @@
     rate = parcel_rate.reshape(ROWS, 128)
     cell = cell_local.reshape(ROWS, 128)
     tiles = tile_block.reshape(1, TILES)
+    plane = (RADIAL, LINE)
     pay, fpay, keep = call(
         pack_kernel,
-        [((PAY_ROWS, 128), BF16), ((9, RADIAL, LINE), F32), ((ROWS, 128), F32)],
+        [((PAY_ROWS, 128), BF16), ((9,) + plane, F32), ((ROWS, 128), F32)],
         [parcel_vel, vol, rate, cell, tiles, parcel_count, leave_lists, mig_counts, fluid_vel, pressure],
-        scratch=[pltpu.VMEM((3, ROWS, 128), F32), pltpu.VMEM((16, 128), F32)],
-        smem=(5, 7),
-    )
+        scratch=[
+            pltpu.VMEM((3, PCAP), F32),
+            pltpu.VMEM((ROWS, 128), F32),
+            pltpu.VMEM((ROWS, 128), F32),
+            pltpu.VMEM((ROWS, 128), I32),
+            pltpu.VMEM((1, TILES), I32),
+            pltpu.SMEM((1,), I32),
+            pltpu.VMEM((2, MIG), I32),
+            pltpu.VMEM((2, 1), I32),
+            pltpu.VMEM((3, ROWS, 128), F32),
+            pltpu.VMEM((16, 128), F32),
+            pltpu.SemaphoreType.DMA((12,)),
+        ],
+        hbm=range(10),
+        limit=PACK_LIMIT,
+    )
+    pay_far = swap(pay, "z")
     fpay_far = swap(fpay, "z")
-    pay_far = swap(pay, "z")
-    fpay_side = swap(fpay, "c")
-    fpay_side_far = swap(fpay_far, "c")
-    planes, send = call(
-        planes_kernel,
-        [((4, 8, RADIAL, LINE), F32), ((6, RADIAL, LINE), F32)],
-        [fpay, fpay_far, fpay_side, fpay_side_far],
+    pays = over_y(jnp.concatenate([pay, pay_far]))
+    pays, fpay_far = lax.optimization_barrier((pays, fpay_far))
+    edge, side = call(
+        edge_kernel, [((4,) + plane, F32), ((9,) + plane, F32)], [fpay, fpay_far]
     )
     route = halo_route()
-    halo = lax.ppermute(send, ALL, route)
-    pays = over_y(jnp.concatenate([pay, pay_far]))
-    pays = lax.all_gather(pays, "c", axis=0).reshape(SOURCES, PAY_ROWS, 128)
+    pays_c = swap(pays, "c")
+    side = swap(side, "c")
+    edge = lax.ppermute(edge, ALL, route)
+    deposit_scratch = [
+        pltpu.VMEM((SOURCES * SCR_ROWS, 128), F32),
+        pltpu.VMEM((SOURCES, 128), I32),
+        pltpu.SMEM((SOURCES, 128), I32),
+        pltpu.SMEM((LIST_CAP,), I32),
+        pltpu.SemaphoreType.DMA,
+    ]
+    sums_shape = (OWN_BLOCKS + 1, 80, 128)
+    (sums,) = call(
+        first_deposit_kernel,
+        [(sums_shape, F32)],
+        [pays.reshape(SOURCES, PAY_ROWS, 128)],
+        scratch=deposit_scratch,
+        flops=1 << 31,
+    )
     u_star, porosity, flux_y, flux_c = call(
-        deposit_kernel,
-        [
-            ((3, 4, RADIAL, LINE), F32),
-            ((4, RADIAL, LINE), F32),
-            ((9, RADIAL, LINE), F32),
-            ((9, RADIAL, LINE), F32),
-        ],
-        [pays, planes, halo],
+        velocity_kernel,
+        [((3, 4) + plane, F32), ((4,) + plane, F32), ((12,) + plane, F32), ((9,) + plane, F32)],
+        [pays_c.reshape(SOURCES, PAY_ROWS, 128), sums, fpay, fpay_far, side, edge],
         scratch=[
-            pltpu.VMEM((SOURCES * SCR_ROWS, 128), F32),
-            pltpu.VMEM((OWN_BLOCKS + 1, 80, 128), F32),
-            pltpu.VMEM((SOURCES, 128), I32),
-            pltpu.SMEM((SOURCES, 128), I32),
-            pltpu.SMEM((LIST_CAP,), I32),
-            pltpu.VMEM((4, 6, RADIAL, LINE), F32),
-            pltpu.VMEM((3, 4, RADIAL, LINE), F32),
-            pltpu.SemaphoreType.DMA,
-        ],
+            pltpu.VMEM((4, 6) + plane, F32),
+            pltpu.VMEM((3, 4) + plane, F32),
+            pltpu.VMEM(sums_shape, F32),
+        ]
+        + deposit_scratch,
+        flops=1 << 31,
     )
     from_y = lax.ppermute(flux_y, ALL, route)
     from_c = swap(flux_c, "c")
     fields, kept, sent = call(
         fluid_kernel,
-        [
-            ((OWN_BLOCKS, 64, 128), BF16),
-            ((4, 2, RADIAL, LINE), F32),
-            ((4, 2, RADIAL, LINE), F32),
+        [((N_Y, OWN_BLOCKS, 64, 128), BF16), ((4, 2) + plane, F32), ((4, 2) + plane, F32)],
+        [u_star, porosity, fpay, fpay_far, side, from_y, from_c],
+        scratch=[
+            pltpu.VMEM((3, 10) + plane, F32),
+            pltpu.VMEM((10,) + plane, F32),
+            pltpu.VMEM((4, 4) + plane, F32),
         ],
-        [u_star, porosity, planes, halo, from_y, from_c],
-        scratch=[
-            pltpu.VMEM((3, 10, RADIAL, LINE), F32),
-            pltpu.VMEM((10, RADIAL, LINE), F32),
-            pltpu.VMEM((4, 4, RADIAL, LINE), F32),
-        ],
-    )
-    fields = lax.all_gather(over_y(fields), "c", axis=0)
+    )
+    fields = lax.all_to_all(fields, "y", 0, 0)
+    fields_c = swap(fields, "c")
     swapped = swap(sent, "c")
     mine = lax.axis_index("c") == lax.axis_index("z")
     out0, out1 = call(
-        leave_kernel, [((5, MIG), F32), ((5, MIG), F32)], [fields, fpay, fpay_far]
+        leave_kernel,
+        [((5, MIG), F32), ((5, MIG), F32)],
+        [fields, fields_c, fpay, fpay_far],
+        flops=1 << 30,
     )
     arrive0 = lax.ppermute(out0, ALL, leave_route(-1))
     arrive1 = lax.ppermute(out1, ALL, leave_route(1))
     (parcel_next,) = call(
         move_kernel,
         [((3, PCAP), F32)],
-        [fields, tile_block, cell, keep, parcel_vel, rate],
-        smem=(1,),
+        [fields, fields_c, tile_block, cell, keep, parcel_vel, rate],
+        scratch=[
+            pltpu.SMEM((TILES,), I32),
+            pltpu.VMEM((ROWS, 128), I32),
+            pltpu.VMEM((3, PCAP), F32),
+            pltpu.VMEM((ROWS, 128), F32),
+            pltpu.SemaphoreType.DMA((4,)),
+        ],
+        hbm=(2, 3, 5, 6),
+        flops=1 << 31,
     )
     fluid_next = jnp.where(mine, kept[:3], swapped[:3])
     pressure_next = jnp.where(mine, kept[3], swapped[3])
-    return fluid_next, pressure_next, parcel_next, jnp.stack([arrive0, arrive1])
+    arrivals = jnp.stack([arrive0, arrive1], axis=1).transpose(1, 0, 2)
+    return fluid_next, pressure_next, parcel_next, arrivals
 
 
 def solution(mesh):

time: 161 us -> 122 us (0.76)
  blocking collectives: 27 us -> 0 us
  starting transfers between devices: 75.8 us -> 90.1 us
  between operations: 14.9 us -> 1.57 us
  local copies, waits for them, and re-layouts: 10.4 us -> 2.3 us
  waiting for transfers between devices: 18.5 us -> 11.1 us
    all_to_all x2 -> x0, blocking collectives: 27 us -> none  [over_y(): return lax.all_to_all(copies, 'y', 0, 0, tiled=False)]
    all_gather x2 -> x0, waiting for transfers between devices: 9.72 us -> none  [the longest x1 9.72 us: per_device(): fields = lax.all_gather(over_y(fields), 'c', axis=0)]
    unnamed x30 -> x16, local copies, waits for them, and re-layouts: 10.2 us -> 1.28 us
    all_to_all x0 -> x2, starting transfers between devices: none -> 8.06 us  [the longest x1 4.59 us: over_y(): return lax.all_to_all(copies, 'y', 0, 0, tiled=False)]
    all_to_all x0 -> x2, waiting for transfers between devices: none -> 4.5 us  [the longest x1 4.5 us: per_device(): fields = lax.all_to_all(fields, 'y', 0, 0)]
    ppermute x6 -> x7, starting transfers between devices: 62.6 us -> 66.6 us  [swap(): return lax.ppermute(values, axis, [(0, 1), (1, 0)])]
    ppermute x1, waiting for transfers between devices: 3.49 us -> 0.01 us  [per_device(): edge = lax.ppermute(edge, ALL, route)]
    pallas_call x6 -> x7, Pallas kernels: 12.6 us -> 14.1 us  [call(): pl.pallas_call(kernel, out_shape=[jax.ShapeDtypeStruct(shape, dtype) for...]
  transfers between devices with their start and end apart: 12 -> 13, of which waited for: 6 -> 5; matrix products, arithmetic and copies ran while one was open for 1% -> 1% of each run, Pallas kernels for 2% -> 5%
where the time goes in v2:
time: 122 us; the launch traced here: 121 us
  starting transfers between devices  90.1 us (74%)
  Pallas kernels  14.1 us (12%)
  waiting for transfers between devices  11.1 us (9%)
  local copies, waits for them, and re-layouts  2.3 us (2%)
  other arithmetic  2.19 us (2%)
  between operations  1.57 us (1%)
    ppermute x7, starting transfers between devices, swap(): return lax.ppermute(values, axis, [(0, 1), (1, 0)])  66.6 us
    pallas_call x7, Pallas kernels, call(): pl.pallas_call(kernel, out_shape=[jax.ShapeDtypeStruct(shape, dtype) for...  14.1 us
    ppermute x1, starting transfers between devices, per_device(): arrive0 = lax.ppermute(out0, ALL, leave_route(-1))  6.68 us
    ppermute x7, waiting for transfers between devices, swap(): return lax.ppermute(values, axis, [(0, 1), (1, 0)])  6.61 us
    all_to_all x1, starting transfers between devices, over_y(): return lax.all_to_all(copies, 'y', 0, 0, tiled=False)  4.59 us
    all_to_all x1, waiting for transfers between devices, per_device(): fields = lax.all_to_all(fields, 'y', 0, 0)  4.5 us
    ppermute x1, starting transfers between devices, per_device(): edge = lax.ppermute(edge, ALL, route)  3.97 us
    all_to_all x1, starting transfers between devices, per_device(): fields = lax.all_to_all(fields, 'y', 0, 0)  3.47 us
  transfers between devices with their start and end apart: 13, of which 5 were waited for; matrix products, arithmetic and copies ran while one was open for 1% of the time, Pallas kernels for 5%

profile of v2, /device:TPU:1, one launch (start us, length us, event | category | flops | bytes accessed | tf_op | source)
XLA Modules:
  0.0 121.4 jit_solution(1892783280655037579)
XLA Ops:
  2.0 2.3 %shard_map.129 = (bf16[400,128]{1,0:T(8,128)(2,1)}, f32[9,16,256]{2,1,0:T(8,128)}, f32[64,128]{1,0:T(8,128)}) custom-call(f32[3,8192]{1,0:T(4,128)} %vel_in.1, f32[64,128]{1,0:T(8,128)} %bitcast.19, f32[64,128]{1,0:T(8,128)} %bitcast.13, s32[64,128]{1,0:T(8,128)} %bitcast.15, s32[1,32]{1,0:T(1,128)} %bitcast.17, s32[1]{0:T(128)S(6)} %copy.16.refs_5_, ...), custom_call_target="tpu_custom_call" | custom-call | bytes 1048576 | tf_op jit(solution)/shard_map/pallas_call | solution.py:81
  4.3 16.3 %collective-permute-start = (bf16[400,128]{1,0:T(8,128)(2,1)}, bf16[400,128]{1,0:T(8,128)(2,1)S(1)}, u32[]{:S(2)}, u32[]{:S(2)}) collective-permute-start(bf16[400,128]{1,0:T(8,128)(2,1)} %get-tuple-element.20), channel_id=1, source_target_pairs={{0,2},{2,0},{1,3},{3,1},{4,6},{6,4},{5,7},{7,5},{8,10},{10,8},{9,1... | collective-permute-start | bytes 307208 | tf_op jit(solution)/shard_map/ppermute | solution.py:73
  20.5 2.5 %collective-permute-done = bf16[400,128]{1,0:T(8,128)(2,1)S(1)} collective-permute-done((bf16[400,128]{1,0:T(8,128)(2,1)}, bf16[400,128]{1,0:T(8,128)(2,1)S(1)}, u32[]{:S(2)}, u32[]{:S(2)}) %collective-permute-start) | collective-permute-done | bytes 102432 | tf_op jit(solution)/shard_map/ppermute | solution.py:73
  24.0 1.0 broadcast_in_dim.2
  25.0 4.6 %all-to-all-start = ((bf16[4,800,128]{2,1,0:T(8,128)(2,1)}), bf16[4,800,128]{2,1,0:T(8,128)(2,1)S(1)}, u32[]{:S(2)}, u32[]{:S(2)}) async-start(bf16[4,800,128]{2,1,0:T(8,128)(2,1)} %broadcast_in_dim.2), calls=%async_computation | async-start | bytes 1638400 | tf_op jit(solution)/shard_map/all_to_all | solution.py:475
  29.6 11.7 %collective-permute-start.1 = (f32[9,16,256]{2,1,0:T(8,128)S(1)}, f32[9,16,256]{2,1,0:T(8,128)S(1)}, u32[]{:S(2)}, u32[]{:S(2)}) collective-permute-start(f32[9,16,256]{2,1,0:T(8,128)S(1)} %copy-done), channel_id=1, source_target_pairs={{0,2},{2,0},{1,3},{3,1},{4,6},{6,4},{5,7},{7,5},{8,10},{10,8},{9,1... | collective-permute-start | bytes 442376 | tf_op jit(solution)/shard_map/ppermute | solution.py:73
  41.3 2.9 %collective-permute-done.1.far = f32[9,16,256]{2,1,0:T(8,128)S(1)} collective-permute-done((f32[9,16,256]{2,1,0:T(8,128)S(1)}, f32[9,16,256]{2,1,0:T(8,128)S(1)}, u32[]{:S(2)}, u32[]{:S(2)}) %collective-permute-start.1) | collective-permute-done | bytes 147488 | tf_op jit(solution)/shard_map/ppermute | solution.py:73
  44.2 5.8 %collective-permute-start.2 = (bf16[4,800,128]{2,1,0:T(8,128)(2,1)S(1)}, bf16[4,800,128]{2,1,0:T(8,128)(2,1)S(1)}, u32[]{:S(2)}, u32[]{:S(2)}) collective-permute-start(bf16[4,800,128]{2,1,0:T(8,128)(2,1)S(1)} %all-to-all-done), channel_id=1, source_target_pairs={{0,1},{1,0},{2,3},{3,2},{4,5},{5,4},{6,7},{7,6},{8,9},{9,8},{10,11... | collective-permute-start | bytes 2457608 | tf_op jit(solution)/shard_map/ppermute | solution.py:73
  50.1 1.9 %collective-permute-start.3 = (f32[9,16,256]{2,1,0:T(8,128)S(1)}, f32[9,16,256]{2,1,0:T(8,128)S(1)}, u32[]{:S(2)}, u32[]{:S(2)}) collective-permute-start(f32[9,16,256]{2,1,0:T(8,128)S(1)} %get-tuple-element.24), channel_id=1, source_target_pairs={{0,1},{1,0},{2,3},{3,2},{4,5},{5,4},{6,7},{7,6},{8,9},{9,8},{10,11... | collective-permute-start | bytes 442376 | tf_op jit(solution)/shard_map/ppermute | solution.py:73
  52.0 4.0 %collective-permute-start.4 = (f32[4,16,256]{2,1,0:T(8,128)S(1)}, f32[4,16,256]{2,1,0:T(8,128)S(1)}, u32[]{:S(2)}, u32[]{:S(2)}) collective-permute-start(f32[4,16,256]{2,1,0:T(8,128)S(1)} %get-tuple-element.25), channel_id=1, source_target_pairs={{1,4},{4,1},{3,6},{6,3},{5,8},{8,5},{7,10},{10,7},{9,12},{12,9},{1... | collective-permute-start | bytes 196616 | tf_op jit(solution)/shard_map/ppermute | solution.py:525
  56.0 2.6 %shard_map.130.before = f32[9,80,128]{2,1,0:T(8,128)S(1)} custom-call(bf16[8,400,128]{2,1,0:T(8,128)(2,1)S(1)} %bitcast.12), custom_call_target="tpu_custom_call" | custom-call | flops 2147483648 | bytes 1048576 | tf_op jit(solution)/shard_map/pallas_call | solution.py:81
  58.7 3.0 %shard_map.132 = (f32[3,4,16,256]{3,2,1,0:T(8,128)S(1)}, f32[4,16,256]{2,1,0:T(8,128)S(1)}, f32[12,16,256]{2,1,0:T(8,128)S(1)}, f32[9,16,256]{2,1,0:T(8,128)S(1)}) custom-call(bf16[8,400,128]{2,1,0:T(8,128)(2,1)S(1)} %bitcast.18, f32[9,80,128]{2,1,0:T(8,128)S(1)} %shard_map.130.before, f32[9,16,256]{2,1,0:T(8,128)S(1)} %copy-done, ...), custom_call_target="tpu_custom_call" | custom-call | flops 2147483648 | bytes 1048576 | tf_op jit(solution)/shard_map/pallas_call | solution.py:81
  61.7 2.9 %collective-permute-start.5 = (f32[12,16,256]{2,1,0:T(8,128)S(1)}, f32[12,16,256]{2,1,0:T(8,128)S(1)}, u32[]{:S(2)}, u32[]{:S(2)}) collective-permute-start(f32[12,16,256]{2,1,0:T(8,128)S(1)} %get-tuple-element.28), channel_id=1, source_target_pairs={{1,4},{4,1},{3,6},{6,3},{5,8},{8,5},{7,10},{10,7},{9,12},{12,9},{1... | collective-permute-start | bytes 589832 | tf_op jit(solution)/shard_map/ppermute | solution.py:553
  64.6 23.0 %collective-permute-start.6 = (f32[9,16,256]{2,1,0:T(8,128)S(1)}, f32[9,16,256]{2,1,0:T(8,128)S(1)}, u32[]{:S(2)}, u32[]{:S(2)}) collective-permute-start(f32[9,16,256]{2,1,0:T(8,128)S(1)} %get-tuple-element.29), channel_id=1, source_target_pairs={{0,1},{1,0},{2,3},{3,2},{4,5},{5,4},{6,7},{7,6},{8,9},{9,8},{10,11... | collective-permute-start | bytes 442376 | tf_op jit(solution)/shard_map/ppermute | solution.py:73
  87.6 1.0 collective-permute-done.6.from_c
  88.6 1.3 %shard_map.133 = (bf16[4,8,64,128]{3,2,1,0:T(8,128)(2,1)}, f32[4,2,16,256]{3,2,1,0:T(8,128)S(1)}, f32[4,2,16,256]{3,2,1,0:T(8,128)S(1)}) custom-call(f32[3,4,16,256]{3,2,1,0:T(8,128)S(1)} %get-tuple-element.26.u_in, f32[4,16,256]{2,1,0:T(8,128)S(1)} %get-tuple-element.27.por_in, f32[9,16,256]{2,1,0:T(8,128)S(1)} %copy-done, ...), custom_call_target="tpu_custom_call" | custom-call | bytes 1048576 | tf_op jit(solution)/shard_map/pallas_call | solution.py:81
  89.9 3.5 %all-to-all-start.1 = ((bf16[4,8,64,128]{3,2,1,0:T(8,128)(2,1)}), bf16[4,8,64,128]{3,2,1,0:T(8,128)(2,1)S(1)}, u32[]{:S(2)}, u32[]{:S(2)}) async-start(bf16[4,8,64,128]{3,2,1,0:T(8,128)(2,1)} %get-tuple-element.32), calls=%async_computation.1 | async-start | bytes 1048576 | tf_op jit(solution)/shard_map/all_to_all | solution.py:565
  93.4 3.3 %collective-permute-start.7 = (f32[4,2,16,256]{3,2,1,0:T(8,128)S(1)}, f32[4,2,16,256]{3,2,1,0:T(8,128)S(1)}, u32[]{:S(2)}, u32[]{:S(2)}) collective-permute-start(f32[4,2,16,256]{3,2,1,0:T(8,128)S(1)} %get-tuple-element.31), channel_id=1, source_target_pairs={{0,1},{1,0},{2,3},{3,2},{4,5},{5,4},{6,7},{7,6},{8,9},{9,8},{10,11... | collective-permute-start | bytes 393224 | tf_op jit(solution)/shard_map/ppermute | solution.py:73
  96.7 4.5 %all-to-all-done.1.near = bf16[4,8,64,128]{3,2,1,0:T(8,128)(2,1)S(1)} async-done(((bf16[4,8,64,128]{3,2,1,0:T(8,128)(2,1)}), bf16[4,8,64,128]{3,2,1,0:T(8,128)(2,1)S(1)}, u32[]{:S(2)}, u32[]{:S(2)}) %all-to-all-start.1) | async-done | bytes 524320 | tf_op jit(solution)/shard_map/all_to_all | solution.py:565
  101.2 4.5 %collective-permute-start.8 = (bf16[4,8,64,128]{3,2,1,0:T(8,128)(2,1)S(1)}, bf16[4,8,64,128]{3,2,1,0:T(8,128)(2,1)S(1)}, u32[]{:S(2)}, u32[]{:S(2)}) collective-permute-start(bf16[4,8,64,128]{3,2,1,0:T(8,128)(2,1)S(1)} %all-to-all-done.1.near), channel_id=1, source_target_pairs={{0,1},{1,0},{2,3},{3,2},{4,5},{5,4},{6,7},{7,6},{8,9},{9,8},{10,11... | collective-permute-start | bytes 1572872 | tf_op jit(solution)/shard_map/ppermute | solution.py:73
  107.2 1.9 %shard_map.135 = (f32[5,256]{1,0:T(8,128)S(1)}, f32[5,256]{1,0:T(8,128)S(1)}) custom-call(bf16[4,8,64,128]{3,2,1,0:T(8,128)(2,1)S(1)} %all-to-all-done.1.near, bf16[4,8,64,128]{3,2,1,0:T(8,128)(2,1)S(1)} %collective-permute-done.8.other, f32[9,16,256]{2,1,0:T(8,128)S(1)} %copy-done, f32[9,16,256]{2,1,0:T(8,128)S(1)} %collective-permute-done.1.far), custom_call_target="tpu_custom_call" | custom-call | flops 1073741824 | bytes 1048576 | tf_op jit(solution)/shard_map/pallas_call | solution.py:81
  109.1 1.9 %collective-permute-start.10 = (f32[5,256]{1,0:T(8,128)S(1)}, f32[5,256]{1,0:T(8,128)S(1)}, u32[]{:S(2)}, u32[]{:S(2)}) collective-permute-start(f32[5,256]{1,0:T(8,128)S(1)} %get-tuple-element.35), channel_id=1, source_target_pairs={{0,16},{1,17},{2,18},{3,19},{4,20},{5,21},{6,22},{7,23},{8,24},{9,... | collective-permute-start | bytes 15368 | tf_op jit(solution)/shard_map/ppermute | solution.py:576
  111.0 6.7 %collective-permute-start.9 = (f32[5,256]{1,0:T(8,128)S(1)}, f32[5,256]{1,0:T(8,128)S(1)}, u32[]{:S(2)}, u32[]{:S(2)}) collective-permute-start(f32[5,256]{1,0:T(8,128)S(1)} %get-tuple-element.34), channel_id=1, source_target_pairs={{2,496},{3,497},{0,498},{1,499},{6,500},{7,501},{4,502},{5,503},{1... | collective-permute-start | bytes 15368 | tf_op jit(solution)/shard_map/ppermute | solution.py:575
  117.8 3.0 %shard_map.134 = f32[3,8192]{1,0:T(4,128)} custom-call(bf16[4,8,64,128]{3,2,1,0:T(8,128)(2,1)S(1)} %all-to-all-done.1.near, bf16[4,8,64,128]{3,2,1,0:T(8,128)(2,1)S(1)} %collective-permute-done.8.other, s32[32]{0:T(128)S(1)} %copy-done.4, s32[64,128]{1,0:T(8,128)S(1)} %bitcast.16, f32[64,128]{1,0:T(8,128)S(1)} %copy-done.5, f32[3,8192]{1,0:T(4,128)S(1)} %copy-done.1, ...), custom_call_target="tpu_custom_call" | custom-call | flops 2147483648 | bytes 1048576 | tf_op jit(solution)/shard_map/pallas_call | solution.py:81
  (30 shorter events, 3.7 us)
Async XLA Ops:
  0.6 0.7 copy-start.6
  4.3 18.8 %collective-permute-start = (bf16[400,128]{1,0:T(8,128)(2,1)}, bf16[400,128]{1,0:T(8,128)(2,1)S(1)}, u32[]{:S(2)}, u32[]{:S(2)}) collective-permute-start(bf16[400,128]{1,0:T(8,128)(2,1)} %get-tuple-element.20), channel_id=1, source_target_pairs={{0,2},{2,0},{1,3},{3,1},{4,6},{6,4},{5,7},{7,5},{8,10},{10,8},{9,1... | collective-permute-start | bytes 307208 | tf_op jit(solution)/shard_map/ppermute | solution.py:73
  25.0 4.6 %copy-start = (f32[9,16,256]{2,1,0:T(8,128)S(1)}, f32[9,16,256]{2,1,0:T(8,128)}, u32[]{:S(2)}) copy-start(f32[9,16,256]{2,1,0:T(8,128)} %get-tuple-element.21.own) | copy-start | bytes 442372
  25.0 19.2 %all-to-all-start = ((bf16[4,800,128]{2,1,0:T(8,128)(2,1)}), bf16[4,800,128]{2,1,0:T(8,128)(2,1)S(1)}, u32[]{:S(2)}, u32[]{:S(2)}) async-start(bf16[4,800,128]{2,1,0:T(8,128)(2,1)} %broadcast_in_dim.2), calls=%async_computation | async-start | bytes 1638400 | tf_op jit(solution)/shard_map/all_to_all | solution.py:475
  29.6 14.6 %collective-permute-start.1 = (f32[9,16,256]{2,1,0:T(8,128)S(1)}, f32[9,16,256]{2,1,0:T(8,128)S(1)}, u32[]{:S(2)}, u32[]{:S(2)}) collective-permute-start(f32[9,16,256]{2,1,0:T(8,128)S(1)} %copy-done), channel_id=1, source_target_pairs={{0,2},{2,0},{1,3},{3,1},{4,6},{6,4},{5,7},{7,5},{8,10},{10,8},{9,1... | collective-permute-start | bytes 442376 | tf_op jit(solution)/shard_map/ppermute | solution.py:73
  44.2 14.5 %collective-permute-start.2 = (bf16[4,800,128]{2,1,0:T(8,128)(2,1)S(1)}, bf16[4,800,128]{2,1,0:T(8,128)(2,1)S(1)}, u32[]{:S(2)}, u32[]{:S(2)}) collective-permute-start(bf16[4,800,128]{2,1,0:T(8,128)(2,1)S(1)} %all-to-all-done), channel_id=1, source_target_pairs={{0,1},{1,0},{2,3},{3,2},{4,5},{5,4},{6,7},{7,6},{8,9},{9,8},{10,11... | collective-permute-start | bytes 2457608 | tf_op jit(solution)/shard_map/ppermute | solution.py:73
  50.1 8.6 %collective-permute-start.3 = (f32[9,16,256]{2,1,0:T(8,128)S(1)}, f32[9,16,256]{2,1,0:T(8,128)S(1)}, u32[]{:S(2)}, u32[]{:S(2)}) collective-permute-start(f32[9,16,256]{2,1,0:T(8,128)S(1)} %get-tuple-element.24), channel_id=1, source_target_pairs={{0,1},{1,0},{2,3},{3,2},{4,5},{5,4},{6,7},{7,6},{8,9},{9,8},{10,11... | collective-permute-start | bytes 442376 | tf_op jit(solution)/shard_map/ppermute | solution.py:73
  52.0 6.6 %collective-permute-start.4 = (f32[4,16,256]{2,1,0:T(8,128)S(1)}, f32[4,16,256]{2,1,0:T(8,128)S(1)}, u32[]{:S(2)}, u32[]{:S(2)}) collective-permute-start(f32[4,16,256]{2,1,0:T(8,128)S(1)} %get-tuple-element.25), channel_id=1, source_target_pairs={{1,4},{4,1},{3,6},{6,3},{5,8},{8,5},{7,10},{10,7},{9,12},{12,9},{1... | collective-permute-start | bytes 196616 | tf_op jit(solution)/shard_map/ppermute | solution.py:525
  61.7 26.9 %collective-permute-start.5 = (f32[12,16,256]{2,1,0:T(8,128)S(1)}, f32[12,16,256]{2,1,0:T(8,128)S(1)}, u32[]{:S(2)}, u32[]{:S(2)}) collective-permute-start(f32[12,16,256]{2,1,0:T(8,128)S(1)} %get-tuple-element.28), channel_id=1, source_target_pairs={{1,4},{4,1},{3,6},{6,3},{5,8},{8,5},{7,10},{10,7},{9,12},{12,9},{1... | collective-permute-start | bytes 589832 | tf_op jit(solution)/shard_map/ppermute | solution.py:553
  64.6 24.0 %collective-permute-start.6 = (f32[9,16,256]{2,1,0:T(8,128)S(1)}, f32[9,16,256]{2,1,0:T(8,128)S(1)}, u32[]{:S(2)}, u32[]{:S(2)}) collective-permute-start(f32[9,16,256]{2,1,0:T(8,128)S(1)} %get-tuple-element.29), channel_id=1, source_target_pairs={{0,1},{1,0},{2,3},{3,2},{4,5},{5,4},{6,7},{7,6},{8,9},{9,8},{10,11... | collective-permute-start | bytes 442376 | tf_op jit(solution)/shard_map/ppermute | solution.py:73
  89.9 11.3 %all-to-all-start.1 = ((bf16[4,8,64,128]{3,2,1,0:T(8,128)(2,1)}), bf16[4,8,64,128]{3,2,1,0:T(8,128)(2,1)S(1)}, u32[]{:S(2)}, u32[]{:S(2)}) async-start(bf16[4,8,64,128]{3,2,1,0:T(8,128)(2,1)} %get-tuple-element.32), calls=%async_computation.1 | async-start | bytes 1048576 | tf_op jit(solution)/shard_map/all_to_all | solution.py:565
  93.4 12.3 %collective-permute-start.7 = (f32[4,2,16,256]{3,2,1,0:T(8,128)S(1)}, f32[4,2,16,256]{3,2,1,0:T(8,128)S(1)}, u32[]{:S(2)}, u32[]{:S(2)}) collective-permute-start(f32[4,2,16,256]{3,2,1,0:T(8,128)S(1)} %get-tuple-element.31), channel_id=1, source_target_pairs={{0,1},{1,0},{2,3},{3,2},{4,5},{5,4},{6,7},{7,6},{8,9},{9,8},{10,11... | collective-permute-start | bytes 393224 | tf_op jit(solution)/shard_map/ppermute | solution.py:73
  101.2 6.0 %collective-permute-start.8 = (bf16[4,8,64,128]{3,2,1,0:T(8,128)(2,1)S(1)}, bf16[4,8,64,128]{3,2,1,0:T(8,128)(2,1)S(1)}, u32[]{:S(2)}, u32[]{:S(2)}) collective-permute-start(bf16[4,8,64,128]{3,2,1,0:T(8,128)(2,1)S(1)} %all-to-all-done.1.near), channel_id=1, source_target_pairs={{0,1},{1,0},{2,3},{3,2},{4,5},{5,4},{6,7},{7,6},{8,9},{9,8},{10,11... | collective-permute-start | bytes 1572872 | tf_op jit(solution)/shard_map/ppermute | solution.py:73
  107.0 10.7 %copy-start.1 = (f32[3,8192]{1,0:T(4,128)S(1)}, f32[3,8192]{1,0:T(4,128)}, u32[]{:S(2)}) copy-start(f32[3,8192]{1,0:T(4,128)} %vel_in.1) | copy-start | bytes 294916
  107.0 10.7 %copy-start.2 = (f32[8192]{0:T(1024)S(1)}, f32[8192]{0:T(1024)}, u32[]{:S(2)}) copy-start(f32[8192]{0:T(1024)} %param.14) | copy-start | bytes 98308
  107.0 10.7 %copy-start.3 = (s32[8192]{0:T(1024)S(1)}, s32[8192]{0:T(1024)}, u32[]{:S(2)}) copy-start(s32[8192]{0:T(1024)} %param.15) | copy-start | bytes 98308
  107.0 10.7 %copy-start.5 = (f32[64,128]{1,0:T(8,128)S(1)}, f32[64,128]{1,0:T(8,128)}, u32[]{:S(2)}) copy-start(f32[64,128]{1,0:T(8,128)} %get-tuple-element.33.keep) | copy-start | bytes 98308
  109.1 11.7 %collective-permute-start.10 = (f32[5,256]{1,0:T(8,128)S(1)}, f32[5,256]{1,0:T(8,128)S(1)}, u32[]{:S(2)}, u32[]{:S(2)}) collective-permute-start(f32[5,256]{1,0:T(8,128)S(1)} %get-tuple-element.35), channel_id=1, source_target_pairs={{0,16},{1,17},{2,18},{3,19},{4,20},{5,21},{6,22},{7,23},{8,24},{9,... | collective-permute-start | bytes 15368 | tf_op jit(solution)/shard_map/ppermute | solution.py:576
  111.0 6.7 %copy-start.4 = (s32[32]{0:T(128)S(1)}, s32[32]{0:T(128)}, u32[]{:S(2)}) copy-start(s32[32]{0:T(128)} %tiles_in.1) | copy-start | bytes 388
  111.0 9.8 %collective-permute-start.9 = (f32[5,256]{1,0:T(8,128)S(1)}, f32[5,256]{1,0:T(8,128)S(1)}, u32[]{:S(2)}, u32[]{:S(2)}) collective-permute-start(f32[5,256]{1,0:T(8,128)S(1)} %get-tuple-element.34), channel_id=1, source_target_pairs={{2,496},{3,497},{0,498},{1,499},{6,500},{7,501},{4,502},{5,503},{1... | collective-permute-start | bytes 15368 | tf_op jit(solution)/shard_map/ppermute | solution.py:575

commit v3 on v2

--- a/solution.py
+++ b/solution.py
@@ -147,7 +147,7 @@
     pay[6 * ROWS : 6 * ROWS + 16, :] = tsc[...].astype(BF16)
     slots = jnp.concatenate([lists[0:1, :], lists[1:2, :]], axis=1)
     lane512 = lax.broadcasted_iota(I32, (1, 2 * MIG), 1)
-    ends = jnp.where(lane512 < MIG, mig[0:1, :], mig[1:2, :] + MIG)
+    ends = jnp.where(lane512 < MIG, mig[:, 0:1], mig[:, 1:2] + MIG)
     valid = jnp.where(lane512 < ends, F32(1.0), F32(0.0))
     low = (rows_iota(128, 2 * MIG) == (slots & 127)).astype(F32).astype(BF16)
     row_mask = rows_iota(ROWS, 2 * MIG) == (slots >> 7)
@@ -281,13 +281,14 @@
     add_deposits(pays, acc, *scratch)
 
 
-def velocity_kernel(
-    pays, before, own, far, side, edge, u_out, por_out, flux_y, flux_c, wide, flux, acc, *scratch
-):
+def second_deposit_kernel(pays, before, acc, *scratch):
+    acc[...] = before[...]
+    add_deposits(pays, acc, *scratch)
+
+
+def velocity_kernel(acc, own, far, side, edge, u_out, por_out, flux_y, flux_c, wide, flux):
     c = lax.axis_index("c")
     native = lax.axis_index("z") == c
-    acc[...] = before[...]
-    add_deposits(pays, acc, *scratch)
 
     def amount(k):
         halves = []
@@ -338,7 +339,7 @@
         flux[k, 3:7] = por_in[...] * u_in[k]
         for i in range(3):
             flux[k, 7 * c + i] = from_y[3 * k + i]
-            flux[k, 7 * (1 - c) + i] = from_c[3 * k + i]
+            flux[k, 7 * (1 - c) + i] = from_c[1 - c, 3 * k + i]
     for i in range(3):
         pres[7 * c + i] = from_y[9 + i]
     for i in range(2):
@@ -495,7 +496,7 @@
     pay, fpay, keep = call(
         pack_kernel,
         [((PAY_ROWS, 128), BF16), ((9,) + plane, F32), ((ROWS, 128), F32)],
-        [parcel_vel, vol, rate, cell, tiles, parcel_count, leave_lists, mig_counts, fluid_vel, pressure],
+        [parcel_vel, vol, rate, cell, tiles, parcel_count, leave_lists, mig_counts.reshape(1, 2), fluid_vel, pressure],
         scratch=[
             pltpu.VMEM((3, PCAP), F32),
             pltpu.VMEM((ROWS, 128), F32),
@@ -504,7 +505,7 @@
             pltpu.VMEM((1, TILES), I32),
             pltpu.SMEM((1,), I32),
             pltpu.VMEM((2, MIG), I32),
-            pltpu.VMEM((2, 1), I32),
+            pltpu.VMEM((1, 2), I32),
             pltpu.VMEM((3, ROWS, 128), F32),
             pltpu.VMEM((16, 128), F32),
             pltpu.SemaphoreType.DMA((12,)),
@@ -515,14 +516,6 @@
     pay_far = swap(pay, "z")
     fpay_far = swap(fpay, "z")
     pays = over_y(jnp.concatenate([pay, pay_far]))
-    pays, fpay_far = lax.optimization_barrier((pays, fpay_far))
-    edge, side = call(
-        edge_kernel, [((4,) + plane, F32), ((9,) + plane, F32)], [fpay, fpay_far]
-    )
-    route = halo_route()
-    pays_c = swap(pays, "c")
-    side = swap(side, "c")
-    edge = lax.ppermute(edge, ALL, route)
     deposit_scratch = [
         pltpu.VMEM((SOURCES * SCR_ROWS, 128), F32),
         pltpu.VMEM((SOURCES, 128), I32),
@@ -536,22 +529,31 @@
         [(sums_shape, F32)],
         [pays.reshape(SOURCES, PAY_ROWS, 128)],
         scratch=deposit_scratch,
-        flops=1 << 31,
+    flops=1 << 36,
+    )
+    pays_c = swap(pays, "c")
+    fpay_far, sums = lax.optimization_barrier((fpay_far, sums))
+    edge, side = call(
+        edge_kernel, [((4,) + plane, F32), ((9,) + plane, F32)], [fpay, fpay_far]
+    )
+    route = halo_route()
+    side = swap(side, "c")
+    edge = lax.ppermute(edge, ALL, route)
+    (sums,) = call(
+        second_deposit_kernel,
+        [(sums_shape, F32)],
+        [pays_c.reshape(SOURCES, PAY_ROWS, 128), sums],
+        scratch=deposit_scratch,
+        flops=1 << 36,
     )
     u_star, porosity, flux_y, flux_c = call(
         velocity_kernel,
         [((3, 4) + plane, F32), ((4,) + plane, F32), ((12,) + plane, F32), ((9,) + plane, F32)],
-        [pays_c.reshape(SOURCES, PAY_ROWS, 128), sums, fpay, fpay_far, side, edge],
-        scratch=[
-            pltpu.VMEM((4, 6) + plane, F32),
-            pltpu.VMEM((3, 4) + plane, F32),
-            pltpu.VMEM(sums_shape, F32),
-        ]
-        + deposit_scratch,
-        flops=1 << 31,
+        [sums, fpay, fpay_far, side, edge],
+        scratch=[pltpu.VMEM((4, 6) + plane, F32), pltpu.VMEM((3, 4) + plane, F32)],
     )
     from_y = lax.ppermute(flux_y, ALL, route)
-    from_c = swap(flux_c, "c")
+    from_c = lax.all_gather(flux_c, "c", axis=0)
     fields, kept, sent = call(
         fluid_kernel,
         [((N_Y, OWN_BLOCKS, 64, 128), BF16), ((4, 2) + plane, F32), ((4, 2) + plane, F32)],

time: 122 us -> 116 us (0.951)
  blocking collectives: 0 us -> 21.9 us
  starting transfers between devices: 90.1 us -> 69.1 us
  waiting for transfers between devices: 11.1 us -> 4.92 us
    all_gather x0 -> x1, blocking collectives: none -> 21.9 us  [per_device(): from_c = lax.all_gather(flux_c, 'c', axis=0)]
    ppermute x7 -> x6, starting transfers between devices: 66.6 us -> 46.3 us  [swap(): return lax.ppermute(values, axis, [(0, 1), (1, 0)])]
    ppermute x7 -> x6, waiting for transfers between devices: 6.61 us -> 2.77 us  [swap(): return lax.ppermute(values, axis, [(0, 1), (1, 0)])]
    all_to_all x1, waiting for transfers between devices: 4.5 us -> 2.14 us  [per_device(): fields = lax.all_to_all(fields, 'y', 0, 0)]
    pallas_call x7 -> x8, Pallas kernels: 14.1 us -> 14.1 us  [call(): pl.pallas_call(kernel, out_shape=[jax.ShapeDtypeStruct(shape, dtype) for...]
  transfers between devices with their start and end apart: 13 -> 12, of which waited for: 5 -> 3; matrix products, arithmetic and copies ran while one was open for 1% -> 1% of each run, Pallas kernels for 5% -> 7%
where the time goes in v3:
time: 116 us; the launch traced here: 115 us
  starting transfers between devices  69.1 us (60%)
  blocking collectives  21.9 us (19%)
  Pallas kernels  14.1 us (12%)
  waiting for transfers between devices  4.92 us (4%)
  other arithmetic  2.19 us (2%)
  local copies, waits for them, and re-layouts  1.64 us (1%)
  between operations  1.55 us (1%)
    ppermute x6, starting transfers between devices, swap(): return lax.ppermute(values, axis, [(0, 1), (1, 0)])  46.3 us
    all_gather x1, blocking collectives, per_device(): from_c = lax.all_gather(flux_c, 'c', axis=0)  21.9 us
    pallas_call x8, Pallas kernels, call(): pl.pallas_call(kernel, out_shape=[jax.ShapeDtypeStruct(shape, dtype) for...  14.1 us
    ppermute x1, starting transfers between devices, per_device(): arrive0 = lax.ppermute(out0, ALL, leave_route(-1))  6.68 us
    all_to_all x1, starting transfers between devices, over_y(): return lax.all_to_all(copies, 'y', 0, 0, tiled=False)  4.57 us
    ppermute x1, starting transfers between devices, per_device(): edge = lax.ppermute(edge, ALL, route)  3.53 us
    all_to_all x1, starting transfers between devices, per_device(): fields = lax.all_to_all(fields, 'y', 0, 0)  3.47 us
    ppermute x6, waiting for transfers between devices, swap(): return lax.ppermute(values, axis, [(0, 1), (1, 0)])  2.77 us
  transfers between devices with their start and end apart: 12, of which 3 were waited for; matrix products, arithmetic and copies ran while one was open for 1% of the time, Pallas kernels for 7%

profile of v3, /device:TPU:1, one launch (start us, length us, event | category | flops | bytes accessed | tf_op | source)
XLA Modules:
  0.0 115.4 jit_solution(450767005618367678)
XLA Ops:
  1.3 2.3 %shard_map.129 = (bf16[400,128]{1,0:T(8,128)(2,1)}, f32[9,16,256]{2,1,0:T(8,128)}, f32[64,128]{1,0:T(8,128)}) custom-call(f32[3,8192]{1,0:T(4,128)} %vel_in.1, f32[64,128]{1,0:T(8,128)} %bitcast.22, f32[64,128]{1,0:T(8,128)} %bitcast.16, s32[64,128]{1,0:T(8,128)} %bitcast.18, s32[1,32]{1,0:T(1,128)} %bitcast.20, s32[1]{0:T(128)S(6)} %copy.16.refs_5_, ...), custom_call_target="tpu_custom_call" | custom-call | bytes 1048576 | tf_op jit(solution)/shard_map/pallas_call | solution.py:81
  3.6 16.3 %collective-permute-start = (bf16[400,128]{1,0:T(8,128)(2,1)}, bf16[400,128]{1,0:T(8,128)(2,1)S(1)}, u32[]{:S(2)}, u32[]{:S(2)}) collective-permute-start(bf16[400,128]{1,0:T(8,128)(2,1)} %get-tuple-element.20), channel_id=1, source_target_pairs={{0,2},{2,0},{1,3},{3,1},{4,6},{6,4},{5,7},{7,5},{8,10},{10,8},{9,1... | collective-permute-start | bytes 307208 | tf_op jit(solution)/shard_map/ppermute | solution.py:73
  19.9 2.5 %collective-permute-done = bf16[400,128]{1,0:T(8,128)(2,1)S(1)} collective-permute-done((bf16[400,128]{1,0:T(8,128)(2,1)}, bf16[400,128]{1,0:T(8,128)(2,1)S(1)}, u32[]{:S(2)}, u32[]{:S(2)}) %collective-permute-start) | collective-permute-done | bytes 102432 | tf_op jit(solution)/shard_map/ppermute | solution.py:73
  22.4 0.9 pad_maximum_fusion
  23.3 1.0 broadcast_in_dim.2
  24.3 4.6 %all-to-all-start = ((bf16[4,800,128]{2,1,0:T(8,128)(2,1)}), bf16[4,800,128]{2,1,0:T(8,128)(2,1)S(1)}, u32[]{:S(2)}, u32[]{:S(2)}) async-start(bf16[4,800,128]{2,1,0:T(8,128)(2,1)} %broadcast_in_dim.2), calls=%async_computation | async-start | bytes 1638400 | tf_op jit(solution)/shard_map/all_to_all | solution.py:476
  28.9 11.8 %collective-permute-start.2 = (f32[9,16,256]{2,1,0:T(8,128)S(1)}, f32[9,16,256]{2,1,0:T(8,128)S(1)}, u32[]{:S(2)}, u32[]{:S(2)}) collective-permute-start(f32[9,16,256]{2,1,0:T(8,128)S(1)} %copy-done), channel_id=1, source_target_pairs={{0,2},{2,0},{1,3},{3,1},{4,6},{6,4},{5,7},{7,5},{8,10},{10,8},{9,1... | collective-permute-start | bytes 442376 | tf_op jit(solution)/shard_map/ppermute | solution.py:73
  40.7 5.2 %collective-permute-start.1 = (bf16[4,800,128]{2,1,0:T(8,128)(2,1)S(1)}, bf16[4,800,128]{2,1,0:T(8,128)(2,1)S(1)}, u32[]{:S(2)}, u32[]{:S(2)}) collective-permute-start(bf16[4,800,128]{2,1,0:T(8,128)(2,1)S(1)} %all-to-all-done), channel_id=1, source_target_pairs={{0,1},{1,0},{2,3},{3,2},{4,5},{5,4},{6,7},{7,6},{8,9},{9,8},{10,11... | collective-permute-start | bytes 2457608 | tf_op jit(solution)/shard_map/ppermute | solution.py:73
  45.9 2.4 %shard_map.130.before = f32[9,80,128]{2,1,0:T(8,128)S(1)} custom-call(bf16[8,400,128]{2,1,0:T(8,128)(2,1)S(1)} %bitcast.15), custom_call_target="tpu_custom_call" | custom-call | flops 68719476736 | bytes 1048576 | tf_op jit(solution)/shard_map/pallas_call | solution.py:81
  48.4 2.4 %collective-permute-start.3 = (f32[9,16,256]{2,1,0:T(8,128)S(1)}, f32[9,16,256]{2,1,0:T(8,128)S(1)}, u32[]{:S(2)}, u32[]{:S(2)}) collective-permute-start(f32[9,16,256]{2,1,0:T(8,128)S(1)} %get-tuple-element.24), channel_id=1, source_target_pairs={{0,1},{1,0},{2,3},{3,2},{4,5},{5,4},{6,7},{7,6},{8,9},{9,8},{10,11... | collective-permute-start | bytes 442376 | tf_op jit(solution)/shard_map/ppermute | solution.py:73
  50.8 3.5 %collective-permute-start.4 = (f32[4,16,256]{2,1,0:T(8,128)S(1)}, f32[4,16,256]{2,1,0:T(8,128)S(1)}, u32[]{:S(2)}, u32[]{:S(2)}) collective-permute-start(f32[4,16,256]{2,1,0:T(8,128)S(1)} %get-tuple-element.25), channel_id=1, source_target_pairs={{1,4},{4,1},{3,6},{6,3},{5,8},{8,5},{7,10},{10,7},{9,12},{12,9},{1... | collective-permute-start | bytes 196616 | tf_op jit(solution)/shard_map/ppermute | solution.py:541
  54.3 2.8 %shard_map.131.acc = f32[9,80,128]{2,1,0:T(8,128)S(1)} custom-call(bf16[8,400,128]{2,1,0:T(8,128)(2,1)S(1)} %bitcast.21, f32[9,80,128]{2,1,0:T(8,128)S(1)} %shard_map.130.before), custom_call_target="tpu_custom_call" | custom-call | flops 68719476736 | bytes 1048576 | tf_op jit(solution)/shard_map/pallas_call | solution.py:81
  57.6 2.7 %collective-permute-start.5 = (f32[12,16,256]{2,1,0:T(8,128)S(1)}, f32[12,16,256]{2,1,0:T(8,128)S(1)}, u32[]{:S(2)}, u32[]{:S(2)}) collective-permute-start(f32[12,16,256]{2,1,0:T(8,128)S(1)} %get-tuple-element.28), channel_id=1, source_target_pairs={{1,4},{4,1},{3,6},{6,3},{5,8},{8,5},{7,10},{10,7},{9,12},{12,9},{1... | collective-permute-start | bytes 589832 | tf_op jit(solution)/shard_map/ppermute | solution.py:555
  60.2 21.9 %all-gather = f32[18,16,256]{2,1,0:T(8,128)S(1)} all-gather(f32[9,16,256]{2,1,0:T(8,128)S(1)} %get-tuple-element.29), channel_id=2, replica_groups=mesh['blk'=32,'y'=4,'z'=2,'c'=2] {'c'}, dimensions={0}, use_global_device_ids=true | all-gather | bytes 442368 | tf_op jit(solution)/shard_map/all_gather | solution.py:556
  82.1 1.3 %shard_map.134 = (bf16[4,8,64,128]{3,2,1,0:T(8,128)(2,1)}, f32[4,2,16,256]{3,2,1,0:T(8,128)S(1)}, f32[4,2,16,256]{3,2,1,0:T(8,128)S(1)}) custom-call(f32[3,4,16,256]{3,2,1,0:T(8,128)S(1)} %get-tuple-element.26.u_in, f32[4,16,256]{2,1,0:T(8,128)S(1)} %get-tuple-element.27.por_in, f32[9,16,256]{2,1,0:T(8,128)S(1)} %copy-done, ...), custom_call_target="tpu_custom_call" | custom-call | bytes 1048576 | tf_op jit(solution)/shard_map/pallas_call | solution.py:81
  83.4 3.5 %all-to-all-start.1 = ((bf16[4,8,64,128]{3,2,1,0:T(8,128)(2,1)}), bf16[4,8,64,128]{3,2,1,0:T(8,128)(2,1)S(1)}, u32[]{:S(2)}, u32[]{:S(2)}) async-start(bf16[4,8,64,128]{3,2,1,0:T(8,128)(2,1)} %get-tuple-element.32), calls=%async_computation.1 | async-start | bytes 1048576 | tf_op jit(solution)/shard_map/all_to_all | solution.py:567
  86.9 4.8 %collective-permute-start.6 = (f32[4,2,16,256]{3,2,1,0:T(8,128)S(1)}, f32[4,2,16,256]{3,2,1,0:T(8,128)S(1)}, u32[]{:S(2)}, u32[]{:S(2)}) collective-permute-start(f32[4,2,16,256]{3,2,1,0:T(8,128)S(1)} %get-tuple-element.31), channel_id=1, source_target_pairs={{0,1},{1,0},{2,3},{3,2},{4,5},{5,4},{6,7},{7,6},{8,9},{9,8},{10,11... | collective-permute-start | bytes 393224 | tf_op jit(solution)/shard_map/ppermute | solution.py:73
  91.7 2.1 %all-to-all-done.1.near = bf16[4,8,64,128]{3,2,1,0:T(8,128)(2,1)S(1)} async-done(((bf16[4,8,64,128]{3,2,1,0:T(8,128)(2,1)}), bf16[4,8,64,128]{3,2,1,0:T(8,128)(2,1)S(1)}, u32[]{:S(2)}, u32[]{:S(2)}) %all-to-all-start.1) | async-done | bytes 524320 | tf_op jit(solution)/shard_map/all_to_all | solution.py:567
  93.8 5.9 %collective-permute-start.7 = (bf16[4,8,64,128]{3,2,1,0:T(8,128)(2,1)S(1)}, bf16[4,8,64,128]{3,2,1,0:T(8,128)(2,1)S(1)}, u32[]{:S(2)}, u32[]{:S(2)}) collective-permute-start(bf16[4,8,64,128]{3,2,1,0:T(8,128)(2,1)S(1)} %all-to-all-done.1.near), channel_id=1, source_target_pairs={{0,1},{1,0},{2,3},{3,2},{4,5},{5,4},{6,7},{7,6},{8,9},{9,8},{10,11... | collective-permute-start | bytes 1572872 | tf_op jit(solution)/shard_map/ppermute | solution.py:73
  100.3 0.7 slice_select_fusion
  101.2 1.9 %shard_map.136 = (f32[5,256]{1,0:T(8,128)S(1)}, f32[5,256]{1,0:T(8,128)S(1)}) custom-call(bf16[4,8,64,128]{3,2,1,0:T(8,128)(2,1)S(1)} %all-to-all-done.1.near, bf16[4,8,64,128]{3,2,1,0:T(8,128)(2,1)S(1)} %collective-permute-done.7.other, f32[9,16,256]{2,1,0:T(8,128)S(1)} %copy-done, f32[9,16,256]{2,1,0:T(8,128)S(1)} %collective-permute-done.2.far), custom_call_target="tpu_custom_call" | custom-call | flops 1073741824 | bytes 1048576 | tf_op jit(solution)/shard_map/pallas_call | solution.py:81
  103.1 1.9 %collective-permute-start.9 = (f32[5,256]{1,0:T(8,128)S(1)}, f32[5,256]{1,0:T(8,128)S(1)}, u32[]{:S(2)}, u32[]{:S(2)}) collective-permute-start(f32[5,256]{1,0:T(8,128)S(1)} %get-tuple-element.35), channel_id=1, source_target_pairs={{0,16},{1,17},{2,18},{3,19},{4,20},{5,21},{6,22},{7,23},{8,24},{9,... | collective-permute-start | bytes 15368 | tf_op jit(solution)/shard_map/ppermute | solution.py:578
  105.0 6.7 %collective-permute-start.8 = (f32[5,256]{1,0:T(8,128)S(1)}, f32[5,256]{1,0:T(8,128)S(1)}, u32[]{:S(2)}, u32[]{:S(2)}) collective-permute-start(f32[5,256]{1,0:T(8,128)S(1)} %get-tuple-element.34), channel_id=1, source_target_pairs={{2,496},{3,497},{0,498},{1,499},{6,500},{7,501},{4,502},{5,503},{1... | collective-permute-start | bytes 15368 | tf_op jit(solution)/shard_map/ppermute | solution.py:577
  111.8 3.0 %shard_map.135 = f32[3,8192]{1,0:T(4,128)} custom-call(bf16[4,8,64,128]{3,2,1,0:T(8,128)(2,1)S(1)} %all-to-all-done.1.near, bf16[4,8,64,128]{3,2,1,0:T(8,128)(2,1)S(1)} %collective-permute-done.7.other, s32[32]{0:T(128)S(1)} %copy-done.4, s32[64,128]{1,0:T(8,128)S(1)} %bitcast.19, f32[64,128]{1,0:T(8,128)S(1)} %copy-done.5, f32[3,8192]{1,0:T(4,128)S(1)} %copy-done.1, ...), custom_call_target="tpu_custom_call" | custom-call | flops 2147483648 | bytes 1048576 | tf_op jit(solution)/shard_map/pallas_call | solution.py:81
  (27 shorter events, 1.9 us)
Async XLA Ops:
  3.6 18.8 %collective-permute-start = (bf16[400,128]{1,0:T(8,128)(2,1)}, bf16[400,128]{1,0:T(8,128)(2,1)S(1)}, u32[]{:S(2)}, u32[]{:S(2)}) collective-permute-start(bf16[400,128]{1,0:T(8,128)(2,1)} %get-tuple-element.20), channel_id=1, source_target_pairs={{0,2},{2,0},{1,3},{3,1},{4,6},{6,4},{5,7},{7,5},{8,10},{10,8},{9,1... | collective-permute-start | bytes 307208 | tf_op jit(solution)/shard_map/ppermute | solution.py:73
  24.3 4.6 %copy-start = (f32[9,16,256]{2,1,0:T(8,128)S(1)}, f32[9,16,256]{2,1,0:T(8,128)}, u32[]{:S(2)}) copy-start(f32[9,16,256]{2,1,0:T(8,128)} %get-tuple-element.21.own) | copy-start | bytes 442372
  24.3 16.3 %all-to-all-start = ((bf16[4,800,128]{2,1,0:T(8,128)(2,1)}), bf16[4,800,128]{2,1,0:T(8,128)(2,1)S(1)}, u32[]{:S(2)}, u32[]{:S(2)}) async-start(bf16[4,800,128]{2,1,0:T(8,128)(2,1)} %broadcast_in_dim.2), calls=%async_computation | async-start | bytes 1638400 | tf_op jit(solution)/shard_map/all_to_all | solution.py:476
  28.9 19.4 %collective-permute-start.2 = (f32[9,16,256]{2,1,0:T(8,128)S(1)}, f32[9,16,256]{2,1,0:T(8,128)S(1)}, u32[]{:S(2)}, u32[]{:S(2)}) collective-permute-start(f32[9,16,256]{2,1,0:T(8,128)S(1)} %copy-done), channel_id=1, source_target_pairs={{0,2},{2,0},{1,3},{3,1},{4,6},{6,4},{5,7},{7,5},{8,10},{10,8},{9,1... | collective-permute-start | bytes 442376 | tf_op jit(solution)/shard_map/ppermute | solution.py:73
  40.7 13.6 %collective-permute-start.1 = (bf16[4,800,128]{2,1,0:T(8,128)(2,1)S(1)}, bf16[4,800,128]{2,1,0:T(8,128)(2,1)S(1)}, u32[]{:S(2)}, u32[]{:S(2)}) collective-permute-start(bf16[4,800,128]{2,1,0:T(8,128)(2,1)S(1)} %all-to-all-done), channel_id=1, source_target_pairs={{0,1},{1,0},{2,3},{3,2},{4,5},{5,4},{6,7},{7,6},{8,9},{9,8},{10,11... | collective-permute-start | bytes 2457608 | tf_op jit(solution)/shard_map/ppermute | solution.py:73
  48.4 8.8 %collective-permute-start.3 = (f32[9,16,256]{2,1,0:T(8,128)S(1)}, f32[9,16,256]{2,1,0:T(8,128)S(1)}, u32[]{:S(2)}, u32[]{:S(2)}) collective-permute-start(f32[9,16,256]{2,1,0:T(8,128)S(1)} %get-tuple-element.24), channel_id=1, source_target_pairs={{0,1},{1,0},{2,3},{3,2},{4,5},{5,4},{6,7},{7,6},{8,9},{9,8},{10,11... | collective-permute-start | bytes 442376 | tf_op jit(solution)/shard_map/ppermute | solution.py:73
  50.8 6.4 %collective-permute-start.4 = (f32[4,16,256]{2,1,0:T(8,128)S(1)}, f32[4,16,256]{2,1,0:T(8,128)S(1)}, u32[]{:S(2)}, u32[]{:S(2)}) collective-permute-start(f32[4,16,256]{2,1,0:T(8,128)S(1)} %get-tuple-element.25), channel_id=1, source_target_pairs={{1,4},{4,1},{3,6},{6,3},{5,8},{8,5},{7,10},{10,7},{9,12},{12,9},{1... | collective-permute-start | bytes 196616 | tf_op jit(solution)/shard_map/ppermute | solution.py:541
  57.6 24.6 %collective-permute-start.5 = (f32[12,16,256]{2,1,0:T(8,128)S(1)}, f32[12,16,256]{2,1,0:T(8,128)S(1)}, u32[]{:S(2)}, u32[]{:S(2)}) collective-permute-start(f32[12,16,256]{2,1,0:T(8,128)S(1)} %get-tuple-element.28), channel_id=1, source_target_pairs={{1,4},{4,1},{3,6},{6,3},{5,8},{8,5},{7,10},{10,7},{9,12},{12,9},{1... | collective-permute-start | bytes 589832 | tf_op jit(solution)/shard_map/ppermute | solution.py:555
  83.4 10.4 %all-to-all-start.1 = ((bf16[4,8,64,128]{3,2,1,0:T(8,128)(2,1)}), bf16[4,8,64,128]{3,2,1,0:T(8,128)(2,1)S(1)}, u32[]{:S(2)}, u32[]{:S(2)}) async-start(bf16[4,8,64,128]{3,2,1,0:T(8,128)(2,1)} %get-tuple-element.32), calls=%async_computation.1 | async-start | bytes 1048576 | tf_op jit(solution)/shard_map/all_to_all | solution.py:567
  86.9 12.8 %collective-permute-start.6 = (f32[4,2,16,256]{3,2,1,0:T(8,128)S(1)}, f32[4,2,16,256]{3,2,1,0:T(8,128)S(1)}, u32[]{:S(2)}, u32[]{:S(2)}) collective-permute-start(f32[4,2,16,256]{3,2,1,0:T(8,128)S(1)} %get-tuple-element.31), channel_id=1, source_target_pairs={{0,1},{1,0},{2,3},{3,2},{4,5},{5,4},{6,7},{7,6},{8,9},{9,8},{10,11... | collective-permute-start | bytes 393224 | tf_op jit(solution)/shard_map/ppermute | solution.py:73
  93.8 7.4 %collective-permute-start.7 = (bf16[4,8,64,128]{3,2,1,0:T(8,128)(2,1)S(1)}, bf16[4,8,64,128]{3,2,1,0:T(8,128)(2,1)S(1)}, u32[]{:S(2)}, u32[]{:S(2)}) collective-permute-start(bf16[4,8,64,128]{3,2,1,0:T(8,128)(2,1)S(1)} %all-to-all-done.1.near), channel_id=1, source_target_pairs={{0,1},{1,0},{2,3},{3,2},{4,5},{5,4},{6,7},{7,6},{8,9},{9,8},{10,11... | collective-permute-start | bytes 1572872 | tf_op jit(solution)/shard_map/ppermute | solution.py:73
  101.0 10.7 %copy-start.1 = (f32[3,8192]{1,0:T(4,128)S(1)}, f32[3,8192]{1,0:T(4,128)}, u32[]{:S(2)}) copy-start(f32[3,8192]{1,0:T(4,128)} %vel_in.1) | copy-start | bytes 294916
  101.0 10.7 %copy-start.2 = (f32[8192]{0:T(1024)S(1)}, f32[8192]{0:T(1024)}, u32[]{:S(2)}) copy-start(f32[8192]{0:T(1024)} %param.14) | copy-start | bytes 98308
  101.0 10.7 %copy-start.3 = (s32[8192]{0:T(1024)S(1)}, s32[8192]{0:T(1024)}, u32[]{:S(2)}) copy-start(s32[8192]{0:T(1024)} %param.15) | copy-start | bytes 98308
  101.0 10.7 %copy-start.5 = (f32[64,128]{1,0:T(8,128)S(1)}, f32[64,128]{1,0:T(8,128)}, u32[]{:S(2)}) copy-start(f32[64,128]{1,0:T(8,128)} %get-tuple-element.33.keep) | copy-start | bytes 98308
  103.1 11.7 %collective-permute-start.9 = (f32[5,256]{1,0:T(8,128)S(1)}, f32[5,256]{1,0:T(8,128)S(1)}, u32[]{:S(2)}, u32[]{:S(2)}) collective-permute-start(f32[5,256]{1,0:T(8,128)S(1)} %get-tuple-element.35), channel_id=1, source_target_pairs={{0,16},{1,17},{2,18},{3,19},{4,20},{5,21},{6,22},{7,23},{8,24},{9,... | collective-permute-start | bytes 15368 | tf_op jit(solution)/shard_map/ppermute | solution.py:578
  105.0 6.7 %copy-start.4 = (s32[32]{0:T(128)S(1)}, s32[32]{0:T(128)}, u32[]{:S(2)}) copy-start(s32[32]{0:T(128)} %tiles_in.1) | copy-start | bytes 388
  105.0 9.8 %collective-permute-start.8 = (f32[5,256]{1,0:T(8,128)S(1)}, f32[5,256]{1,0:T(8,128)S(1)}, u32[]{:S(2)}, u32[]{:S(2)}) collective-permute-start(f32[5,256]{1,0:T(8,128)S(1)} %get-tuple-element.34), channel_id=1, source_target_pairs={{2,496},{3,497},{0,498},{1,499},{6,500},{7,501},{4,502},{5,503},{1... | collective-permute-start | bytes 15368 | tf_op jit(solution)/shard_map/ppermute | solution.py:577

commit v4 on v3

--- a/solution.py
+++ b/solution.py
@@ -1,3 +1,5 @@
+import functools
+
 import jax
 import jax.numpy as jnp
 from jax import lax
@@ -213,9 +215,11 @@
     return at(values, values.ndim - 1, -1)
 
 
-def add_deposits(pays, acc, scr, tile_v, tile_s, picks, sem):
-    first = lax.axis_index("y") * 16 + lax.axis_index("c") * OWN_BLOCKS
-    for s in range(SOURCES):
+def add_deposits(pays, acc, scr, tile_v, tile_s, picks, sem, skip_own=False):
+    y = lax.axis_index("y")
+    first = y * 16 + lax.axis_index("c") * OWN_BLOCKS
+    sources = pays.shape[0]
+    for s in range(sources):
         tile_v[s : s + 1, :] = pays[s, 6 * ROWS : 6 * ROWS + 16, :].astype(F32)[0:1, :].astype(I32)
     copy = pltpu.make_async_copy(tile_v, tile_s, sem)
     copy.start()
@@ -233,18 +237,19 @@
         scr[pl.ds(base + 6 * ROWS, ROWS), :] = code - 128.0
         return carry
 
-    lax.fori_loop(0, SOURCES, widen, 0)
+    lax.fori_loop(0, sources, widen, 0)
     copy.wait()
 
     def choose(s, found):
+        base = first + jnp.where(s // N_Z == y, 1024, 0) if skip_own else first
         for t in range(TILES):
-            block = tile_s[s, t] - first
+            block = tile_s[s, t] - base
             picks[found] = (s * SCR_ROWS + 2 * t) * 16 + block
             mine = jnp.logical_and(block >= 0, block < OWN_BLOCKS)
             found = found + mine.astype(I32)
         return found
 
-    found = lax.fori_loop(0, SOURCES, choose, jnp.int32(0))
+    found = lax.fori_loop(0, sources, choose, jnp.int32(0))
     for i in range(UNROLL):
         picks[found + i] = OWN_BLOCKS
     iota16 = lax.broadcasted_iota(I32, (16, 128), 0).astype(F32)
@@ -281,9 +286,17 @@
     add_deposits(pays, acc, *scratch)
 
 
-def second_deposit_kernel(pays, before, acc, *scratch):
+def next_deposit_kernel(skip_own, pays, before, acc, *scratch):
     acc[...] = before[...]
-    add_deposits(pays, acc, *scratch)
+    add_deposits(pays, acc, *scratch, skip_own=skip_own)
+
+
+def spread_kernel(own, far, both, out):
+    both[0] = own[...]
+    both[1] = far[...]
+    for y in range(N_Y):
+        out[y, 0] = own[...]
+        out[y, 1] = far[...]
 
 
 def velocity_kernel(acc, own, far, side, edge, u_out, por_out, flux_y, flux_c, wide, flux):
@@ -469,11 +482,6 @@
         return carry
 
     lax.fori_loop(0, TILES // 4, some, 0)
-
-
-def over_y(values):
-    copies = jnp.broadcast_to(values[None], (N_Y,) + values.shape)
-    return lax.all_to_all(copies, "y", 0, 0, tiled=False)
 
 
 def per_device(
@@ -515,7 +523,12 @@
     )
     pay_far = swap(pay, "z")
     fpay_far = swap(fpay, "z")
-    pays = over_y(jnp.concatenate([pay, pay_far]))
+    pay_pair, pays = call(
+        spread_kernel,
+        [((N_Z, PAY_ROWS, 128), BF16), ((N_Y, N_Z, PAY_ROWS, 128), BF16)],
+        [pay, pay_far],
+    )
+    pays = lax.all_to_all(pays, "y", 0, 0)
     deposit_scratch = [
         pltpu.VMEM((SOURCES * SCR_ROWS, 128), F32),
         pltpu.VMEM((SOURCES, 128), I32),
@@ -527,9 +540,16 @@
     (sums,) = call(
         first_deposit_kernel,
         [(sums_shape, F32)],
-        [pays.reshape(SOURCES, PAY_ROWS, 128)],
+        [pay_pair],
         scratch=deposit_scratch,
-    flops=1 << 36,
+        flops=1 << 36,
+    )
+    (sums,) = call(
+        functools.partial(next_deposit_kernel, True),
+        [(sums_shape, F32)],
+        [pays.reshape(SOURCES, PAY_ROWS, 128), sums],
+        scratch=deposit_scratch,
+        flops=1 << 36,
     )
     pays_c = swap(pays, "c")
     fpay_far, sums = lax.optimization_barrier((fpay_far, sums))
@@ -540,7 +560,7 @@
     side = swap(side, "c")
     edge = lax.ppermute(edge, ALL, route)
     (sums,) = call(
-        second_deposit_kernel,
+        functools.partial(next_deposit_kernel, False),
         [(sums_shape, F32)],
         [pays_c.reshape(SOURCES, PAY_ROWS, 128), sums],
         scratch=deposit_scratch,

time: 116 us -> 110 us (0.948)
  starting transfers between devices: 69.1 us -> 59.9 us
  waiting for transfers between devices: 4.92 us -> 11.5 us
  blocking collectives: 21.9 us -> 17.4 us
  Pallas kernels: 14.1 us -> 16.7 us
    all_to_all x1, waiting for transfers between devices: 0.01 us -> 7.49 us  [per_device(): pays = lax.all_to_all(pays, 'y', 0, 0)]
    ppermute x6, starting transfers between devices: 46.3 us -> 38.9 us  [swap(): return lax.ppermute(values, axis, [(0, 1), (1, 0)])]
    all_gather x1, blocking collectives: 21.9 us -> 17.4 us  [per_device(): from_c = lax.all_gather(flux_c, 'c', axis=0)]
    pallas_call x8 -> x10, Pallas kernels: 14.1 us -> 16.7 us  [call(): pl.pallas_call(kernel, out_shape=[jax.ShapeDtypeStruct(shape, dtype) for...]
    ppermute x6, waiting for transfers between devices: 2.77 us -> 0.84 us  [swap(): return lax.ppermute(values, axis, [(0, 1), (1, 0)])]
    ppermute x1, starting transfers between devices: 3.53 us -> 2.14 us  [per_device(): edge = lax.ppermute(edge, ALL, route)]
  transfers between devices with their start and end apart: 12 -> 12, of which waited for: 3 -> 5; matrix products, arithmetic and copies ran while one was open for 1% -> 1% of each run, Pallas kernels for 7% -> 10%
where the time goes in v4:
time: 110 us
  starting transfers between devices  59.9 us (54%)
  blocking collectives  17.4 us (16%)
  Pallas kernels  16.7 us (15%)
  waiting for transfers between devices  11.5 us (10%)
  between operations  1.55 us (1%)
  local copies, waits for them, and re-layouts  1.52 us (1%)
  other arithmetic  1.28 us (1%)
    ppermute x6, starting transfers between devices, swap(): return lax.ppermute(values, axis, [(0, 1), (1, 0)])  38.9 us
    all_gather x1, blocking collectives, per_device(): from_c = lax.all_gather(flux_c, 'c', axis=0)  17.4 us
    pallas_call x10, Pallas kernels, call(): pl.pallas_call(kernel, out_shape=[jax.ShapeDtypeStruct(shape, dtype) for...  16.7 us
    all_to_all x1, waiting for transfers between devices, per_device(): pays = lax.all_to_all(pays, 'y', 0, 0)  7.49 us
    ppermute x1, starting transfers between devices, per_device(): arrive0 = lax.ppermute(out0, ALL, leave_route(-1))  6.68 us
    all_to_all x1, starting transfers between devices, per_device(): pays = lax.all_to_all(pays, 'y', 0, 0)  4.44 us
    all_to_all x1, starting transfers between devices, per_device(): fields = lax.all_to_all(fields, 'y', 0, 0)  3.47 us
    all_to_all x1, waiting for transfers between devices, per_device(): fields = lax.all_to_all(fields, 'y', 0, 0)  2.6 us
  transfers between devices with their start and end apart: 12, of which 5 were waited for; matrix products, arithmetic and copies ran while one was open for 1% of the time, Pallas kernels for 10%

profile of v4, /device:TPU:1, one launch (start us, length us, event | category | flops | bytes accessed | tf_op | source)
XLA Modules:
  0.0 109.9 jit_solution(3716561407413102402)
XLA Ops:
  1.3 2.3 %shard_map.129 = (bf16[400,128]{1,0:T(8,128)(2,1)}, f32[9,16,256]{2,1,0:T(8,128)}, f32[64,128]{1,0:T(8,128)}) custom-call(f32[3,8192]{1,0:T(4,128)} %vel_in.1, f32[64,128]{1,0:T(8,128)} %bitcast.22, f32[64,128]{1,0:T(8,128)} %bitcast.16, s32[64,128]{1,0:T(8,128)} %bitcast.18, s32[1,32]{1,0:T(1,128)} %bitcast.20, s32[1]{0:T(128)S(6)} %copy.16.refs_5_, ...), custom_call_target="tpu_custom_call" | custom-call | bytes 1048576 | tf_op jit(solution)/shard_map/pallas_call | solution.py:83
  3.6 16.3 %collective-permute-start = (bf16[400,128]{1,0:T(8,128)(2,1)}, bf16[400,128]{1,0:T(8,128)(2,1)S(1)}, u32[]{:S(2)}, u32[]{:S(2)}) collective-permute-start(bf16[400,128]{1,0:T(8,128)(2,1)} %get-tuple-element.22.own), channel_id=1, source_target_pairs={{0,2},{2,0},{1,3},{3,1},{4,6},{6,4},{5,7},{7,5},{8,10},{10,8},{9,1... | collective-permute-start | bytes 307208 | tf_op jit(solution)/shard_map/ppermute | solution.py:75
  19.8 1.9 %collective-permute-start.2 = (f32[9,16,256]{2,1,0:T(8,128)}, f32[9,16,256]{2,1,0:T(8,128)S(1)}, u32[]{:S(2)}, u32[]{:S(2)}) collective-permute-start(f32[9,16,256]{2,1,0:T(8,128)} %get-tuple-element.24.own), channel_id=1, source_target_pairs={{0,2},{2,0},{1,3},{3,1},{4,6},{6,4},{5,7},{7,5},{8,10},{10,8},{9,1... | collective-permute-start | bytes 442376 | tf_op jit(solution)/shard_map/ppermute | solution.py:75
  22.4 0.9 copy-done.2
  23.3 1.0 shard_map.130
  24.3 4.4 %all-to-all-start = ((bf16[4,2,400,128]{3,2,1,0:T(8,128)(2,1)}), bf16[4,2,400,128]{3,2,1,0:T(8,128)(2,1)S(1)}, u32[]{:S(2)}, u32[]{:S(2)}) async-start(bf16[4,2,400,128]{3,2,1,0:T(8,128)(2,1)} %get-tuple-element.23), calls=%async_computation | async-start | bytes 1638400 | tf_op jit(solution)/shard_map/all_to_all | solution.py:531
  28.8 1.3 %shard_map.131.before = f32[9,80,128]{2,1,0:T(8,128)S(1)} custom-call(bf16[2,400,128]{2,1,0:T(8,128)(2,1)S(1)} %get-tuple-element.25.pays), custom_call_target="tpu_custom_call" | custom-call | flops 68719476736 | bytes 1048576 | tf_op jit(solution)/shard_map/pallas_call | solution.py:83
  30.1 7.5 %all-to-all-done = bf16[4,2,400,128]{3,2,1,0:T(8,128)(2,1)S(1)} async-done(((bf16[4,2,400,128]{3,2,1,0:T(8,128)(2,1)}), bf16[4,2,400,128]{3,2,1,0:T(8,128)(2,1)S(1)}, u32[]{:S(2)}, u32[]{:S(2)}) %all-to-all-start) | async-done | bytes 819232 | tf_op jit(solution)/shard_map/all_to_all | solution.py:531
  37.6 8.6 %collective-permute-start.1 = (bf16[4,2,400,128]{3,2,1,0:T(8,128)(2,1)S(1)}, bf16[4,2,400,128]{3,2,1,0:T(8,128)(2,1)S(1)}, u32[]{:S(2)}, u32[]{:S(2)}) collective-permute-start(bf16[4,2,400,128]{3,2,1,0:T(8,128)(2,1)S(1)} %all-to-all-done), channel_id=1, source_target_pairs={{0,1},{1,0},{2,3},{3,2},{4,5},{5,4},{6,7},{7,6},{8,9},{9,8},{10,11... | collective-permute-start | bytes 2457608 | tf_op jit(solution)/shard_map/ppermute | solution.py:75
  46.2 2.7 %shard_map.132.before = f32[9,80,128]{2,1,0:T(8,128)S(1)} custom-call(bf16[8,400,128]{2,1,0:T(8,128)(2,1)S(1)} %bitcast.15, f32[9,80,128]{2,1,0:T(8,128)S(1)} %shard_map.131.before), custom_call_target="tpu_custom_call" | custom-call | flops 68719476736 | bytes 1048576 | tf_op jit(solution)/shard_map/pallas_call | solution.py:83
  48.9 2.4 %collective-permute-start.3 = (f32[9,16,256]{2,1,0:T(8,128)S(1)}, f32[9,16,256]{2,1,0:T(8,128)S(1)}, u32[]{:S(2)}, u32[]{:S(2)}) collective-permute-start(f32[9,16,256]{2,1,0:T(8,128)S(1)} %get-tuple-element.28), channel_id=1, source_target_pairs={{0,1},{1,0},{2,3},{3,2},{4,5},{5,4},{6,7},{7,6},{8,9},{9,8},{10,11... | collective-permute-start | bytes 442376 | tf_op jit(solution)/shard_map/ppermute | solution.py:75
  51.3 2.1 %collective-permute-start.4 = (f32[4,16,256]{2,1,0:T(8,128)S(1)}, f32[4,16,256]{2,1,0:T(8,128)S(1)}, u32[]{:S(2)}, u32[]{:S(2)}) collective-permute-start(f32[4,16,256]{2,1,0:T(8,128)S(1)} %get-tuple-element.29), channel_id=1, source_target_pairs={{1,4},{4,1},{3,6},{6,3},{5,8},{8,5},{7,10},{10,7},{9,12},{12,9},{1... | collective-permute-start | bytes 196616 | tf_op jit(solution)/shard_map/ppermute | solution.py:561
  53.4 2.8 %shard_map.133.acc = f32[9,80,128]{2,1,0:T(8,128)S(1)} custom-call(bf16[8,400,128]{2,1,0:T(8,128)(2,1)S(1)} %bitcast.21, f32[9,80,128]{2,1,0:T(8,128)S(1)} %shard_map.132.before), custom_call_target="tpu_custom_call" | custom-call | flops 68719476736 | bytes 1048576 | tf_op jit(solution)/shard_map/pallas_call | solution.py:83
  57.2 2.4 %collective-permute-start.5 = (f32[12,16,256]{2,1,0:T(8,128)S(1)}, f32[12,16,256]{2,1,0:T(8,128)S(1)}, u32[]{:S(2)}, u32[]{:S(2)}) collective-permute-start(f32[12,16,256]{2,1,0:T(8,128)S(1)} %get-tuple-element.32), channel_id=1, source_target_pairs={{1,4},{4,1},{3,6},{6,3},{5,8},{8,5},{7,10},{10,7},{9,12},{12,9},{1... | collective-permute-start | bytes 589832 | tf_op jit(solution)/shard_map/ppermute | solution.py:575
  59.7 17.4 %all-gather = f32[18,16,256]{2,1,0:T(8,128)S(1)} all-gather(f32[9,16,256]{2,1,0:T(8,128)S(1)} %get-tuple-element.33), channel_id=2, replica_groups=mesh['blk'=32,'y'=4,'z'=2,'c'=2] {'c'}, dimensions={0}, use_global_device_ids=true | all-gather | bytes 442368 | tf_op jit(solution)/shard_map/all_gather | solution.py:576
  77.0 1.3 %shard_map.136 = (bf16[4,8,64,128]{3,2,1,0:T(8,128)(2,1)}, f32[4,2,16,256]{3,2,1,0:T(8,128)S(1)}, f32[4,2,16,256]{3,2,1,0:T(8,128)S(1)}) custom-call(f32[3,4,16,256]{3,2,1,0:T(8,128)S(1)} %get-tuple-element.30.u_in, f32[4,16,256]{2,1,0:T(8,128)S(1)} %get-tuple-element.31.por_in, f32[9,16,256]{2,1,0:T(8,128)S(1)} %copy-done, ...), custom_call_target="tpu_custom_call" | custom-call | bytes 1048576 | tf_op jit(solution)/shard_map/pallas_call | solution.py:83
  78.3 3.5 %all-to-all-start.1 = ((bf16[4,8,64,128]{3,2,1,0:T(8,128)(2,1)}), bf16[4,8,64,128]{3,2,1,0:T(8,128)(2,1)S(1)}, u32[]{:S(2)}, u32[]{:S(2)}) async-start(bf16[4,8,64,128]{3,2,1,0:T(8,128)(2,1)} %get-tuple-element.36), calls=%async_computation.1 | async-start | bytes 1048576 | tf_op jit(solution)/shard_map/all_to_all | solution.py:587
  81.8 4.3 %collective-permute-start.6 = (f32[4,2,16,256]{3,2,1,0:T(8,128)S(1)}, f32[4,2,16,256]{3,2,1,0:T(8,128)S(1)}, u32[]{:S(2)}, u32[]{:S(2)}) collective-permute-start(f32[4,2,16,256]{3,2,1,0:T(8,128)S(1)} %get-tuple-element.35), channel_id=1, source_target_pairs={{0,1},{1,0},{2,3},{3,2},{4,5},{5,4},{6,7},{7,6},{8,9},{9,8},{10,11... | collective-permute-start | bytes 393224 | tf_op jit(solution)/shard_map/ppermute | solution.py:75
  86.1 2.6 %all-to-all-done.1.near = bf16[4,8,64,128]{3,2,1,0:T(8,128)(2,1)S(1)} async-done(((bf16[4,8,64,128]{3,2,1,0:T(8,128)(2,1)}), bf16[4,8,64,128]{3,2,1,0:T(8,128)(2,1)S(1)}, u32[]{:S(2)}, u32[]{:S(2)}) %all-to-all-start.1) | async-done | bytes 524320 | tf_op jit(solution)/shard_map/all_to_all | solution.py:587
  88.7 5.4 %collective-permute-start.7 = (bf16[4,8,64,128]{3,2,1,0:T(8,128)(2,1)S(1)}, bf16[4,8,64,128]{3,2,1,0:T(8,128)(2,1)S(1)}, u32[]{:S(2)}, u32[]{:S(2)}) collective-permute-start(bf16[4,8,64,128]{3,2,1,0:T(8,128)(2,1)S(1)} %all-to-all-done.1.near), channel_id=1, source_target_pairs={{0,1},{1,0},{2,3},{3,2},{4,5},{5,4},{6,7},{7,6},{8,9},{9,8},{10,11... | collective-permute-start | bytes 1572872 | tf_op jit(solution)/shard_map/ppermute | solution.py:75
  95.7 1.9 %shard_map.138 = (f32[5,256]{1,0:T(8,128)S(1)}, f32[5,256]{1,0:T(8,128)S(1)}) custom-call(bf16[4,8,64,128]{3,2,1,0:T(8,128)(2,1)S(1)} %all-to-all-done.1.near, bf16[4,8,64,128]{3,2,1,0:T(8,128)(2,1)S(1)} %collective-permute-done.7.other, f32[9,16,256]{2,1,0:T(8,128)S(1)} %copy-done, f32[9,16,256]{2,1,0:T(8,128)S(1)} %collective-permute-done.2.far), custom_call_target="tpu_custom_call" | custom-call | flops 1073741824 | bytes 1048576 | tf_op jit(solution)/shard_map/pallas_call | solution.py:83
  97.5 1.9 %collective-permute-start.9 = (f32[5,256]{1,0:T(8,128)S(1)}, f32[5,256]{1,0:T(8,128)S(1)}, u32[]{:S(2)}, u32[]{:S(2)}) collective-permute-start(f32[5,256]{1,0:T(8,128)S(1)} %get-tuple-element.39), channel_id=1, source_target_pairs={{0,16},{1,17},{2,18},{3,19},{4,20},{5,21},{6,22},{7,23},{8,24},{9,... | collective-permute-start | bytes 15368 | tf_op jit(solution)/shard_map/ppermute | solution.py:598
  99.5 6.7 %collective-permute-start.8 = (f32[5,256]{1,0:T(8,128)S(1)}, f32[5,256]{1,0:T(8,128)S(1)}, u32[]{:S(2)}, u32[]{:S(2)}) collective-permute-start(f32[5,256]{1,0:T(8,128)S(1)} %get-tuple-element.38), channel_id=1, source_target_pairs={{2,496},{3,497},{0,498},{1,499},{6,500},{7,501},{4,502},{5,503},{1... | collective-permute-start | bytes 15368 | tf_op jit(solution)/shard_map/ppermute | solution.py:597
  106.2 3.0 %shard_map.137 = f32[3,8192]{1,0:T(4,128)} custom-call(bf16[4,8,64,128]{3,2,1,0:T(8,128)(2,1)S(1)} %all-to-all-done.1.near, bf16[4,8,64,128]{3,2,1,0:T(8,128)(2,1)S(1)} %collective-permute-done.7.other, s32[32]{0:T(128)S(1)} %copy-done.5, s32[64,128]{1,0:T(8,128)S(1)} %bitcast.19, f32[64,128]{1,0:T(8,128)S(1)} %copy-done.6, f32[3,8192]{1,0:T(4,128)S(1)} %copy-done.1, ...), custom_call_target="tpu_custom_call" | custom-call | flops 2147483648 | bytes 1048576 | tf_op jit(solution)/shard_map/pallas_call | solution.py:83
  (29 shorter events, 3.7 us)
Async XLA Ops:
  3.6 18.8 %collective-permute-start = (bf16[400,128]{1,0:T(8,128)(2,1)}, bf16[400,128]{1,0:T(8,128)(2,1)S(1)}, u32[]{:S(2)}, u32[]{:S(2)}) collective-permute-start(bf16[400,128]{1,0:T(8,128)(2,1)} %get-tuple-element.22.own), channel_id=1, source_target_pairs={{0,2},{2,0},{1,3},{3,1},{4,6},{6,4},{5,7},{7,5},{8,10},{10,8},{9,1... | collective-permute-start | bytes 307208 | tf_op jit(solution)/shard_map/ppermute | solution.py:75
  19.8 29.0 %collective-permute-start.2 = (f32[9,16,256]{2,1,0:T(8,128)}, f32[9,16,256]{2,1,0:T(8,128)S(1)}, u32[]{:S(2)}, u32[]{:S(2)}) collective-permute-start(f32[9,16,256]{2,1,0:T(8,128)} %get-tuple-element.24.own), channel_id=1, source_target_pairs={{0,2},{2,0},{1,3},{3,1},{4,6},{6,4},{5,7},{7,5},{8,10},{10,8},{9,1... | collective-permute-start | bytes 442376 | tf_op jit(solution)/shard_map/ppermute | solution.py:75
  22.4 0.9 copy-start.2
  24.3 13.3 %all-to-all-start = ((bf16[4,2,400,128]{3,2,1,0:T(8,128)(2,1)}), bf16[4,2,400,128]{3,2,1,0:T(8,128)(2,1)S(1)}, u32[]{:S(2)}, u32[]{:S(2)}) async-start(bf16[4,2,400,128]{3,2,1,0:T(8,128)(2,1)} %get-tuple-element.23), calls=%async_computation | async-start | bytes 1638400 | tf_op jit(solution)/shard_map/all_to_all | solution.py:531
  37.6 15.8 %collective-permute-start.1 = (bf16[4,2,400,128]{3,2,1,0:T(8,128)(2,1)S(1)}, bf16[4,2,400,128]{3,2,1,0:T(8,128)(2,1)S(1)}, u32[]{:S(2)}, u32[]{:S(2)}) collective-permute-start(bf16[4,2,400,128]{3,2,1,0:T(8,128)(2,1)S(1)} %all-to-all-done), channel_id=1, source_target_pairs={{0,1},{1,0},{2,3},{3,2},{4,5},{5,4},{6,7},{7,6},{8,9},{9,8},{10,11... | collective-permute-start | bytes 2457608 | tf_op jit(solution)/shard_map/ppermute | solution.py:75
  46.2 2.7 %copy-start = (f32[9,16,256]{2,1,0:T(8,128)S(1)}, f32[9,16,256]{2,1,0:T(8,128)}, u32[]{:S(2)}) copy-start(f32[9,16,256]{2,1,0:T(8,128)} %get-tuple-element.24.own) | copy-start | bytes 442372
  48.9 8.0 %collective-permute-start.3 = (f32[9,16,256]{2,1,0:T(8,128)S(1)}, f32[9,16,256]{2,1,0:T(8,128)S(1)}, u32[]{:S(2)}, u32[]{:S(2)}) collective-permute-start(f32[9,16,256]{2,1,0:T(8,128)S(1)} %get-tuple-element.28), channel_id=1, source_target_pairs={{0,1},{1,0},{2,3},{3,2},{4,5},{5,4},{6,7},{7,6},{8,9},{9,8},{10,11... | collective-permute-start | bytes 442376 | tf_op jit(solution)/shard_map/ppermute | solution.py:75
  51.3 5.6 %collective-permute-start.4 = (f32[4,16,256]{2,1,0:T(8,128)S(1)}, f32[4,16,256]{2,1,0:T(8,128)S(1)}, u32[]{:S(2)}, u32[]{:S(2)}) collective-permute-start(f32[4,16,256]{2,1,0:T(8,128)S(1)} %get-tuple-element.29), channel_id=1, source_target_pairs={{1,4},{4,1},{3,6},{6,3},{5,8},{8,5},{7,10},{10,7},{9,12},{12,9},{1... | collective-permute-start | bytes 196616 | tf_op jit(solution)/shard_map/ppermute | solution.py:561
  57.2 19.8 %collective-permute-start.5 = (f32[12,16,256]{2,1,0:T(8,128)S(1)}, f32[12,16,256]{2,1,0:T(8,128)S(1)}, u32[]{:S(2)}, u32[]{:S(2)}) collective-permute-start(f32[12,16,256]{2,1,0:T(8,128)S(1)} %get-tuple-element.32), channel_id=1, source_target_pairs={{1,4},{4,1},{3,6},{6,3},{5,8},{8,5},{7,10},{10,7},{9,12},{12,9},{1... | collective-permute-start | bytes 589832 | tf_op jit(solution)/shard_map/ppermute | solution.py:575
  78.3 10.4 %all-to-all-start.1 = ((bf16[4,8,64,128]{3,2,1,0:T(8,128)(2,1)}), bf16[4,8,64,128]{3,2,1,0:T(8,128)(2,1)S(1)}, u32[]{:S(2)}, u32[]{:S(2)}) async-start(bf16[4,8,64,128]{3,2,1,0:T(8,128)(2,1)} %get-tuple-element.36), calls=%async_computation.1 | async-start | bytes 1048576 | tf_op jit(solution)/shard_map/all_to_all | solution.py:587
  81.8 12.4 %collective-permute-start.6 = (f32[4,2,16,256]{3,2,1,0:T(8,128)S(1)}, f32[4,2,16,256]{3,2,1,0:T(8,128)S(1)}, u32[]{:S(2)}, u32[]{:S(2)}) collective-permute-start(f32[4,2,16,256]{3,2,1,0:T(8,128)S(1)} %get-tuple-element.35), channel_id=1, source_target_pairs={{0,1},{1,0},{2,3},{3,2},{4,5},{5,4},{6,7},{7,6},{8,9},{9,8},{10,11... | collective-permute-start | bytes 393224 | tf_op jit(solution)/shard_map/ppermute | solution.py:75
  88.7 7.0 %collective-permute-start.7 = (bf16[4,8,64,128]{3,2,1,0:T(8,128)(2,1)S(1)}, bf16[4,8,64,128]{3,2,1,0:T(8,128)(2,1)S(1)}, u32[]{:S(2)}, u32[]{:S(2)}) collective-permute-start(bf16[4,8,64,128]{3,2,1,0:T(8,128)(2,1)S(1)} %all-to-all-done.1.near), channel_id=1, source_target_pairs={{0,1},{1,0},{2,3},{3,2},{4,5},{5,4},{6,7},{7,6},{8,9},{9,8},{10,11... | collective-permute-start | bytes 1572872 | tf_op jit(solution)/shard_map/ppermute | solution.py:75
  95.5 10.7 %copy-start.1 = (f32[3,8192]{1,0:T(4,128)S(1)}, f32[3,8192]{1,0:T(4,128)}, u32[]{:S(2)}) copy-start(f32[3,8192]{1,0:T(4,128)} %vel_in.1) | copy-start | bytes 294916
  95.5 10.7 %copy-start.3 = (f32[8192]{0:T(1024)S(1)}, f32[8192]{0:T(1024)}, u32[]{:S(2)}) copy-start(f32[8192]{0:T(1024)} %param.14) | copy-start | bytes 98308
  95.5 10.7 %copy-start.4 = (s32[8192]{0:T(1024)S(1)}, s32[8192]{0:T(1024)}, u32[]{:S(2)}) copy-start(s32[8192]{0:T(1024)} %param.15) | copy-start | bytes 98308
  95.5 10.7 %copy-start.6 = (f32[64,128]{1,0:T(8,128)S(1)}, f32[64,128]{1,0:T(8,128)}, u32[]{:S(2)}) copy-start(f32[64,128]{1,0:T(8,128)} %get-tuple-element.37.keep) | copy-start | bytes 98308
  97.5 11.7 %collective-permute-start.9 = (f32[5,256]{1,0:T(8,128)S(1)}, f32[5,256]{1,0:T(8,128)S(1)}, u32[]{:S(2)}, u32[]{:S(2)}) collective-permute-start(f32[5,256]{1,0:T(8,128)S(1)} %get-tuple-element.39), channel_id=1, source_target_pairs={{0,16},{1,17},{2,18},{3,19},{4,20},{5,21},{6,22},{7,23},{8,24},{9,... | collective-permute-start | bytes 15368 | tf_op jit(solution)/shard_map/ppermute | solution.py:598
  99.5 6.7 %copy-start.5 = (s32[32]{0:T(128)S(1)}, s32[32]{0:T(128)}, u32[]{:S(2)}) copy-start(s32[32]{0:T(128)} %tiles_in.1) | copy-start | bytes 388
  99.5 9.8 %collective-permute-start.8 = (f32[5,256]{1,0:T(8,128)S(1)}, f32[5,256]{1,0:T(8,128)S(1)}, u32[]{:S(2)}, u32[]{:S(2)}) collective-permute-start(f32[5,256]{1,0:T(8,128)S(1)} %get-tuple-element.38), channel_id=1, source_target_pairs={{2,496},{3,497},{0,498},{1,499},{6,500},{7,501},{4,502},{5,503},{1... | collective-permute-start | bytes 15368 | tf_op jit(solution)/shard_map/ppermute | solution.py:597

commit v5 on v4

--- a/solution.py
+++ b/solution.py
@@ -410,27 +410,36 @@
     return [(vel[k] + pull * sampled[k]) / below for k in range(3)]
 
 
-def leave_kernel(near, other, own, far, out0, out1):
-    c = lax.axis_index("c")
+def leave_lists_of(own, far):
     z_lo = lax.rem(lax.axis_index("blk"), Z_LO)
     list0 = jnp.where(z_lo == 0, far[8, 0:8, :], own[8, 0:8, :])
     list1 = jnp.where(z_lo == Z_LO - 1, far[8, 8:16, :], own[8, 8:16, :])
-    both = jnp.concatenate([list0, list1], axis=1)
+    return jnp.concatenate([list0, list1], axis=1)
+
+
+def sample_lists(fields, core, both, total):
     place = both[5:6, :].astype(I32)
     block = place >> 11
-    hi = hi_of(place & (BLOCK - 1))
     low = (rows_iota(128, 2 * MIG) == (place & 127)).astype(F32).astype(BF16)
-    mask = rows_iota(16, 2 * MIG) == hi
 
     def gather(i, total):
         for u in range(OWN_BLOCKS):
-            for half, core in ((near, c), (other, 1 - c)):
-                picked = dot_nn(half[i, u], low)
-                wanted = i * 16 + core * OWN_BLOCKS + u
-                total = total + jnp.where(block == wanted, picked, 0.0)
+            picked = dot_nn(fields[i, u], low)
+            total = total + jnp.where(block == i * 16 + core * OWN_BLOCKS + u, picked, 0.0)
         return total
 
-    total = lax.fori_loop(0, N_Y, gather, jnp.zeros((64, 2 * MIG), F32))
+    return lax.fori_loop(0, N_Y, gather, total)
+
+
+def first_leave_kernel(near, own, far, out):
+    start = jnp.zeros((64, 2 * MIG), F32)
+    out[...] = sample_lists(near, lax.axis_index("c"), leave_lists_of(own, far), start)
+
+
+def last_leave_kernel(other, own, far, half, out0, out1):
+    both = leave_lists_of(own, far)
+    total = sample_lists(other, 1 - lax.axis_index("c"), both, half[...])
+    mask = rows_iota(16, 2 * MIG) == hi_of(both[5:6, :].astype(I32) & (BLOCK - 1))
     sampled = [
         jnp.sum(jnp.where(mask, total[16 * k : 16 * k + 16], 0.0), axis=0, keepdims=True)
         for k in range(4)
@@ -552,7 +561,6 @@
         flops=1 << 36,
     )
     pays_c = swap(pays, "c")
-    fpay_far, sums = lax.optimization_barrier((fpay_far, sums))
     edge, side = call(
         edge_kernel, [((4,) + plane, F32), ((9,) + plane, F32)], [fpay, fpay_far]
     )
@@ -588,11 +596,16 @@
     fields_c = swap(fields, "c")
     swapped = swap(sent, "c")
     mine = lax.axis_index("c") == lax.axis_index("z")
+    (half,) = call(
+        first_leave_kernel,
+        [((64, 2 * MIG), F32)],
+        [fields, fpay, fpay_far],
+        flops=1 << 36,
+    )
     out0, out1 = call(
-        leave_kernel,
+        last_leave_kernel,
         [((5, MIG), F32), ((5, MIG), F32)],
-        [fields, fields_c, fpay, fpay_far],
-        flops=1 << 30,
+        [fields_c, fpay, fpay_far, half],
     )
     arrive0 = lax.ppermute(out0, ALL, leave_route(-1))
     arrive1 = lax.ppermute(out1, ALL, leave_route(1))
@@ -610,6 +623,7 @@
         hbm=(2, 3, 5, 6),
         flops=1 << 31,
     )
+    kept, swapped, parcel_next = lax.optimization_barrier((kept, swapped, parcel_next))
     fluid_next = jnp.where(mine, kept[:3], swapped[:3])
     pressure_next = jnp.where(mine, kept[3], swapped[3])
     arrivals = jnp.stack([arrive0, arrive1], axis=1).transpose(1, 0, 2)

time: 110 us -> 105 us (0.955)
  blocking collectives: 17.4 us -> 3.55 us
  waiting for transfers between devices: 11.5 us -> 17.8 us
  starting transfers between devices: 59.9 us -> 61.5 us
    ppermute x6, waiting for transfers between devices: 0.84 us -> 16.1 us  [swap(): return lax.ppermute(values, axis, [(0, 1), (1, 0)])]
    all_gather x1, blocking collectives: 17.4 us -> 3.55 us  [per_device(): from_c = lax.all_gather(flux_c, 'c', axis=0)]
    all_to_all x1, waiting for transfers between devices: 7.49 us -> 0.01 us  [per_device(): pays = lax.all_to_all(pays, 'y', 0, 0)]
    ppermute x6, starting transfers between devices: 38.9 us -> 34.6 us  [swap(): return lax.ppermute(values, axis, [(0, 1), (1, 0)])]
    ppermute x1, starting transfers between devices: 2.14 us -> 4.87 us  [per_device(): edge = lax.ppermute(edge, ALL, route)]
    all_to_all x1, starting transfers between devices: 3.47 us -> 5.18 us  [per_device(): fields = lax.all_to_all(fields, 'y', 0, 0)]
    ppermute x1, starting transfers between devices: 2.42 us -> 3.8 us  [per_device(): from_y = lax.ppermute(flux_y, ALL, route)]
    pallas_call x10 -> x11, Pallas kernels: 16.7 us -> 17.4 us  [call(): pl.pallas_call(kernel, out_shape=[jax.ShapeDtypeStruct(shape, dtype) for...]
  transfers between devices with their start and end apart: 12 -> 12, of which waited for: 5 -> 4; matrix products, arithmetic and copies ran while one was open for 1% -> 1% of each run, Pallas kernels for 10% -> 13%
where the time goes in v5:
time: 105 us
  starting transfers between devices  61.5 us (59%)
  waiting for transfers between devices  17.8 us (17%)
  Pallas kernels  17.4 us (17%)
  blocking collectives  3.55 us (3%)
  between operations  1.55 us (1%)
  local copies, waits for them, and re-layouts  1.54 us (1%)
  other arithmetic  1.28 us (1%)
    ppermute x6, starting transfers between devices, swap(): return lax.ppermute(values, axis, [(0, 1), (1, 0)])  34.6 us
    pallas_call x11, Pallas kernels, call(): pl.pallas_call(kernel, out_shape=[jax.ShapeDtypeStruct(shape, dtype) for...  17.4 us
    ppermute x6, waiting for transfers between devices, swap(): return lax.ppermute(values, axis, [(0, 1), (1, 0)])  16.1 us
    ppermute x1, starting transfers between devices, per_device(): arrive0 = lax.ppermute(out0, ALL, leave_route(-1))  6.2 us
    all_to_all x1, starting transfers between devices, per_device(): fields = lax.all_to_all(fields, 'y', 0, 0)  5.18 us
    ppermute x1, starting transfers between devices, per_device(): edge = lax.ppermute(edge, ALL, route)  4.87 us
    all_to_all x1, starting transfers between devices, per_device(): pays = lax.all_to_all(pays, 'y', 0, 0)  4.44 us
    ppermute x1, starting transfers between devices, per_device(): from_y = lax.ppermute(flux_y, ALL, route)  3.8 us
  transfers between devices with their start and end apart: 12, of which 4 were waited for; matrix products, arithmetic and copies ran while one was open for 1% of the time, Pallas kernels for 13%

profile of v5, /device:TPU:1, one launch (start us, length us, event | category | flops | bytes accessed | tf_op | source)
XLA Modules:
  0.0 104.5 jit_solution(17696477029929153002)
XLA Ops:
  1.3 2.3 %shard_map.129 = (bf16[400,128]{1,0:T(8,128)(2,1)}, f32[9,16,256]{2,1,0:T(8,128)}, f32[64,128]{1,0:T(8,128)}) custom-call(f32[3,8192]{1,0:T(4,128)} %vel_in.1, f32[64,128]{1,0:T(8,128)} %bitcast.22, f32[64,128]{1,0:T(8,128)} %bitcast.16, s32[64,128]{1,0:T(8,128)} %bitcast.18, s32[1,32]{1,0:T(1,128)} %bitcast.20, s32[1]{0:T(128)S(6)} %copy.16.refs_5_, ...), custom_call_target="tpu_custom_call" | custom-call | bytes 1048576 | tf_op jit(solution)/shard_map/pallas_call | solution.py:83
  3.6 16.3 %collective-permute-start = (bf16[400,128]{1,0:T(8,128)(2,1)}, bf16[400,128]{1,0:T(8,128)(2,1)S(1)}, u32[]{:S(2)}, u32[]{:S(2)}) collective-permute-start(bf16[400,128]{1,0:T(8,128)(2,1)} %get-tuple-element.23.own), channel_id=1, source_target_pairs={{0,2},{2,0},{1,3},{3,1},{4,6},{6,4},{5,7},{7,5},{8,10},{10,8},{9,1... | collective-permute-start | bytes 307208 | tf_op jit(solution)/shard_map/ppermute | solution.py:75
  19.9 1.9 %collective-permute-start.2 = (f32[9,16,256]{2,1,0:T(8,128)}, f32[9,16,256]{2,1,0:T(8,128)S(1)}, u32[]{:S(2)}, u32[]{:S(2)}) collective-permute-start(f32[9,16,256]{2,1,0:T(8,128)} %get-tuple-element.26.own), channel_id=1, source_target_pairs={{0,2},{2,0},{1,3},{3,1},{4,6},{6,4},{5,7},{7,5},{8,10},{10,8},{9,1... | collective-permute-start | bytes 442376 | tf_op jit(solution)/shard_map/ppermute | solution.py:75
  23.3 1.0 shard_map.130
  24.3 4.4 %all-to-all-start = ((bf16[4,2,400,128]{3,2,1,0:T(8,128)(2,1)}), bf16[4,2,400,128]{3,2,1,0:T(8,128)(2,1)S(1)}, u32[]{:S(2)}, u32[]{:S(2)}) async-start(bf16[4,2,400,128]{3,2,1,0:T(8,128)(2,1)} %get-tuple-element.24), calls=%async_computation | async-start | bytes 1638400 | tf_op jit(solution)/shard_map/all_to_all | solution.py:540
  28.8 1.3 %shard_map.131.before = f32[9,80,128]{2,1,0:T(8,128)S(1)} custom-call(bf16[2,400,128]{2,1,0:T(8,128)(2,1)S(1)} %get-tuple-element.25.pays), custom_call_target="tpu_custom_call" | custom-call | flops 68719476736 | bytes 1048576 | tf_op jit(solution)/shard_map/pallas_call | solution.py:83
  30.1 15.3 %collective-permute-done.2.far = f32[9,16,256]{2,1,0:T(8,128)S(1)} collective-permute-done((f32[9,16,256]{2,1,0:T(8,128)}, f32[9,16,256]{2,1,0:T(8,128)S(1)}, u32[]{:S(2)}, u32[]{:S(2)}) %collective-permute-start.2) | collective-permute-done | bytes 147488 | tf_op jit(solution)/shard_map/ppermute | solution.py:75
  45.4 2.7 %collective-permute-start.3 = (f32[9,16,256]{2,1,0:T(8,128)S(1)}, f32[9,16,256]{2,1,0:T(8,128)S(1)}, u32[]{:S(2)}, u32[]{:S(2)}) collective-permute-start(f32[9,16,256]{2,1,0:T(8,128)S(1)} %get-tuple-element.27), channel_id=1, source_target_pairs={{0,1},{1,0},{2,3},{3,2},{4,5},{5,4},{6,7},{7,6},{8,9},{9,8},{10,11... | collective-permute-start | bytes 442376 | tf_op jit(solution)/shard_map/ppermute | solution.py:75
  48.2 4.9 %collective-permute-start.4 = (f32[4,16,256]{2,1,0:T(8,128)S(1)}, f32[4,16,256]{2,1,0:T(8,128)S(1)}, u32[]{:S(2)}, u32[]{:S(2)}) collective-permute-start(f32[4,16,256]{2,1,0:T(8,128)S(1)} %get-tuple-element.28), channel_id=1, source_target_pairs={{1,4},{4,1},{3,6},{6,3},{5,8},{8,5},{7,10},{10,7},{9,12},{12,9},{1... | collective-permute-start | bytes 196616 | tf_op jit(solution)/shard_map/ppermute | solution.py:569
  53.1 1.9 %collective-permute-start.1 = (bf16[4,2,400,128]{3,2,1,0:T(8,128)(2,1)S(1)}, bf16[4,2,400,128]{3,2,1,0:T(8,128)(2,1)S(1)}, u32[]{:S(2)}, u32[]{:S(2)}) collective-permute-start(bf16[4,2,400,128]{3,2,1,0:T(8,128)(2,1)S(1)} %all-to-all-done), channel_id=1, source_target_pairs={{0,1},{1,0},{2,3},{3,2},{4,5},{5,4},{6,7},{7,6},{8,9},{9,8},{10,11... | collective-permute-start | bytes 2457608 | tf_op jit(solution)/shard_map/ppermute | solution.py:75
  55.0 2.9 %shard_map.132.before = f32[9,80,128]{2,1,0:T(8,128)S(1)} custom-call(bf16[8,400,128]{2,1,0:T(8,128)(2,1)S(1)} %bitcast.15, f32[9,80,128]{2,1,0:T(8,128)S(1)} %shard_map.131.before), custom_call_target="tpu_custom_call" | custom-call | flops 68719476736 | bytes 1048576 | tf_op jit(solution)/shard_map/pallas_call | solution.py:83
  57.9 2.6 %shard_map.133.acc = f32[9,80,128]{2,1,0:T(8,128)S(1)} custom-call(bf16[8,400,128]{2,1,0:T(8,128)(2,1)S(1)} %bitcast.21, f32[9,80,128]{2,1,0:T(8,128)S(1)} %shard_map.132.before), custom_call_target="tpu_custom_call" | custom-call | flops 68719476736 | bytes 1048576 | tf_op jit(solution)/shard_map/pallas_call | solution.py:83
  60.9 3.8 %collective-permute-start.5 = (f32[12,16,256]{2,1,0:T(8,128)S(1)}, f32[12,16,256]{2,1,0:T(8,128)S(1)}, u32[]{:S(2)}, u32[]{:S(2)}) collective-permute-start(f32[12,16,256]{2,1,0:T(8,128)S(1)} %get-tuple-element.31), channel_id=1, source_target_pairs={{1,4},{4,1},{3,6},{6,3},{5,8},{8,5},{7,10},{10,7},{9,12},{12,9},{1... | collective-permute-start | bytes 589832 | tf_op jit(solution)/shard_map/ppermute | solution.py:583
  64.7 3.5 %all-gather = f32[18,16,256]{2,1,0:T(8,128)S(1)} all-gather(f32[9,16,256]{2,1,0:T(8,128)S(1)} %get-tuple-element.32), channel_id=2, replica_groups=mesh['blk'=32,'y'=4,'z'=2,'c'=2] {'c'}, dimensions={0}, use_global_device_ids=true | all-gather | bytes 442368 | tf_op jit(solution)/shard_map/all_gather | solution.py:584
  68.3 1.3 %shard_map.136 = (bf16[4,8,64,128]{3,2,1,0:T(8,128)(2,1)}, f32[4,2,16,256]{3,2,1,0:T(8,128)S(1)}, f32[4,2,16,256]{3,2,1,0:T(8,128)S(1)}) custom-call(f32[3,4,16,256]{3,2,1,0:T(8,128)S(1)} %get-tuple-element.29.u_in, f32[4,16,256]{2,1,0:T(8,128)S(1)} %get-tuple-element.30.por_in, f32[9,16,256]{2,1,0:T(8,128)S(1)} %copy-done, ...), custom_call_target="tpu_custom_call" | custom-call | bytes 1048576 | tf_op jit(solution)/shard_map/pallas_call | solution.py:83
  69.6 5.2 %all-to-all-start.1 = ((bf16[4,8,64,128]{3,2,1,0:T(8,128)(2,1)}), bf16[4,8,64,128]{3,2,1,0:T(8,128)(2,1)S(1)}, u32[]{:S(2)}, u32[]{:S(2)}) async-start(bf16[4,8,64,128]{3,2,1,0:T(8,128)(2,1)} %get-tuple-element.35), calls=%async_computation.1 | async-start | bytes 1048576 | tf_op jit(solution)/shard_map/all_to_all | solution.py:595
  74.7 5.3 %collective-permute-start.6 = (f32[4,2,16,256]{3,2,1,0:T(8,128)S(1)}, f32[4,2,16,256]{3,2,1,0:T(8,128)S(1)}, u32[]{:S(2)}, u32[]{:S(2)}) collective-permute-start(f32[4,2,16,256]{3,2,1,0:T(8,128)S(1)} %get-tuple-element.34), channel_id=1, source_target_pairs={{0,1},{1,0},{2,3},{3,2},{4,5},{5,4},{6,7},{7,6},{8,9},{9,8},{10,11... | collective-permute-start | bytes 393224 | tf_op jit(solution)/shard_map/ppermute | solution.py:75
  80.1 1.6 %all-to-all-done.1.near = bf16[4,8,64,128]{3,2,1,0:T(8,128)(2,1)S(1)} async-done(((bf16[4,8,64,128]{3,2,1,0:T(8,128)(2,1)}), bf16[4,8,64,128]{3,2,1,0:T(8,128)(2,1)S(1)}, u32[]{:S(2)}, u32[]{:S(2)}) %all-to-all-start.1) | async-done | bytes 524320 | tf_op jit(solution)/shard_map/all_to_all | solution.py:595
  81.7 6.4 %collective-permute-start.7 = (bf16[4,8,64,128]{3,2,1,0:T(8,128)(2,1)S(1)}, bf16[4,8,64,128]{3,2,1,0:T(8,128)(2,1)S(1)}, u32[]{:S(2)}, u32[]{:S(2)}) collective-permute-start(bf16[4,8,64,128]{3,2,1,0:T(8,128)(2,1)S(1)} %all-to-all-done.1.near), channel_id=1, source_target_pairs={{0,1},{1,0},{2,3},{3,2},{4,5},{5,4},{6,7},{7,6},{8,9},{9,8},{10,11... | collective-permute-start | bytes 1572872 | tf_op jit(solution)/shard_map/ppermute | solution.py:75
  88.1 1.3 %shard_map.138.half = f32[64,512]{1,0:T(8,128)S(1)} custom-call(bf16[4,8,64,128]{3,2,1,0:T(8,128)(2,1)S(1)} %all-to-all-done.1.near, f32[9,16,256]{2,1,0:T(8,128)S(1)} %copy-done, f32[9,16,256]{2,1,0:T(8,128)S(1)} %collective-permute-done.2.far), custom_call_target="tpu_custom_call" | custom-call | flops 68719476736 | bytes 1048576 | tf_op jit(solution)/shard_map/pallas_call | solution.py:83
  89.6 1.3 %shard_map.139 = (f32[5,256]{1,0:T(8,128)S(1)}, f32[5,256]{1,0:T(8,128)S(1)}) custom-call(bf16[4,8,64,128]{3,2,1,0:T(8,128)(2,1)S(1)} %collective-permute-done.7.other, f32[9,16,256]{2,1,0:T(8,128)S(1)} %copy-done, f32[9,16,256]{2,1,0:T(8,128)S(1)} %collective-permute-done.2.far, f32[64,512]{1,0:T(8,128)S(1)} %shard_map.138.half), custom_call_target="tpu_custom_call" | custom-call | bytes 1048576 | tf_op jit(solution)/shard_map/pallas_call | solution.py:83
  90.9 2.4 %collective-permute-start.9 = (f32[5,256]{1,0:T(8,128)S(1)}, f32[5,256]{1,0:T(8,128)S(1)}, u32[]{:S(2)}, u32[]{:S(2)}) collective-permute-start(f32[5,256]{1,0:T(8,128)S(1)} %get-tuple-element.41), channel_id=1, source_target_pairs={{0,16},{1,17},{2,18},{3,19},{4,20},{5,21},{6,22},{7,23},{8,24},{9,... | collective-permute-start | bytes 15368 | tf_op jit(solution)/shard_map/ppermute | solution.py:611
  93.3 6.2 %collective-permute-start.8 = (f32[5,256]{1,0:T(8,128)S(1)}, f32[5,256]{1,0:T(8,128)S(1)}, u32[]{:S(2)}, u32[]{:S(2)}) collective-permute-start(f32[5,256]{1,0:T(8,128)S(1)} %get-tuple-element.40), channel_id=1, source_target_pairs={{2,496},{3,497},{0,498},{1,499},{6,500},{7,501},{4,502},{5,503},{1... | collective-permute-start | bytes 15368 | tf_op jit(solution)/shard_map/ppermute | solution.py:610
  99.6 3.0 %shard_map.137 = f32[3,8192]{1,0:T(4,128)} custom-call(bf16[4,8,64,128]{3,2,1,0:T(8,128)(2,1)S(1)} %all-to-all-done.1.near, bf16[4,8,64,128]{3,2,1,0:T(8,128)(2,1)S(1)} %collective-permute-done.7.other, s32[32]{0:T(128)S(1)} %copy-done.5, s32[64,128]{1,0:T(8,128)S(1)} %bitcast.19, f32[64,128]{1,0:T(8,128)S(1)} %copy-done.6, f32[3,8192]{1,0:T(4,128)S(1)} %copy-done.1, ...), custom_call_target="tpu_custom_call" | custom-call | flops 2147483648 | bytes 1048576 | tf_op jit(solution)/shard_map/pallas_call | solution.py:83
  (30 shorter events, 4.0 us)
Async XLA Ops:
  3.6 18.8 %collective-permute-start = (bf16[400,128]{1,0:T(8,128)(2,1)}, bf16[400,128]{1,0:T(8,128)(2,1)S(1)}, u32[]{:S(2)}, u32[]{:S(2)}) collective-permute-start(bf16[400,128]{1,0:T(8,128)(2,1)} %get-tuple-element.23.own), channel_id=1, source_target_pairs={{0,2},{2,0},{1,3},{3,1},{4,6},{6,4},{5,7},{7,5},{8,10},{10,8},{9,1... | collective-permute-start | bytes 307208 | tf_op jit(solution)/shard_map/ppermute | solution.py:75
  19.9 25.6 %collective-permute-start.2 = (f32[9,16,256]{2,1,0:T(8,128)}, f32[9,16,256]{2,1,0:T(8,128)S(1)}, u32[]{:S(2)}, u32[]{:S(2)}) collective-permute-start(f32[9,16,256]{2,1,0:T(8,128)} %get-tuple-element.26.own), channel_id=1, source_target_pairs={{0,2},{2,0},{1,3},{3,1},{4,6},{6,4},{5,7},{7,5},{8,10},{10,8},{9,1... | collective-permute-start | bytes 442376 | tf_op jit(solution)/shard_map/ppermute | solution.py:75
  22.4 0.9 copy-start.2
  24.3 28.7 %all-to-all-start = ((bf16[4,2,400,128]{3,2,1,0:T(8,128)(2,1)}), bf16[4,2,400,128]{3,2,1,0:T(8,128)(2,1)S(1)}, u32[]{:S(2)}, u32[]{:S(2)}) async-start(bf16[4,2,400,128]{3,2,1,0:T(8,128)(2,1)} %get-tuple-element.24), calls=%async_computation | async-start | bytes 1638400 | tf_op jit(solution)/shard_map/all_to_all | solution.py:540
  28.8 16.6 %copy-start = (f32[9,16,256]{2,1,0:T(8,128)S(1)}, f32[9,16,256]{2,1,0:T(8,128)}, u32[]{:S(2)}) copy-start(f32[9,16,256]{2,1,0:T(8,128)} %get-tuple-element.26.own) | copy-start | bytes 442372
  45.4 15.1 %collective-permute-start.3 = (f32[9,16,256]{2,1,0:T(8,128)S(1)}, f32[9,16,256]{2,1,0:T(8,128)S(1)}, u32[]{:S(2)}, u32[]{:S(2)}) collective-permute-start(f32[9,16,256]{2,1,0:T(8,128)S(1)} %get-tuple-element.27), channel_id=1, source_target_pairs={{0,1},{1,0},{2,3},{3,2},{4,5},{5,4},{6,7},{7,6},{8,9},{9,8},{10,11... | collective-permute-start | bytes 442376 | tf_op jit(solution)/shard_map/ppermute | solution.py:75
  48.2 12.4 %collective-permute-start.4 = (f32[4,16,256]{2,1,0:T(8,128)S(1)}, f32[4,16,256]{2,1,0:T(8,128)S(1)}, u32[]{:S(2)}, u32[]{:S(2)}) collective-permute-start(f32[4,16,256]{2,1,0:T(8,128)S(1)} %get-tuple-element.28), channel_id=1, source_target_pairs={{1,4},{4,1},{3,6},{6,3},{5,8},{8,5},{7,10},{10,7},{9,12},{12,9},{1... | collective-permute-start | bytes 196616 | tf_op jit(solution)/shard_map/ppermute | solution.py:569
  53.1 4.8 %collective-permute-start.1 = (bf16[4,2,400,128]{3,2,1,0:T(8,128)(2,1)S(1)}, bf16[4,2,400,128]{3,2,1,0:T(8,128)(2,1)S(1)}, u32[]{:S(2)}, u32[]{:S(2)}) collective-permute-start(bf16[4,2,400,128]{3,2,1,0:T(8,128)(2,1)S(1)} %all-to-all-done), channel_id=1, source_target_pairs={{0,1},{1,0},{2,3},{3,2},{4,5},{5,4},{6,7},{7,6},{8,9},{9,8},{10,11... | collective-permute-start | bytes 2457608 | tf_op jit(solution)/shard_map/ppermute | solution.py:75
  60.9 7.4 %collective-permute-start.5 = (f32[12,16,256]{2,1,0:T(8,128)S(1)}, f32[12,16,256]{2,1,0:T(8,128)S(1)}, u32[]{:S(2)}, u32[]{:S(2)}) collective-permute-start(f32[12,16,256]{2,1,0:T(8,128)S(1)} %get-tuple-element.31), channel_id=1, source_target_pairs={{1,4},{4,1},{3,6},{6,3},{5,8},{8,5},{7,10},{10,7},{9,12},{12,9},{1... | collective-permute-start | bytes 589832 | tf_op jit(solution)/shard_map/ppermute | solution.py:583
  69.6 12.1 %all-to-all-start.1 = ((bf16[4,8,64,128]{3,2,1,0:T(8,128)(2,1)}), bf16[4,8,64,128]{3,2,1,0:T(8,128)(2,1)S(1)}, u32[]{:S(2)}, u32[]{:S(2)}) async-start(bf16[4,8,64,128]{3,2,1,0:T(8,128)(2,1)} %get-tuple-element.35), calls=%async_computation.1 | async-start | bytes 1048576 | tf_op jit(solution)/shard_map/all_to_all | solution.py:595
  74.7 27.9 %collective-permute-start.6 = (f32[4,2,16,256]{3,2,1,0:T(8,128)S(1)}, f32[4,2,16,256]{3,2,1,0:T(8,128)S(1)}, u32[]{:S(2)}, u32[]{:S(2)}) collective-permute-start(f32[4,2,16,256]{3,2,1,0:T(8,128)S(1)} %get-tuple-element.34), channel_id=1, source_target_pairs={{0,1},{1,0},{2,3},{3,2},{4,5},{5,4},{6,7},{7,6},{8,9},{9,8},{10,11... | collective-permute-start | bytes 393224 | tf_op jit(solution)/shard_map/ppermute | solution.py:75
  81.7 7.9 %collective-permute-start.7 = (bf16[4,8,64,128]{3,2,1,0:T(8,128)(2,1)S(1)}, bf16[4,8,64,128]{3,2,1,0:T(8,128)(2,1)S(1)}, u32[]{:S(2)}, u32[]{:S(2)}) collective-permute-start(bf16[4,8,64,128]{3,2,1,0:T(8,128)(2,1)S(1)} %all-to-all-done.1.near), channel_id=1, source_target_pairs={{0,1},{1,0},{2,3},{3,2},{4,5},{5,4},{6,7},{7,6},{8,9},{9,8},{10,11... | collective-permute-start | bytes 1572872 | tf_op jit(solution)/shard_map/ppermute | solution.py:75
  89.4 10.2 %copy-start.1 = (f32[3,8192]{1,0:T(4,128)S(1)}, f32[3,8192]{1,0:T(4,128)}, u32[]{:S(2)}) copy-start(f32[3,8192]{1,0:T(4,128)} %vel_in.1) | copy-start | bytes 294916
  89.4 10.2 %copy-start.3 = (f32[8192]{0:T(1024)S(1)}, f32[8192]{0:T(1024)}, u32[]{:S(2)}) copy-start(f32[8192]{0:T(1024)} %param.14) | copy-start | bytes 98308
  89.4 10.2 %copy-start.4 = (s32[8192]{0:T(1024)S(1)}, s32[8192]{0:T(1024)}, u32[]{:S(2)}) copy-start(s32[8192]{0:T(1024)} %param.15) | copy-start | bytes 98308
  89.4 10.2 %copy-start.6 = (f32[64,128]{1,0:T(8,128)S(1)}, f32[64,128]{1,0:T(8,128)}, u32[]{:S(2)}) copy-start(f32[64,128]{1,0:T(8,128)} %get-tuple-element.36.keep) | copy-start | bytes 98308
  90.9 13.0 %collective-permute-start.9 = (f32[5,256]{1,0:T(8,128)S(1)}, f32[5,256]{1,0:T(8,128)S(1)}, u32[]{:S(2)}, u32[]{:S(2)}) collective-permute-start(f32[5,256]{1,0:T(8,128)S(1)} %get-tuple-element.41), channel_id=1, source_target_pairs={{0,16},{1,17},{2,18},{3,19},{4,20},{5,21},{6,22},{7,23},{8,24},{9,... | collective-permute-start | bytes 15368 | tf_op jit(solution)/shard_map/ppermute | solution.py:611
  93.3 6.3 %copy-start.5 = (s32[32]{0:T(128)S(1)}, s32[32]{0:T(128)}, u32[]{:S(2)}) copy-start(s32[32]{0:T(128)} %tiles_in.1) | copy-start | bytes 388
  93.3 10.6 %collective-permute-start.8 = (f32[5,256]{1,0:T(8,128)S(1)}, f32[5,256]{1,0:T(8,128)S(1)}, u32[]{:S(2)}, u32[]{:S(2)}) collective-permute-start(f32[5,256]{1,0:T(8,128)S(1)} %get-tuple-element.40), channel_id=1, source_target_pairs={{2,496},{3,497},{0,498},{1,499},{6,500},{7,501},{4,502},{5,503},{1... | collective-permute-start | bytes 15368 | tf_op jit(solution)/shard_map/ppermute | solution.py:610

commit v6 on v5

--- a/solution.py
+++ b/solution.py
@@ -26,7 +26,7 @@
 SCR_ROWS = 7 * ROWS
 SOURCES = N_Y * N_Z
 OWN_BLOCKS = 8
-UNROLL = 4
+UNROLL = 8
 LIST_CAP = SOURCES * TILES + UNROLL
 
 PACK_LIMIT = 56 << 20
@@ -107,29 +107,31 @@
     return ((cell >> 7) & 1) * 8 + (cell >> 8)
 
 
-def pack_kernel(*refs):
-    sources, (pay, fpay, keep), (vel, vol, rate, cell, tiles, count, lists, mig, vsc, tsc, sems) = (
-        refs[:10],
-        refs[10:13],
-        refs[13:],
-    )
-    fluid, press = sources[8:]
-    targets = [vel, vol, rate, cell, tiles, count, lists, mig]
-    targets += [fpay.at[2 * k : 2 * k + 2] for k in range(3)] + [fpay.at[6:8]]
-    origins = list(sources[:8]) + [fluid.at[k] for k in range(3)] + [press]
-    copies = [
-        pltpu.make_async_copy(origin, target, sems.at[i])
-        for i, (origin, target) in enumerate(zip(origins, targets))
-    ]
+def load_all(pairs, sems):
+    copies = [pltpu.make_async_copy(a, b, sems.at[i]) for i, (a, b) in enumerate(pairs)]
     for copy in copies:
         copy.start()
     for copy in copies:
         copy.wait()
+
+
+def fold_rows(vel, vsc):
     for r in range(ROWS):
         for k in range(3):
             vsc[k, r : r + 1, :] = vel[k : k + 1, r * 128 : (r + 1) * 128]
+
+
+def active_slots(count):
     slot = rows_iota(ROWS, 128) * 128 + lax.broadcasted_iota(I32, (ROWS, 128), 1)
-    active = (slot < count[0]).astype(F32)
+    return (slot < count[0]).astype(F32)
+
+
+def pack_kernel(*refs):
+    sources, pay, held, (vsc, tsc, sems) = refs[:6], refs[6], refs[7:13], refs[13:]
+    vel, vol, rate, cell, tiles, count = held
+    load_all(list(zip(sources, held)), sems)
+    fold_rows(vel, vsc)
+    active = active_slots(count)
     drag = vol[...] * rate[...]
     pay[0:ROWS, :] = (vol[...] * active).astype(BF16)
     pay[ROWS : 2 * ROWS, :] = (drag * active).astype(BF16)
@@ -143,10 +145,22 @@
     pay[5 * ROWS : 6 * ROWS, :] = code.astype(BF16)
     lane = lax.broadcasted_iota(I32, (1, TILES), 1)
     tsc[...] = jnp.zeros((16, 128), F32)
+    tsc[0:1, 0:TILES] = jnp.where(lane * TP < count[0], tiles[...].astype(F32), 255.0)
+    pay[6 * ROWS : 6 * ROWS + 16, :] = tsc[...].astype(BF16)
+
+
+def leaver_kernel(*refs):
+    sources, (fpay, keep), held, (vsc, tsc, sems) = refs[:10], refs[10:12], refs[12:20], refs[20:]
+    vel, vol, rate, cell, tiles, count, lists, mig = held
+    fluid, press = sources[8:]
+    pairs = list(zip(sources[:8], held))
+    pairs += [(fluid.at[k], fpay.at[2 * k : 2 * k + 2]) for k in range(3)] + [(press, fpay.at[6:8])]
+    load_all(pairs, sems)
+    fold_rows(vel, vsc)
+    cells = cell[...]
+    tsc[...] = jnp.zeros((16, 128), F32)
     tsc[0:1, 0:TILES] = tiles[...].astype(F32)
     raw_tiles = tsc[...].astype(BF16)
-    tsc[0:1, 0:TILES] = jnp.where(lane * TP < count[0], tiles[...].astype(F32), 255.0)
-    pay[6 * ROWS : 6 * ROWS + 16, :] = tsc[...].astype(BF16)
     slots = jnp.concatenate([lists[0:1, :], lists[1:2, :]], axis=1)
     lane512 = lax.broadcasted_iota(I32, (1, 2 * MIG), 1)
     ends = jnp.where(lane512 < MIG, mig[:, 0:1], mig[:, 1:2] + MIG)
@@ -154,7 +168,7 @@
     low = (rows_iota(128, 2 * MIG) == (slots & 127)).astype(F32).astype(BF16)
     row_mask = rows_iota(ROWS, 2 * MIG) == (slots >> 7)
     counts = dot_nt(jnp.where(row_mask, valid, 0.0).astype(BF16), low)
-    keep[...] = active * jnp.where(counts > 0.5, 0.0, 1.0)
+    keep[...] = active_slots(count) * jnp.where(counts > 0.5, 0.0, 1.0)
 
     def picked(values, parts):
         total = None
@@ -453,13 +467,11 @@
         out1[k : k + 1, :] = values[:, MIG:]
 
 
-def move_kernel(near, other, tiles_in, cell_in, keep, vel_in, rate_in, out, tiles, cell, vel, rate, sems):
-    moves = ((tiles_in, tiles), (cell_in, cell), (vel_in, vel), (rate_in, rate))
-    copies = [pltpu.make_async_copy(a, b, sems.at[i]) for i, (a, b) in enumerate(moves)]
-    for copy in copies:
-        copy.start()
-    for copy in copies:
-        copy.wait()
+def move_kernel(
+    near, other, tiles_in, cell_in, keep, vel_in, rate_in, kept, swapped, out, fluid, press, *scratch
+):
+    tiles, cell, vel, rate, sems = scratch
+    load_all([(tiles_in, tiles), (cell_in, cell), (vel_in, vel), (rate_in, rate)], sems)
     c = lax.axis_index("c")
     iota16 = rows_iota(16, TP)
     iota128 = rows_iota(128, TP)
@@ -491,6 +503,10 @@
         return carry
 
     lax.fori_loop(0, TILES // 4, some, 0)
+    mine = lax.axis_index("z") == c
+    for k in range(3):
+        fluid[k] = jnp.where(mine, kept[k], swapped[k])
+    press[...] = jnp.where(mine, kept[3], swapped[3])
 
 
 def per_device(
@@ -510,23 +526,32 @@
     cell = cell_local.reshape(ROWS, 128)
     tiles = tile_block.reshape(1, TILES)
     plane = (RADIAL, LINE)
-    pay, fpay, keep = call(
+    parcels = [parcel_vel, vol, rate, cell, tiles, parcel_count]
+    held = [
+        pltpu.VMEM((3, PCAP), F32),
+        pltpu.VMEM((ROWS, 128), F32),
+        pltpu.VMEM((ROWS, 128), F32),
+        pltpu.VMEM((ROWS, 128), I32),
+        pltpu.VMEM((1, TILES), I32),
+        pltpu.SMEM((1,), I32),
+    ]
+    folded = [pltpu.VMEM((3, ROWS, 128), F32), pltpu.VMEM((16, 128), F32)]
+    (pay,) = call(
         pack_kernel,
-        [((PAY_ROWS, 128), BF16), ((9,) + plane, F32), ((ROWS, 128), F32)],
-        [parcel_vel, vol, rate, cell, tiles, parcel_count, leave_lists, mig_counts.reshape(1, 2), fluid_vel, pressure],
-        scratch=[
-            pltpu.VMEM((3, PCAP), F32),
-            pltpu.VMEM((ROWS, 128), F32),
-            pltpu.VMEM((ROWS, 128), F32),
-            pltpu.VMEM((ROWS, 128), I32),
-            pltpu.VMEM((1, TILES), I32),
-            pltpu.SMEM((1,), I32),
-            pltpu.VMEM((2, MIG), I32),
-            pltpu.VMEM((1, 2), I32),
-            pltpu.VMEM((3, ROWS, 128), F32),
-            pltpu.VMEM((16, 128), F32),
-            pltpu.SemaphoreType.DMA((12,)),
-        ],
+        [((PAY_ROWS, 128), BF16)],
+        parcels,
+        scratch=held + folded + [pltpu.SemaphoreType.DMA((6,))],
+        hbm=range(6),
+        limit=PACK_LIMIT,
+    )
+    fpay, keep = call(
+        leaver_kernel,
+        [((9,) + plane, F32), ((ROWS, 128), F32)],
+        parcels + [leave_lists, mig_counts.reshape(1, 2), fluid_vel, pressure],
+        scratch=held
+        + [pltpu.VMEM((2, MIG), I32), pltpu.VMEM((1, 2), I32)]
+        + folded
+        + [pltpu.SemaphoreType.DMA((12,))],
         hbm=range(10),
         limit=PACK_LIMIT,
     )
@@ -595,7 +620,6 @@
     fields = lax.all_to_all(fields, "y", 0, 0)
     fields_c = swap(fields, "c")
     swapped = swap(sent, "c")
-    mine = lax.axis_index("c") == lax.axis_index("z")
     (half,) = call(
         first_leave_kernel,
         [((64, 2 * MIG), F32)],
@@ -609,10 +633,10 @@
     )
     arrive0 = lax.ppermute(out0, ALL, leave_route(-1))
     arrive1 = lax.ppermute(out1, ALL, leave_route(1))
-    (parcel_next,) = call(
+    parcel_next, fluid_next, pressure_next = call(
         move_kernel,
-        [((3, PCAP), F32)],
-        [fields, fields_c, tile_block, cell, keep, parcel_vel, rate],
+        [((3, PCAP), F32), ((3, 2) + plane, F32), ((2,) + plane, F32)],
+        [fields, fields_c, tile_block, cell, keep, parcel_vel, rate, kept, swapped],
         scratch=[
             pltpu.SMEM((TILES,), I32),
             pltpu.VMEM((ROWS, 128), I32),
@@ -623,9 +647,6 @@
         hbm=(2, 3, 5, 6),
         flops=1 << 31,
     )
-    kept, swapped, parcel_next = lax.optimization_barrier((kept, swapped, parcel_next))
-    fluid_next = jnp.where(mine, kept[:3], swapped[:3])
-    pressure_next = jnp.where(mine, kept[3], swapped[3])
     arrivals = jnp.stack([arrive0, arrive1], axis=1).transpose(1, 0, 2)
     return fluid_next, pressure_next, parcel_next, arrivals
 

time: 105 us -> 102 us (0.971)
  starting transfers between devices: 61.5 us -> 56.1 us
  blocking collectives: 3.55 us -> 5.63 us
  other arithmetic: 1.28 us -> 0.01 us
  waiting for transfers between devices: 17.8 us -> 19 us
    ppermute x6, waiting for transfers between devices: 16.1 us -> 11.1 us  [swap(): return lax.ppermute(values, axis, [(0, 1), (1, 0)])]
    all_to_all x1, waiting for transfers between devices: 1.6 us -> 5.87 us  [per_device(): fields = lax.all_to_all(fields, 'y', 0, 0)]
    all_to_all x1, starting transfers between devices: 5.18 us -> 7.45 us  [per_device(): fields = lax.all_to_all(fields, 'y', 0, 0)]
    all_gather x1, blocking collectives: 3.55 us -> 5.63 us  [per_device(): from_c = lax.all_gather(flux_c, 'c', axis=0)]
    ppermute x1, waiting for transfers between devices: 0.01 us -> 2.04 us  [per_device(): arrive1 = lax.ppermute(out1, ALL, leave_route(1))]
    ppermute x1, starting transfers between devices: 3.8 us -> 1.92 us  [per_device(): from_y = lax.ppermute(flux_y, ALL, route)]
    ppermute x1, starting transfers between devices: 6.2 us -> 4.46 us  [per_device(): arrive0 = lax.ppermute(out0, ALL, leave_route(-1))]
    ppermute x1, starting transfers between devices: 4.87 us -> 3.22 us  [per_device(): edge = lax.ppermute(edge, ALL, route)]
  transfers between devices with their start and end apart: 12 -> 12, of which waited for: 4 -> 4; matrix products, arithmetic and copies ran while one was open for 1% -> 0% of each run, Pallas kernels for 13% -> 15%
where the time goes in v6:
time: 102 us
  starting transfers between devices  56.1 us (55%)
  waiting for transfers between devices  19 us (19%)
  Pallas kernels  18.3 us (18%)
  blocking collectives  5.63 us (6%)
  between operations  1.58 us (2%)
  local copies, waits for them, and re-layouts  1.25 us (1%)
    ppermute x6, starting transfers between devices, swap(): return lax.ppermute(values, axis, [(0, 1), (1, 0)])  33 us
    pallas_call x12, Pallas kernels, call(): pl.pallas_call(kernel, out_shape=[jax.ShapeDtypeStruct(shape, dtype) for...  18.3 us
    ppermute x6, waiting for transfers between devices, swap(): return lax.ppermute(values, axis, [(0, 1), (1, 0)])  11.1 us
    all_to_all x1, starting transfers between devices, per_device(): fields = lax.all_to_all(fields, 'y', 0, 0)  7.45 us
    all_to_all x1, waiting for transfers between devices, per_device(): fields = lax.all_to_all(fields, 'y', 0, 0)  5.87 us
    all_gather x1, blocking collectives, per_device(): from_c = lax.all_gather(flux_c, 'c', axis=0)  5.63 us
    ppermute x1, starting transfers between devices, per_device(): arrive0 = lax.ppermute(out0, ALL, leave_route(-1))  4.46 us
    all_to_all x1, starting transfers between devices, per_device(): pays = lax.all_to_all(pays, 'y', 0, 0)  4.18 us
  transfers between devices with their start and end apart: 12, of which 4 were waited for; matrix products, arithmetic and copies ran while one was open for 0% of the time, Pallas kernels for 15%

profile of v6, /device:TPU:1, one launch (start us, length us, event | category | flops | bytes accessed | tf_op | source)
XLA Modules:
  0.0 101.9 jit_solution(17875378786270445564)
XLA Ops:
  1.3 1.7 %shard_map.129.own = bf16[400,128]{1,0:T(8,128)(2,1)} custom-call(f32[3,8192]{1,0:T(4,128)} %vel_in.1, f32[64,128]{1,0:T(8,128)} %bitcast.23, f32[64,128]{1,0:T(8,128)} %bitcast.14, s32[64,128]{1,0:T(8,128)} %bitcast.17, s32[1,32]{1,0:T(1,128)} %bitcast.20, s32[1]{0:T(128)S(6)} %copy.16.refs_5_), custom_call_target="tpu_custom_call" | custom-call | bytes 1048576 | tf_op jit(solution)/shard_map/pallas_call | solution.py:83
  3.0 16.3 %collective-permute-start = (bf16[400,128]{1,0:T(8,128)(2,1)}, bf16[400,128]{1,0:T(8,128)(2,1)S(1)}, u32[]{:S(2)}, u32[]{:S(2)}) collective-permute-start(bf16[400,128]{1,0:T(8,128)(2,1)} %shard_map.129.own), channel_id=1, source_target_pairs={{0,2},{2,0},{1,3},{3,1},{4,6},{6,4},{5,7},{7,5},{8,10},{10,8},{9,1... | collective-permute-start | bytes 307208 | tf_op jit(solution)/shard_map/ppermute | solution.py:75
  19.3 2.3 %shard_map.134 = (f32[9,16,256]{2,1,0:T(8,128)}, f32[64,128]{1,0:T(8,128)}) custom-call(f32[3,8192]{1,0:T(4,128)} %vel_in.1, f32[64,128]{1,0:T(8,128)} %bitcast.24, f32[64,128]{1,0:T(8,128)} %bitcast.15, s32[64,128]{1,0:T(8,128)} %bitcast.18, s32[1,32]{1,0:T(1,128)} %bitcast.21, s32[1]{0:T(128)S(6)} %copy.16.refs_5_, s32[2,256]{1,0:T(2,128)} %refs_6_.1, ...), custom_call_target="tpu_custom_call" | custom-call | bytes 1048576 | tf_op jit(solution)/shard_map/pallas_call | solution.py:83
  21.7 1.9 %collective-permute-start.2 = (f32[9,16,256]{2,1,0:T(8,128)}, f32[9,16,256]{2,1,0:T(8,128)S(1)}, u32[]{:S(2)}, u32[]{:S(2)}) collective-permute-start(f32[9,16,256]{2,1,0:T(8,128)} %get-tuple-element.24.own), channel_id=1, source_target_pairs={{0,2},{2,0},{1,3},{3,1},{4,6},{6,4},{5,7},{7,5},{8,10},{10,8},{9,1... | collective-permute-start | bytes 442376 | tf_op jit(solution)/shard_map/ppermute | solution.py:75
  24.6 4.2 %all-to-all-start = ((bf16[4,2,400,128]{3,2,1,0:T(8,128)(2,1)}), bf16[4,2,400,128]{3,2,1,0:T(8,128)(2,1)S(1)}, u32[]{:S(2)}, u32[]{:S(2)}) async-start(bf16[4,2,400,128]{3,2,1,0:T(8,128)(2,1)} %get-tuple-element.22), calls=%async_computation | async-start | bytes 1638400 | tf_op jit(solution)/shard_map/all_to_all | solution.py:565
  30.0 10.8 %collective-permute-done.2.far = f32[9,16,256]{2,1,0:T(8,128)S(1)} collective-permute-done((f32[9,16,256]{2,1,0:T(8,128)}, f32[9,16,256]{2,1,0:T(8,128)S(1)}, u32[]{:S(2)}, u32[]{:S(2)}) %collective-permute-start.2) | collective-permute-done | bytes 147488 | tf_op jit(solution)/shard_map/ppermute | solution.py:75
  40.9 2.6 %collective-permute-start.3 = (f32[9,16,256]{2,1,0:T(8,128)S(1)}, f32[9,16,256]{2,1,0:T(8,128)S(1)}, u32[]{:S(2)}, u32[]{:S(2)}) collective-permute-start(f32[9,16,256]{2,1,0:T(8,128)S(1)} %get-tuple-element.25), channel_id=1, source_target_pairs={{0,1},{1,0},{2,3},{3,2},{4,5},{5,4},{6,7},{7,6},{8,9},{9,8},{10,11... | collective-permute-start | bytes 442376 | tf_op jit(solution)/shard_map/ppermute | solution.py:75
  43.5 3.2 %collective-permute-start.4 = (f32[4,16,256]{2,1,0:T(8,128)S(1)}, f32[4,16,256]{2,1,0:T(8,128)S(1)}, u32[]{:S(2)}, u32[]{:S(2)}) collective-permute-start(f32[4,16,256]{2,1,0:T(8,128)S(1)} %get-tuple-element.26), channel_id=1, source_target_pairs={{1,4},{4,1},{3,6},{6,3},{5,8},{8,5},{7,10},{10,7},{9,12},{12,9},{1... | collective-permute-start | bytes 196616 | tf_op jit(solution)/shard_map/ppermute | solution.py:594
  46.7 5.8 %collective-permute-start.1 = (bf16[4,2,400,128]{3,2,1,0:T(8,128)(2,1)S(1)}, bf16[4,2,400,128]{3,2,1,0:T(8,128)(2,1)S(1)}, u32[]{:S(2)}, u32[]{:S(2)}) collective-permute-start(bf16[4,2,400,128]{3,2,1,0:T(8,128)(2,1)S(1)} %all-to-all-done), channel_id=1, source_target_pairs={{0,1},{1,0},{2,3},{3,2},{4,5},{5,4},{6,7},{7,6},{8,9},{9,8},{10,11... | collective-permute-start | bytes 2457608 | tf_op jit(solution)/shard_map/ppermute | solution.py:75
  52.5 2.2 %shard_map.132.before = f32[9,80,128]{2,1,0:T(8,128)S(1)} custom-call(bf16[8,400,128]{2,1,0:T(8,128)(2,1)S(1)} %bitcast.13, f32[9,80,128]{2,1,0:T(8,128)S(1)} %shard_map.131.before), custom_call_target="tpu_custom_call" | custom-call | flops 68719476736 | bytes 1048576 | tf_op jit(solution)/shard_map/pallas_call | solution.py:83
  54.8 2.5 %shard_map.133.acc = f32[9,80,128]{2,1,0:T(8,128)S(1)} custom-call(bf16[8,400,128]{2,1,0:T(8,128)(2,1)S(1)} %bitcast.22, f32[9,80,128]{2,1,0:T(8,128)S(1)} %shard_map.132.before), custom_call_target="tpu_custom_call" | custom-call | flops 68719476736 | bytes 1048576 | tf_op jit(solution)/shard_map/pallas_call | solution.py:83
  57.6 1.9 %collective-permute-start.5 = (f32[12,16,256]{2,1,0:T(8,128)S(1)}, f32[12,16,256]{2,1,0:T(8,128)S(1)}, u32[]{:S(2)}, u32[]{:S(2)}) collective-permute-start(f32[12,16,256]{2,1,0:T(8,128)S(1)} %get-tuple-element.29), channel_id=1, source_target_pairs={{1,4},{4,1},{3,6},{6,3},{5,8},{8,5},{7,10},{10,7},{9,12},{12,9},{1... | collective-permute-start | bytes 589832 | tf_op jit(solution)/shard_map/ppermute | solution.py:608
  59.6 5.6 %all-gather = f32[18,16,256]{2,1,0:T(8,128)S(1)} all-gather(f32[9,16,256]{2,1,0:T(8,128)S(1)} %get-tuple-element.30), channel_id=2, replica_groups=mesh['blk'=32,'y'=4,'z'=2,'c'=2] {'c'}, dimensions={0}, use_global_device_ids=true | all-gather | bytes 442368 | tf_op jit(solution)/shard_map/all_gather | solution.py:609
  65.2 1.3 %shard_map.137 = (bf16[4,8,64,128]{3,2,1,0:T(8,128)(2,1)}, f32[4,2,16,256]{3,2,1,0:T(8,128)S(1)}, f32[4,2,16,256]{3,2,1,0:T(8,128)S(1)}) custom-call(f32[3,4,16,256]{3,2,1,0:T(8,128)S(1)} %get-tuple-element.27.u_in, f32[4,16,256]{2,1,0:T(8,128)S(1)} %get-tuple-element.28.por_in, f32[9,16,256]{2,1,0:T(8,128)S(1)} %copy-done, ...), custom_call_target="tpu_custom_call" | custom-call | bytes 1048576 | tf_op jit(solution)/shard_map/pallas_call | solution.py:83
  66.5 7.5 %all-to-all-start.1 = ((bf16[4,8,64,128]{3,2,1,0:T(8,128)(2,1)}), bf16[4,8,64,128]{3,2,1,0:T(8,128)(2,1)S(1)}, u32[]{:S(2)}, u32[]{:S(2)}) async-start(bf16[4,8,64,128]{3,2,1,0:T(8,128)(2,1)} %get-tuple-element.31), calls=%async_computation.1 | async-start | bytes 1048576 | tf_op jit(solution)/shard_map/all_to_all | solution.py:620
  74.0 2.8 %collective-permute-start.7 = (f32[4,2,16,256]{3,2,1,0:T(8,128)S(1)}, f32[4,2,16,256]{3,2,1,0:T(8,128)S(1)}, u32[]{:S(2)}, u32[]{:S(2)}) collective-permute-start(f32[4,2,16,256]{3,2,1,0:T(8,128)S(1)} %get-tuple-element.34), channel_id=1, source_target_pairs={{0,1},{1,0},{2,3},{3,2},{4,5},{5,4},{6,7},{7,6},{8,9},{9,8},{10,11... | collective-permute-start | bytes 393224 | tf_op jit(solution)/shard_map/ppermute | solution.py:75
  76.8 5.9 %all-to-all-done.1.near = bf16[4,8,64,128]{3,2,1,0:T(8,128)(2,1)S(1)} async-done(((bf16[4,8,64,128]{3,2,1,0:T(8,128)(2,1)}), bf16[4,8,64,128]{3,2,1,0:T(8,128)(2,1)S(1)}, u32[]{:S(2)}, u32[]{:S(2)}) %all-to-all-start.1) | async-done | bytes 524320 | tf_op jit(solution)/shard_map/all_to_all | solution.py:620
  82.6 3.7 %collective-permute-start.6 = (bf16[4,8,64,128]{3,2,1,0:T(8,128)(2,1)S(1)}, bf16[4,8,64,128]{3,2,1,0:T(8,128)(2,1)S(1)}, u32[]{:S(2)}, u32[]{:S(2)}) collective-permute-start(bf16[4,8,64,128]{3,2,1,0:T(8,128)(2,1)S(1)} %all-to-all-done.1.near), channel_id=1, source_target_pairs={{0,1},{1,0},{2,3},{3,2},{4,5},{5,4},{6,7},{7,6},{8,9},{9,8},{10,11... | collective-permute-start | bytes 1572872 | tf_op jit(solution)/shard_map/ppermute | solution.py:75
  86.3 1.3 %shard_map.139.half = f32[64,512]{1,0:T(8,128)S(1)} custom-call(bf16[4,8,64,128]{3,2,1,0:T(8,128)(2,1)S(1)} %all-to-all-done.1.near, f32[9,16,256]{2,1,0:T(8,128)S(1)} %copy-done, f32[9,16,256]{2,1,0:T(8,128)S(1)} %collective-permute-done.2.far), custom_call_target="tpu_custom_call" | custom-call | flops 68719476736 | bytes 1048576 | tf_op jit(solution)/shard_map/pallas_call | solution.py:83
  87.8 1.3 %shard_map.140 = (f32[5,256]{1,0:T(8,128)S(1)}, f32[5,256]{1,0:T(8,128)S(1)}) custom-call(bf16[4,8,64,128]{3,2,1,0:T(8,128)(2,1)S(1)} %collective-permute-done.6.other, f32[9,16,256]{2,1,0:T(8,128)S(1)} %copy-done, f32[9,16,256]{2,1,0:T(8,128)S(1)} %collective-permute-done.2.far, f32[64,512]{1,0:T(8,128)S(1)} %shard_map.139.half), custom_call_target="tpu_custom_call" | custom-call | bytes 1048576 | tf_op jit(solution)/shard_map/pallas_call | solution.py:83
  89.1 4.5 %collective-permute-start.8 = (f32[5,256]{1,0:T(8,128)S(1)}, f32[5,256]{1,0:T(8,128)S(1)}, u32[]{:S(2)}, u32[]{:S(2)}) collective-permute-start(f32[5,256]{1,0:T(8,128)S(1)} %get-tuple-element.38), channel_id=1, source_target_pairs={{2,496},{3,497},{0,498},{1,499},{6,500},{7,501},{4,502},{5,503},{1... | collective-permute-start | bytes 15368 | tf_op jit(solution)/shard_map/ppermute | solution.py:634
  93.6 1.9 %collective-permute-start.9 = (f32[5,256]{1,0:T(8,128)S(1)}, f32[5,256]{1,0:T(8,128)S(1)}, u32[]{:S(2)}, u32[]{:S(2)}) collective-permute-start(f32[5,256]{1,0:T(8,128)S(1)} %get-tuple-element.39), channel_id=1, source_target_pairs={{0,16},{1,17},{2,18},{3,19},{4,20},{5,21},{6,22},{7,23},{8,24},{9,... | collective-permute-start | bytes 15368 | tf_op jit(solution)/shard_map/ppermute | solution.py:635
  96.2 3.1 %shard_map.138 = (f32[3,8192]{1,0:T(4,128)}, f32[3,2,16,256]{3,2,1,0:T(8,128)}, f32[2,16,256]{2,1,0:T(8,128)}) custom-call(bf16[4,8,64,128]{3,2,1,0:T(8,128)(2,1)S(1)} %all-to-all-done.1.near, bf16[4,8,64,128]{3,2,1,0:T(8,128)(2,1)S(1)} %collective-permute-done.6.other, s32[32]{0:T(128)S(1)} %copy-done.5, s32[64,128]{1,0:T(8,128)S(1)} %bitcast.19, ...), custom_call_target="tpu_custom_call" | custom-call | flops 2147483648 | bytes 1048576 | tf_op jit(solution)/shard_map/pallas_call | solution.py:83
  99.3 2.0 %collective-permute-done.9 = f32[5,256]{1,0:T(8,128)S(1)} collective-permute-done((f32[5,256]{1,0:T(8,128)S(1)}, f32[5,256]{1,0:T(8,128)S(1)}, u32[]{:S(2)}, u32[]{:S(2)}) %collective-permute-start.9) | collective-permute-done | bytes 5152 | tf_op jit(solution)/shard_map/ppermute | solution.py:635
  (29 shorter events, 4.1 us)
Async XLA Ops:
  3.0 20.6 %collective-permute-start = (bf16[400,128]{1,0:T(8,128)(2,1)}, bf16[400,128]{1,0:T(8,128)(2,1)S(1)}, u32[]{:S(2)}, u32[]{:S(2)}) collective-permute-start(bf16[400,128]{1,0:T(8,128)(2,1)} %shard_map.129.own), channel_id=1, source_target_pairs={{0,2},{2,0},{1,3},{3,1},{4,6},{6,4},{5,7},{7,5},{8,10},{10,8},{9,1... | collective-permute-start | bytes 307208 | tf_op jit(solution)/shard_map/ppermute | solution.py:75
  19.3 4.3 %copy-start.2 = (bf16[400,128]{1,0:T(8,128)(2,1)S(1)}, bf16[400,128]{1,0:T(8,128)(2,1)}, u32[]{:S(2)}) copy-start(bf16[400,128]{1,0:T(8,128)(2,1)} %shard_map.129.own) | copy-start | bytes 307204
  21.7 19.2 %collective-permute-start.2 = (f32[9,16,256]{2,1,0:T(8,128)}, f32[9,16,256]{2,1,0:T(8,128)S(1)}, u32[]{:S(2)}, u32[]{:S(2)}) collective-permute-start(f32[9,16,256]{2,1,0:T(8,128)} %get-tuple-element.24.own), channel_id=1, source_target_pairs={{0,2},{2,0},{1,3},{3,1},{4,6},{6,4},{5,7},{7,5},{8,10},{10,8},{9,1... | collective-permute-start | bytes 442376 | tf_op jit(solution)/shard_map/ppermute | solution.py:75
  24.6 22.1 %all-to-all-start = ((bf16[4,2,400,128]{3,2,1,0:T(8,128)(2,1)}), bf16[4,2,400,128]{3,2,1,0:T(8,128)(2,1)S(1)}, u32[]{:S(2)}, u32[]{:S(2)}) async-start(bf16[4,2,400,128]{3,2,1,0:T(8,128)(2,1)} %get-tuple-element.22), calls=%async_computation | async-start | bytes 1638400 | tf_op jit(solution)/shard_map/all_to_all | solution.py:565
  28.8 12.0 %copy-start = (f32[9,16,256]{2,1,0:T(8,128)S(1)}, f32[9,16,256]{2,1,0:T(8,128)}, u32[]{:S(2)}) copy-start(f32[9,16,256]{2,1,0:T(8,128)} %get-tuple-element.24.own) | copy-start | bytes 442372
  40.9 16.4 %collective-permute-start.3 = (f32[9,16,256]{2,1,0:T(8,128)S(1)}, f32[9,16,256]{2,1,0:T(8,128)S(1)}, u32[]{:S(2)}, u32[]{:S(2)}) collective-permute-start(f32[9,16,256]{2,1,0:T(8,128)S(1)} %get-tuple-element.25), channel_id=1, source_target_pairs={{0,1},{1,0},{2,3},{3,2},{4,5},{5,4},{6,7},{7,6},{8,9},{9,8},{10,11... | collective-permute-start | bytes 442376 | tf_op jit(solution)/shard_map/ppermute | solution.py:75
  43.5 13.8 %collective-permute-start.4 = (f32[4,16,256]{2,1,0:T(8,128)S(1)}, f32[4,16,256]{2,1,0:T(8,128)S(1)}, u32[]{:S(2)}, u32[]{:S(2)}) collective-permute-start(f32[4,16,256]{2,1,0:T(8,128)S(1)} %get-tuple-element.26), channel_id=1, source_target_pairs={{1,4},{4,1},{3,6},{6,3},{5,8},{8,5},{7,10},{10,7},{9,12},{12,9},{1... | collective-permute-start | bytes 196616 | tf_op jit(solution)/shard_map/ppermute | solution.py:594
  46.7 8.0 %collective-permute-start.1 = (bf16[4,2,400,128]{3,2,1,0:T(8,128)(2,1)S(1)}, bf16[4,2,400,128]{3,2,1,0:T(8,128)(2,1)S(1)}, u32[]{:S(2)}, u32[]{:S(2)}) collective-permute-start(bf16[4,2,400,128]{3,2,1,0:T(8,128)(2,1)S(1)} %all-to-all-done), channel_id=1, source_target_pairs={{0,1},{1,0},{2,3},{3,2},{4,5},{5,4},{6,7},{7,6},{8,9},{9,8},{10,11... | collective-permute-start | bytes 2457608 | tf_op jit(solution)/shard_map/ppermute | solution.py:75
  57.6 7.6 %collective-permute-start.5 = (f32[12,16,256]{2,1,0:T(8,128)S(1)}, f32[12,16,256]{2,1,0:T(8,128)S(1)}, u32[]{:S(2)}, u32[]{:S(2)}) collective-permute-start(f32[12,16,256]{2,1,0:T(8,128)S(1)} %get-tuple-element.29), channel_id=1, source_target_pairs={{1,4},{4,1},{3,6},{6,3},{5,8},{8,5},{7,10},{10,7},{9,12},{12,9},{1... | collective-permute-start | bytes 589832 | tf_op jit(solution)/shard_map/ppermute | solution.py:608
  66.5 16.1 %all-to-all-start.1 = ((bf16[4,8,64,128]{3,2,1,0:T(8,128)(2,1)}), bf16[4,8,64,128]{3,2,1,0:T(8,128)(2,1)S(1)}, u32[]{:S(2)}, u32[]{:S(2)}) async-start(bf16[4,8,64,128]{3,2,1,0:T(8,128)(2,1)} %get-tuple-element.31), calls=%async_computation.1 | async-start | bytes 1048576 | tf_op jit(solution)/shard_map/all_to_all | solution.py:620
  74.0 21.6 %collective-permute-start.7 = (f32[4,2,16,256]{3,2,1,0:T(8,128)S(1)}, f32[4,2,16,256]{3,2,1,0:T(8,128)S(1)}, u32[]{:S(2)}, u32[]{:S(2)}) collective-permute-start(f32[4,2,16,256]{3,2,1,0:T(8,128)S(1)} %get-tuple-element.34), channel_id=1, source_target_pairs={{0,1},{1,0},{2,3},{3,2},{4,5},{5,4},{6,7},{7,6},{8,9},{9,8},{10,11... | collective-permute-start | bytes 393224 | tf_op jit(solution)/shard_map/ppermute | solution.py:75
  82.6 5.2 %collective-permute-start.6 = (bf16[4,8,64,128]{3,2,1,0:T(8,128)(2,1)S(1)}, bf16[4,8,64,128]{3,2,1,0:T(8,128)(2,1)S(1)}, u32[]{:S(2)}, u32[]{:S(2)}) collective-permute-start(bf16[4,8,64,128]{3,2,1,0:T(8,128)(2,1)S(1)} %all-to-all-done.1.near), channel_id=1, source_target_pairs={{0,1},{1,0},{2,3},{3,2},{4,5},{5,4},{6,7},{7,6},{8,9},{9,8},{10,11... | collective-permute-start | bytes 1572872 | tf_op jit(solution)/shard_map/ppermute | solution.py:75
  87.6 8.0 %copy-start.1 = (f32[3,8192]{1,0:T(4,128)S(1)}, f32[3,8192]{1,0:T(4,128)}, u32[]{:S(2)}) copy-start(f32[3,8192]{1,0:T(4,128)} %vel_in.1) | copy-start | bytes 294916
  87.6 8.0 %copy-start.3 = (f32[8192]{0:T(1024)S(1)}, f32[8192]{0:T(1024)}, u32[]{:S(2)}) copy-start(f32[8192]{0:T(1024)} %param.14) | copy-start | bytes 98308
  87.6 8.0 %copy-start.4 = (s32[8192]{0:T(1024)S(1)}, s32[8192]{0:T(1024)}, u32[]{:S(2)}) copy-start(s32[8192]{0:T(1024)} %param.15) | copy-start | bytes 98308
  87.6 8.0 %copy-start.6 = (f32[64,128]{1,0:T(8,128)S(1)}, f32[64,128]{1,0:T(8,128)}, u32[]{:S(2)}) copy-start(f32[64,128]{1,0:T(8,128)} %get-tuple-element.32.keep) | copy-start | bytes 98308
  89.1 10.1 %collective-permute-start.8 = (f32[5,256]{1,0:T(8,128)S(1)}, f32[5,256]{1,0:T(8,128)S(1)}, u32[]{:S(2)}, u32[]{:S(2)}) collective-permute-start(f32[5,256]{1,0:T(8,128)S(1)} %get-tuple-element.38), channel_id=1, source_target_pairs={{2,496},{3,497},{0,498},{1,499},{6,500},{7,501},{4,502},{5,503},{1... | collective-permute-start | bytes 15368 | tf_op jit(solution)/shard_map/ppermute | solution.py:634
  93.6 7.7 %collective-permute-start.9 = (f32[5,256]{1,0:T(8,128)S(1)}, f32[5,256]{1,0:T(8,128)S(1)}, u32[]{:S(2)}, u32[]{:S(2)}) collective-permute-start(f32[5,256]{1,0:T(8,128)S(1)} %get-tuple-element.39), channel_id=1, source_target_pairs={{0,16},{1,17},{2,18},{3,19},{4,20},{5,21},{6,22},{7,23},{8,24},{9,... | collective-permute-start | bytes 15368 | tf_op jit(solution)/shard_map/ppermute | solution.py:635
  95.5 0.7 copy-start.5

commit v7 on v6

--- a/solution.py
+++ b/solution.py
@@ -123,7 +123,7 @@
 
 def active_slots(count):
     slot = rows_iota(ROWS, 128) * 128 + lax.broadcasted_iota(I32, (ROWS, 128), 1)
-    return (slot < count[0]).astype(F32)
+    return (slot < count[...]).astype(F32)
 
 
 def pack_kernel(*refs):
@@ -145,12 +145,26 @@
     pay[5 * ROWS : 6 * ROWS, :] = code.astype(BF16)
     lane = lax.broadcasted_iota(I32, (1, TILES), 1)
     tsc[...] = jnp.zeros((16, 128), F32)
-    tsc[0:1, 0:TILES] = jnp.where(lane * TP < count[0], tiles[...].astype(F32), 255.0)
+    tsc[0:1, 0:TILES] = jnp.where(lane * TP < count[...], tiles[...].astype(F32), 255.0)
     pay[6 * ROWS : 6 * ROWS + 16, :] = tsc[...].astype(BF16)
 
 
+def place_rows():
+    return rows_iota(RADIAL, LINE) % 8 == 5
+
+
+def fixed_point(values, places=False):
+    scale = jnp.where(place_rows(), F32(1.0), F32(2.0**20)) if places else F32(2.0**20)
+    return jnp.floor(values * scale + 0.5).astype(I32)
+
+
+def from_fixed_point(code, places=False):
+    scale = jnp.where(place_rows(), F32(1.0), F32(2.0**-20)) if places else F32(2.0**-20)
+    return code.astype(F32) * scale
+
+
 def leaver_kernel(*refs):
-    sources, (fpay, keep), held, (vsc, tsc, sems) = refs[:10], refs[10:12], refs[12:20], refs[20:]
+    sources, (fpay, keep, coded), held, (vsc, tsc, sems) = refs[:10], refs[10:13], refs[13:21], refs[21:]
     vel, vol, rate, cell, tiles, count, lists, mig = held
     fluid, press = sources[8:]
     pairs = list(zip(sources[:8], held))
@@ -194,9 +208,21 @@
     put(5, block * BLOCK + cell_hi * 128.0 + cell_lo)
     put(6, valid)
     put(7, jnp.zeros_like(valid))
-
-
-def edge_kernel(own, far, edge, side):
+    codes = [fixed_point(fpay[p], places=p == 8) for p in range(9)]
+    for p in range(9):
+        coded[p] = (codes[p] >> 8).astype(jnp.int16)
+    for j in range(5):
+        shared = codes[2 * j] & 255
+        if j < 4:
+            shared = shared + (codes[2 * j + 1] & 255) * 256
+        coded[9 + j] = (shared - 32768).astype(jnp.int16)
+
+
+def edge_kernel(own, coded, edge, side, far):
+    for p in range(9):
+        shared = coded[9 + p // 2].astype(I32) + 32768
+        low = shared >> 8 if p % 2 else shared & 255
+        far[p] = from_fixed_point(coded[p].astype(I32) * 256 + low, places=p == 8)
     c = lax.axis_index("c")
     native = lax.axis_index("z") == c
     for k in range(4):
@@ -295,7 +321,10 @@
     lax.fori_loop(0, (found + UNROLL - 1) // UNROLL, deposit, 0)
 
 
-def first_deposit_kernel(pays, acc, *scratch):
+def first_deposit_kernel(pays, *refs):
+    given, (acc, *kept), scratch = refs[:5], refs[5:11], refs[11:]
+    for source, target in zip(given, kept):
+        target[...] = source[...]
     acc[...] = jnp.zeros_like(acc)
     add_deposits(pays, acc, *scratch)
 
@@ -468,10 +497,10 @@
 
 
 def move_kernel(
-    near, other, tiles_in, cell_in, keep, vel_in, rate_in, kept, swapped, out, fluid, press, *scratch
+    near, other, tiles_in, cell, keep, vel, rate, kept, swapped, out, fluid, press, *scratch
 ):
-    tiles, cell, vel, rate, sems = scratch
-    load_all([(tiles_in, tiles), (cell_in, cell), (vel_in, vel), (rate_in, rate)], sems)
+    tiles, sems = scratch
+    load_all([(tiles_in, tiles)], sems)
     c = lax.axis_index("c")
     iota16 = rows_iota(16, TP)
     iota128 = rows_iota(128, TP)
@@ -480,7 +509,7 @@
         return jnp.concatenate([ref[pl.ds(2 * t, 1), :], ref[pl.ds(2 * t + 1, 1), :]], axis=1)
 
     def one_tile(t):
-        block = tiles[t]
+        block = tiles[0, t]
         row, col = block >> 4, block & 7
         here = jnp.where((block >> 3) & 1 == c, near[row, col], other[row, col])
         cells = pair(cell, t)
@@ -526,14 +555,14 @@
     cell = cell_local.reshape(ROWS, 128)
     tiles = tile_block.reshape(1, TILES)
     plane = (RADIAL, LINE)
-    parcels = [parcel_vel, vol, rate, cell, tiles, parcel_count]
+    parcels = [parcel_vel, vol, rate, cell, tiles, parcel_count.reshape(1, 1)]
     held = [
         pltpu.VMEM((3, PCAP), F32),
         pltpu.VMEM((ROWS, 128), F32),
         pltpu.VMEM((ROWS, 128), F32),
         pltpu.VMEM((ROWS, 128), I32),
         pltpu.VMEM((1, TILES), I32),
-        pltpu.SMEM((1,), I32),
+        pltpu.VMEM((1, 1), I32),
     ]
     folded = [pltpu.VMEM((3, ROWS, 128), F32), pltpu.VMEM((16, 128), F32)]
     (pay,) = call(
@@ -544,9 +573,9 @@
         hbm=range(6),
         limit=PACK_LIMIT,
     )
-    fpay, keep = call(
+    fpay, keep, coded = call(
         leaver_kernel,
-        [((9,) + plane, F32), ((ROWS, 128), F32)],
+        [((9,) + plane, F32), ((ROWS, 128), F32), ((14,) + plane, jnp.int16)],
         parcels + [leave_lists, mig_counts.reshape(1, 2), fluid_vel, pressure],
         scratch=held
         + [pltpu.VMEM((2, MIG), I32), pltpu.VMEM((1, 2), I32)]
@@ -556,7 +585,7 @@
         limit=PACK_LIMIT,
     )
     pay_far = swap(pay, "z")
-    fpay_far = swap(fpay, "z")
+    coded_far = swap(coded, "z")
     pay_pair, pays = call(
         spread_kernel,
         [((N_Z, PAY_ROWS, 128), BF16), ((N_Y, N_Z, PAY_ROWS, 128), BF16)],
@@ -571,10 +600,17 @@
         pltpu.SemaphoreType.DMA,
     ]
     sums_shape = (OWN_BLOCKS + 1, 80, 128)
-    (sums,) = call(
+    sums, keep, vel_held, rate_held, cell_held, tiles_held = call(
         first_deposit_kernel,
-        [(sums_shape, F32)],
-        [pay_pair],
+        [
+            (sums_shape, F32),
+            ((ROWS, 128), F32),
+            ((3, PCAP), F32),
+            ((ROWS, 128), F32),
+            ((ROWS, 128), I32),
+            ((1, TILES), I32),
+        ],
+        [pay_pair, keep, parcel_vel, rate, cell, tiles],
         scratch=deposit_scratch,
         flops=1 << 36,
     )
@@ -586,8 +622,10 @@
         flops=1 << 36,
     )
     pays_c = swap(pays, "c")
-    edge, side = call(
-        edge_kernel, [((4,) + plane, F32), ((9,) + plane, F32)], [fpay, fpay_far]
+    edge, side, fpay_far = call(
+        edge_kernel,
+        [((4,) + plane, F32), ((9,) + plane, F32), ((9,) + plane, F32)],
+        [fpay, coded_far],
     )
     route = halo_route()
     side = swap(side, "c")
@@ -636,15 +674,8 @@
     parcel_next, fluid_next, pressure_next = call(
         move_kernel,
         [((3, PCAP), F32), ((3, 2) + plane, F32), ((2,) + plane, F32)],
-        [fields, fields_c, tile_block, cell, keep, parcel_vel, rate, kept, swapped],
-        scratch=[
-            pltpu.SMEM((TILES,), I32),
-            pltpu.VMEM((ROWS, 128), I32),
-            pltpu.VMEM((3, PCAP), F32),
-            pltpu.VMEM((ROWS, 128), F32),
-            pltpu.SemaphoreType.DMA((4,)),
-        ],
-        hbm=(2, 3, 5, 6),
+        [fields, fields_c, tiles_held, cell_held, keep, vel_held, rate_held, kept, swapped],
+        scratch=[pltpu.SMEM((1, TILES), I32), pltpu.SemaphoreType.DMA((1,))],
         flops=1 << 31,
     )
     arrivals = jnp.stack([arrive0, arrive1], axis=1).transpose(1, 0, 2)

time: 102 us -> 99.7 us (0.977)
  waiting for transfers between devices: 19 us -> 11.9 us
  starting transfers between devices: 56.1 us -> 59.5 us
  blocking collectives: 5.63 us -> 7.08 us
    all_to_all x1, waiting for transfers between devices: 5.87 us -> 2.33 us  [per_device(): fields = lax.all_to_all(fields, 'y', 0, 0)]
    ppermute x6, starting transfers between devices: 33 us -> 36.4 us  [swap(): return lax.ppermute(values, axis, [(0, 1), (1, 0)])]
    all_to_all x1, starting transfers between devices: 7.45 us -> 4.81 us  [per_device(): fields = lax.all_to_all(fields, 'y', 0, 0)]
    ppermute x1, waiting for transfers between devices: 2.04 us -> 0.01 us  [per_device(): arrive1 = lax.ppermute(out1, ALL, leave_route(1))]
    ppermute x1, starting transfers between devices: 4.46 us -> 6.2 us  [per_device(): arrive0 = lax.ppermute(out0, ALL, leave_route(-1))]
    ppermute x6, waiting for transfers between devices: 11.1 us -> 9.57 us  [swap(): return lax.ppermute(values, axis, [(0, 1), (1, 0)])]
    all_gather x1, blocking collectives: 5.63 us -> 7.08 us  [per_device(): from_c = lax.all_gather(flux_c, 'c', axis=0)]
  transfers between devices with their start and end apart: 12 -> 12, of which waited for: 4 -> 3; matrix products, arithmetic and copies ran while one was open for 0% -> 0% of each run, Pallas kernels for 15% -> 14%
where the time goes in v7:
time: 99.7 us; the launch traced here: 99.1 us
  starting transfers between devices  59.5 us (60%)
  Pallas kernels  17.7 us (18%)
  waiting for transfers between devices  11.9 us (12%)
  blocking collectives  7.08 us (7%)
  between operations  1.54 us (2%)
  local copies, waits for them, and re-layouts  1.25 us (1%)
    ppermute x6, starting transfers between devices, swap(): return lax.ppermute(values, axis, [(0, 1), (1, 0)])  36.4 us
    pallas_call x12, Pallas kernels, call(): pl.pallas_call(kernel, out_shape=[jax.ShapeDtypeStruct(shape, dtype) for...  17.7 us
    ppermute x6, waiting for transfers between devices, swap(): return lax.ppermute(values, axis, [(0, 1), (1, 0)])  9.57 us
    all_gather x1, blocking collectives, per_device(): from_c = lax.all_gather(flux_c, 'c', axis=0)  7.08 us
    ppermute x1, starting transfers between devices, per_device(): arrive0 = lax.ppermute(out0, ALL, leave_route(-1))  6.2 us
    all_to_all x1, starting transfers between devices, per_device(): fields = lax.all_to_all(fields, 'y', 0, 0)  4.81 us
    all_to_all x1, starting transfers between devices, per_device(): pays = lax.all_to_all(pays, 'y', 0, 0)  4.33 us
    ppermute x1, starting transfers between devices, per_device(): edge = lax.ppermute(edge, ALL, route)  3.32 us
  transfers between devices with their start and end apart: 12, of which 3 were waited for; matrix products, arithmetic and copies ran while one was open for 0% of the time, Pallas kernels for 14%

profile of v7, /device:TPU:1, one launch (start us, length us, event | category | flops | bytes accessed | tf_op | source)
XLA Modules:
  0.0 99.1 jit_solution(12855406618567962224)
XLA Ops:
  1.3 1.7 %shard_map.129.own = bf16[400,128]{1,0:T(8,128)(2,1)} custom-call(f32[3,8192]{1,0:T(4,128)} %refs_1_.1, f32[64,128]{1,0:T(8,128)} %bitcast.27, f32[64,128]{1,0:T(8,128)} %bitcast.17, s32[64,128]{1,0:T(8,128)} %bitcast.20, s32[1,32]{1,0:T(1,128)} %bitcast.23, s32[1,1]{1,0:T(1,128)} %bitcast.13.refs_5_), custom_call_target="tpu_custom_call" | custom-call | bytes 1048576 | tf_op jit(solution)/shard_map/pallas_call | solution.py:83
  3.0 16.3 %collective-permute-start = (bf16[400,128]{1,0:T(8,128)(2,1)}, bf16[400,128]{1,0:T(8,128)(2,1)S(1)}, u32[]{:S(2)}, u32[]{:S(2)}) collective-permute-start(bf16[400,128]{1,0:T(8,128)(2,1)} %shard_map.129.own), channel_id=1, source_target_pairs={{0,2},{2,0},{1,3},{3,1},{4,6},{6,4},{5,7},{7,5},{8,10},{10,8},{9,1... | collective-permute-start | bytes 307208 | tf_op jit(solution)/shard_map/ppermute | solution.py:75
  19.3 2.4 %shard_map.131 = (f32[9,16,256]{2,1,0:T(8,128)}, f32[64,128]{1,0:T(8,128)}, s16[14,16,256]{2,1,0:T(8,128)(2,1)}) custom-call(f32[3,8192]{1,0:T(4,128)} %refs_1_.1, f32[64,128]{1,0:T(8,128)} %bitcast.28, f32[64,128]{1,0:T(8,128)} %bitcast.18, s32[64,128]{1,0:T(8,128)} %bitcast.21, s32[1,32]{1,0:T(1,128)} %bitcast.24, s32[1,1]{1,0:T(1,128)} %bitcast.14.refs_5_, ...), custom_call_target="tpu_custom_call" | custom-call | bytes 1048576 | tf_op jit(solution)/shard_map/pallas_call | solution.py:83
  21.7 1.9 %collective-permute-start.2 = (s16[14,16,256]{2,1,0:T(8,128)(2,1)}, s16[14,16,256]{2,1,0:T(8,128)(2,1)S(1)}, u32[]{:S(2)}, u32[]{:S(2)}) collective-permute-start(s16[14,16,256]{2,1,0:T(8,128)(2,1)} %get-tuple-element.35), channel_id=1, source_target_pairs={{0,2},{2,0},{1,3},{3,1},{4,6},{6,4},{5,7},{7,5},{8,10},{10,8},{9,1... | collective-permute-start | bytes 344072 | tf_op jit(solution)/shard_map/ppermute | solution.py:75
  24.7 4.3 %all-to-all-start = ((bf16[4,2,400,128]{3,2,1,0:T(8,128)(2,1)}), bf16[4,2,400,128]{3,2,1,0:T(8,128)(2,1)S(1)}, u32[]{:S(2)}, u32[]{:S(2)}) async-start(bf16[4,2,400,128]{3,2,1,0:T(8,128)(2,1)} %get-tuple-element.30), calls=%async_computation | async-start | bytes 1638400 | tf_op jit(solution)/shard_map/all_to_all | solution.py:594
  29.7 1.2 %shard_map.132 = (f32[9,80,128]{2,1,0:T(8,128)S(1)}, f32[64,128]{1,0:T(8,128)S(1)}, f32[3,8192]{1,0:T(4,128)S(1)}, f32[64,128]{1,0:T(8,128)S(1)}, s32[64,128]{1,0:T(8,128)S(1)}, /*index=5*/s32[1,32]{1,0:T(1,128)S(1)}) custom-call(bf16[2,400,128]{2,1,0:T(8,128)(2,1)S(1)} %get-tuple-element.31.pays, f32[64,128]{1,0:T(8,128)S(1)} %copy-done.6, ...), custom_call_target="tpu_custom_call" | custom-call | flops 68719476736 | bytes 1048576 | tf_op jit(solution)/shard_map/pallas_call | solution.py:83
  30.9 9.3 %collective-permute-done.2.coded = s16[14,16,256]{2,1,0:T(8,128)(2,1)S(1)} collective-permute-done((s16[14,16,256]{2,1,0:T(8,128)(2,1)}, s16[14,16,256]{2,1,0:T(8,128)(2,1)S(1)}, u32[]{:S(2)}, u32[]{:S(2)}) %collective-permute-start.2) | collective-permute-done | bytes 114720 | tf_op jit(solution)/shard_map/ppermute | solution.py:75
  40.2 2.5 %collective-permute-start.3 = (f32[9,16,256]{2,1,0:T(8,128)S(1)}, f32[9,16,256]{2,1,0:T(8,128)S(1)}, u32[]{:S(2)}, u32[]{:S(2)}) collective-permute-start(f32[9,16,256]{2,1,0:T(8,128)S(1)} %get-tuple-element.37), channel_id=1, source_target_pairs={{0,1},{1,0},{2,3},{3,2},{4,5},{5,4},{6,7},{7,6},{8,9},{9,8},{10,11... | collective-permute-start | bytes 442376 | tf_op jit(solution)/shard_map/ppermute | solution.py:75
  42.8 3.3 %collective-permute-start.4 = (f32[4,16,256]{2,1,0:T(8,128)S(1)}, f32[4,16,256]{2,1,0:T(8,128)S(1)}, u32[]{:S(2)}, u32[]{:S(2)}) collective-permute-start(f32[4,16,256]{2,1,0:T(8,128)S(1)} %get-tuple-element.38), channel_id=1, source_target_pairs={{1,4},{4,1},{3,6},{6,3},{5,8},{8,5},{7,10},{10,7},{9,12},{12,9},{1... | collective-permute-start | bytes 196616 | tf_op jit(solution)/shard_map/ppermute | solution.py:632
  46.1 5.4 %collective-permute-start.1 = (bf16[4,2,400,128]{3,2,1,0:T(8,128)(2,1)S(1)}, bf16[4,2,400,128]{3,2,1,0:T(8,128)(2,1)S(1)}, u32[]{:S(2)}, u32[]{:S(2)}) collective-permute-start(bf16[4,2,400,128]{3,2,1,0:T(8,128)(2,1)S(1)} %all-to-all-done), channel_id=1, source_target_pairs={{0,1},{1,0},{2,3},{3,2},{4,5},{5,4},{6,7},{7,6},{8,9},{9,8},{10,11... | collective-permute-start | bytes 2457608 | tf_op jit(solution)/shard_map/ppermute | solution.py:75
  51.5 1.9 %shard_map.133.before = f32[9,80,128]{2,1,0:T(8,128)S(1)} custom-call(bf16[8,400,128]{2,1,0:T(8,128)(2,1)S(1)} %bitcast.16, f32[9,80,128]{2,1,0:T(8,128)S(1)} %get-tuple-element.33.before), custom_call_target="tpu_custom_call" | custom-call | flops 68719476736 | bytes 1048576 | tf_op jit(solution)/shard_map/pallas_call | solution.py:83
  53.5 2.2 %shard_map.134.acc = f32[9,80,128]{2,1,0:T(8,128)S(1)} custom-call(bf16[8,400,128]{2,1,0:T(8,128)(2,1)S(1)} %bitcast.26, f32[9,80,128]{2,1,0:T(8,128)S(1)} %shard_map.133.before), custom_call_target="tpu_custom_call" | custom-call | flops 68719476736 | bytes 1048576 | tf_op jit(solution)/shard_map/pallas_call | solution.py:83
  56.0 1.9 %collective-permute-start.5 = (f32[12,16,256]{2,1,0:T(8,128)S(1)}, f32[12,16,256]{2,1,0:T(8,128)S(1)}, u32[]{:S(2)}, u32[]{:S(2)}) collective-permute-start(f32[12,16,256]{2,1,0:T(8,128)S(1)} %get-tuple-element.41), channel_id=1, source_target_pairs={{1,4},{4,1},{3,6},{6,3},{5,8},{8,5},{7,10},{10,7},{9,12},{12,9},{1... | collective-permute-start | bytes 589832 | tf_op jit(solution)/shard_map/ppermute | solution.py:646
  58.0 7.1 %all-gather = f32[18,16,256]{2,1,0:T(8,128)S(1)} all-gather(f32[9,16,256]{2,1,0:T(8,128)S(1)} %get-tuple-element.42), channel_id=2, replica_groups=mesh['blk'=32,'y'=4,'z'=2,'c'=2] {'c'}, dimensions={0}, use_global_device_ids=true | all-gather | bytes 442368 | tf_op jit(solution)/shard_map/all_gather | solution.py:647
  65.1 1.3 %shard_map.137 = (bf16[4,8,64,128]{3,2,1,0:T(8,128)(2,1)}, f32[4,2,16,256]{3,2,1,0:T(8,128)S(1)}, f32[4,2,16,256]{3,2,1,0:T(8,128)S(1)}) custom-call(f32[3,4,16,256]{3,2,1,0:T(8,128)S(1)} %get-tuple-element.39.u_in, f32[4,16,256]{2,1,0:T(8,128)S(1)} %get-tuple-element.40.por_in, f32[9,16,256]{2,1,0:T(8,128)S(1)} %copy-done, ...), custom_call_target="tpu_custom_call" | custom-call | bytes 1048576 | tf_op jit(solution)/shard_map/pallas_call | solution.py:83
  66.4 4.8 %all-to-all-start.1 = ((bf16[4,8,64,128]{3,2,1,0:T(8,128)(2,1)}), bf16[4,8,64,128]{3,2,1,0:T(8,128)(2,1)S(1)}, u32[]{:S(2)}, u32[]{:S(2)}) async-start(bf16[4,8,64,128]{3,2,1,0:T(8,128)(2,1)} %get-tuple-element.43), calls=%async_computation.1 | async-start | bytes 1048576 | tf_op jit(solution)/shard_map/all_to_all | solution.py:658
  71.2 4.6 %collective-permute-start.7 = (f32[4,2,16,256]{3,2,1,0:T(8,128)S(1)}, f32[4,2,16,256]{3,2,1,0:T(8,128)S(1)}, u32[]{:S(2)}, u32[]{:S(2)}) collective-permute-start(f32[4,2,16,256]{3,2,1,0:T(8,128)S(1)} %get-tuple-element.50), channel_id=1, source_target_pairs={{0,1},{1,0},{2,3},{3,2},{4,5},{5,4},{6,7},{7,6},{8,9},{9,8},{10,11... | collective-permute-start | bytes 393224 | tf_op jit(solution)/shard_map/ppermute | solution.py:75
  75.8 2.3 %all-to-all-done.1.near = bf16[4,8,64,128]{3,2,1,0:T(8,128)(2,1)S(1)} async-done(((bf16[4,8,64,128]{3,2,1,0:T(8,128)(2,1)}), bf16[4,8,64,128]{3,2,1,0:T(8,128)(2,1)S(1)}, u32[]{:S(2)}, u32[]{:S(2)}) %all-to-all-start.1) | async-done | bytes 524320 | tf_op jit(solution)/shard_map/all_to_all | solution.py:658
  78.1 5.7 %collective-permute-start.6 = (bf16[4,8,64,128]{3,2,1,0:T(8,128)(2,1)S(1)}, bf16[4,8,64,128]{3,2,1,0:T(8,128)(2,1)S(1)}, u32[]{:S(2)}, u32[]{:S(2)}) collective-permute-start(bf16[4,8,64,128]{3,2,1,0:T(8,128)(2,1)S(1)} %all-to-all-done.1.near), channel_id=1, source_target_pairs={{0,1},{1,0},{2,3},{3,2},{4,5},{5,4},{6,7},{7,6},{8,9},{9,8},{10,11... | collective-permute-start | bytes 1572872 | tf_op jit(solution)/shard_map/ppermute | solution.py:75
  83.8 1.3 %shard_map.139.half = f32[64,512]{1,0:T(8,128)S(1)} custom-call(bf16[4,8,64,128]{3,2,1,0:T(8,128)(2,1)S(1)} %all-to-all-done.1.near, f32[9,16,256]{2,1,0:T(8,128)S(1)} %copy-done, f32[9,16,256]{2,1,0:T(8,128)S(1)} %get-tuple-element.36.far), custom_call_target="tpu_custom_call" | custom-call | flops 68719476736 | bytes 1048576 | tf_op jit(solution)/shard_map/pallas_call | solution.py:83
  85.3 1.3 %shard_map.140 = (f32[5,256]{1,0:T(8,128)S(1)}, f32[5,256]{1,0:T(8,128)S(1)}) custom-call(bf16[4,8,64,128]{3,2,1,0:T(8,128)(2,1)S(1)} %collective-permute-done.6.other, f32[9,16,256]{2,1,0:T(8,128)S(1)} %copy-done, f32[9,16,256]{2,1,0:T(8,128)S(1)} %get-tuple-element.36.far, f32[64,512]{1,0:T(8,128)S(1)} %shard_map.139.half), custom_call_target="tpu_custom_call" | custom-call | bytes 1048576 | tf_op jit(solution)/shard_map/pallas_call | solution.py:83
  86.6 2.5 %collective-permute-start.9 = (f32[5,256]{1,0:T(8,128)S(1)}, f32[5,256]{1,0:T(8,128)S(1)}, u32[]{:S(2)}, u32[]{:S(2)}) collective-permute-start(f32[5,256]{1,0:T(8,128)S(1)} %get-tuple-element.55), channel_id=1, source_target_pairs={{0,16},{1,17},{2,18},{3,19},{4,20},{5,21},{6,22},{7,23},{8,24},{9,... | collective-permute-start | bytes 15368 | tf_op jit(solution)/shard_map/ppermute | solution.py:673
  89.2 6.2 %collective-permute-start.8 = (f32[5,256]{1,0:T(8,128)S(1)}, f32[5,256]{1,0:T(8,128)S(1)}, u32[]{:S(2)}, u32[]{:S(2)}) collective-permute-start(f32[5,256]{1,0:T(8,128)S(1)} %get-tuple-element.54), channel_id=1, source_target_pairs={{2,496},{3,497},{0,498},{1,499},{6,500},{7,501},{4,502},{5,503},{1... | collective-permute-start | bytes 15368 | tf_op jit(solution)/shard_map/ppermute | solution.py:672
  95.4 3.0 %shard_map.138 = (f32[3,8192]{1,0:T(4,128)}, f32[3,2,16,256]{3,2,1,0:T(8,128)}, f32[2,16,256]{2,1,0:T(8,128)}) custom-call(bf16[4,8,64,128]{3,2,1,0:T(8,128)(2,1)S(1)} %all-to-all-done.1.near, bf16[4,8,64,128]{3,2,1,0:T(8,128)(2,1)S(1)} %collective-permute-done.6.other, s32[1,32]{1,0:T(1,128)S(1)} %get-tuple-element.44.tiles_in, ...), custom_call_target="tpu_custom_call" | custom-call | flops 2147483648 | bytes 1048576 | tf_op jit(solution)/shard_map/pallas_call | solution.py:83
  (29 shorter events, 3.0 us)
Async XLA Ops:
  3.0 20.6 %collective-permute-start = (bf16[400,128]{1,0:T(8,128)(2,1)}, bf16[400,128]{1,0:T(8,128)(2,1)S(1)}, u32[]{:S(2)}, u32[]{:S(2)}) collective-permute-start(bf16[400,128]{1,0:T(8,128)(2,1)} %shard_map.129.own), channel_id=1, source_target_pairs={{0,2},{2,0},{1,3},{3,1},{4,6},{6,4},{5,7},{7,5},{8,10},{10,8},{9,1... | collective-permute-start | bytes 307208 | tf_op jit(solution)/shard_map/ppermute | solution.py:75
  19.3 4.3 %copy-start.2 = (bf16[400,128]{1,0:T(8,128)(2,1)S(1)}, bf16[400,128]{1,0:T(8,128)(2,1)}, u32[]{:S(2)}) copy-start(bf16[400,128]{1,0:T(8,128)(2,1)} %shard_map.129.own) | copy-start | bytes 307204
  21.7 18.5 %collective-permute-start.2 = (s16[14,16,256]{2,1,0:T(8,128)(2,1)}, s16[14,16,256]{2,1,0:T(8,128)(2,1)S(1)}, u32[]{:S(2)}, u32[]{:S(2)}) collective-permute-start(s16[14,16,256]{2,1,0:T(8,128)(2,1)} %get-tuple-element.35), channel_id=1, source_target_pairs={{0,2},{2,0},{1,3},{3,1},{4,6},{6,4},{5,7},{7,5},{8,10},{10,8},{9,1... | collective-permute-start | bytes 344072 | tf_op jit(solution)/shard_map/ppermute | solution.py:75
  24.7 4.3 %copy-start.1 = (f32[3,8192]{1,0:T(4,128)S(1)}, f32[3,8192]{1,0:T(4,128)}, u32[]{:S(2)}) copy-start(f32[3,8192]{1,0:T(4,128)} %refs_1_.1) | copy-start | bytes 294916
  24.7 4.3 %copy-start.3 = (f32[8192]{0:T(1024)S(1)}, f32[8192]{0:T(1024)}, u32[]{:S(2)}) copy-start(f32[8192]{0:T(1024)} %param.14) | copy-start | bytes 98308
  24.7 4.3 %copy-start.4 = (s32[8192]{0:T(1024)S(1)}, s32[8192]{0:T(1024)}, u32[]{:S(2)}) copy-start(s32[8192]{0:T(1024)} %param.15) | copy-start | bytes 98308
  24.7 4.4 %copy-start.6 = (f32[64,128]{1,0:T(8,128)S(1)}, f32[64,128]{1,0:T(8,128)}, u32[]{:S(2)}) copy-start(f32[64,128]{1,0:T(8,128)} %get-tuple-element.32.refs_0_) | copy-start | bytes 98308
  24.7 21.4 %all-to-all-start = ((bf16[4,2,400,128]{3,2,1,0:T(8,128)(2,1)}), bf16[4,2,400,128]{3,2,1,0:T(8,128)(2,1)S(1)}, u32[]{:S(2)}, u32[]{:S(2)}) async-start(bf16[4,2,400,128]{3,2,1,0:T(8,128)(2,1)} %get-tuple-element.30), calls=%async_computation | async-start | bytes 1638400 | tf_op jit(solution)/shard_map/all_to_all | solution.py:594
  29.0 0.7 copy-start.5
  29.7 10.5 %copy-start = (f32[9,16,256]{2,1,0:T(8,128)S(1)}, f32[9,16,256]{2,1,0:T(8,128)}, u32[]{:S(2)}) copy-start(f32[9,16,256]{2,1,0:T(8,128)} %get-tuple-element.34.own) | copy-start | bytes 442372
  40.2 15.4 %collective-permute-start.3 = (f32[9,16,256]{2,1,0:T(8,128)S(1)}, f32[9,16,256]{2,1,0:T(8,128)S(1)}, u32[]{:S(2)}, u32[]{:S(2)}) collective-permute-start(f32[9,16,256]{2,1,0:T(8,128)S(1)} %get-tuple-element.37), channel_id=1, source_target_pairs={{0,1},{1,0},{2,3},{3,2},{4,5},{5,4},{6,7},{7,6},{8,9},{9,8},{10,11... | collective-permute-start | bytes 442376 | tf_op jit(solution)/shard_map/ppermute | solution.py:75
  42.8 12.9 %collective-permute-start.4 = (f32[4,16,256]{2,1,0:T(8,128)S(1)}, f32[4,16,256]{2,1,0:T(8,128)S(1)}, u32[]{:S(2)}, u32[]{:S(2)}) collective-permute-start(f32[4,16,256]{2,1,0:T(8,128)S(1)} %get-tuple-element.38), channel_id=1, source_target_pairs={{1,4},{4,1},{3,6},{6,3},{5,8},{8,5},{7,10},{10,7},{9,12},{12,9},{1... | collective-permute-start | bytes 196616 | tf_op jit(solution)/shard_map/ppermute | solution.py:632
  46.1 7.4 %collective-permute-start.1 = (bf16[4,2,400,128]{3,2,1,0:T(8,128)(2,1)S(1)}, bf16[4,2,400,128]{3,2,1,0:T(8,128)(2,1)S(1)}, u32[]{:S(2)}, u32[]{:S(2)}) collective-permute-start(bf16[4,2,400,128]{3,2,1,0:T(8,128)(2,1)S(1)} %all-to-all-done), channel_id=1, source_target_pairs={{0,1},{1,0},{2,3},{3,2},{4,5},{5,4},{6,7},{7,6},{8,9},{9,8},{10,11... | collective-permute-start | bytes 2457608 | tf_op jit(solution)/shard_map/ppermute | solution.py:75
  56.0 9.0 %collective-permute-start.5 = (f32[12,16,256]{2,1,0:T(8,128)S(1)}, f32[12,16,256]{2,1,0:T(8,128)S(1)}, u32[]{:S(2)}, u32[]{:S(2)}) collective-permute-start(f32[12,16,256]{2,1,0:T(8,128)S(1)} %get-tuple-element.41), channel_id=1, source_target_pairs={{1,4},{4,1},{3,6},{6,3},{5,8},{8,5},{7,10},{10,7},{9,12},{12,9},{1... | collective-permute-start | bytes 589832 | tf_op jit(solution)/shard_map/ppermute | solution.py:646
  66.4 11.7 %all-to-all-start.1 = ((bf16[4,8,64,128]{3,2,1,0:T(8,128)(2,1)}), bf16[4,8,64,128]{3,2,1,0:T(8,128)(2,1)S(1)}, u32[]{:S(2)}, u32[]{:S(2)}) async-start(bf16[4,8,64,128]{3,2,1,0:T(8,128)(2,1)} %get-tuple-element.43), calls=%async_computation.1 | async-start | bytes 1048576 | tf_op jit(solution)/shard_map/all_to_all | solution.py:658
  71.2 24.2 %collective-permute-start.7 = (f32[4,2,16,256]{3,2,1,0:T(8,128)S(1)}, f32[4,2,16,256]{3,2,1,0:T(8,128)S(1)}, u32[]{:S(2)}, u32[]{:S(2)}) collective-permute-start(f32[4,2,16,256]{3,2,1,0:T(8,128)S(1)} %get-tuple-element.50), channel_id=1, source_target_pairs={{0,1},{1,0},{2,3},{3,2},{4,5},{5,4},{6,7},{7,6},{8,9},{9,8},{10,11... | collective-permute-start | bytes 393224 | tf_op jit(solution)/shard_map/ppermute | solution.py:75
  78.1 7.2 %collective-permute-start.6 = (bf16[4,8,64,128]{3,2,1,0:T(8,128)(2,1)S(1)}, bf16[4,8,64,128]{3,2,1,0:T(8,128)(2,1)S(1)}, u32[]{:S(2)}, u32[]{:S(2)}) collective-permute-start(bf16[4,8,64,128]{3,2,1,0:T(8,128)(2,1)S(1)} %all-to-all-done.1.near), channel_id=1, source_target_pairs={{0,1},{1,0},{2,3},{3,2},{4,5},{5,4},{6,7},{7,6},{8,9},{9,8},{10,11... | collective-permute-start | bytes 1572872 | tf_op jit(solution)/shard_map/ppermute | solution.py:75
  86.6 11.8 %collective-permute-start.9 = (f32[5,256]{1,0:T(8,128)S(1)}, f32[5,256]{1,0:T(8,128)S(1)}, u32[]{:S(2)}, u32[]{:S(2)}) collective-permute-start(f32[5,256]{1,0:T(8,128)S(1)} %get-tuple-element.55), channel_id=1, source_target_pairs={{0,16},{1,17},{2,18},{3,19},{4,20},{5,21},{6,22},{7,23},{8,24},{9,... | collective-permute-start | bytes 15368 | tf_op jit(solution)/shard_map/ppermute | solution.py:673
  89.2 9.3 %collective-permute-start.8 = (f32[5,256]{1,0:T(8,128)S(1)}, f32[5,256]{1,0:T(8,128)S(1)}, u32[]{:S(2)}, u32[]{:S(2)}) collective-permute-start(f32[5,256]{1,0:T(8,128)S(1)} %get-tuple-element.54), channel_id=1, source_target_pairs={{2,496},{3,497},{0,498},{1,499},{6,500},{7,501},{4,502},{5,503},{1... | collective-permute-start | bytes 15368 | tf_op jit(solution)/shard_map/ppermute | solution.py:672

commit v8 on v7

--- a/solution.py
+++ b/solution.py
@@ -321,8 +321,10 @@
     lax.fori_loop(0, (found + UNROLL - 1) // UNROLL, deposit, 0)
 
 
-def first_deposit_kernel(pays, *refs):
-    given, (acc, *kept), scratch = refs[:5], refs[5:11], refs[11:]
+def first_deposit_kernel(own, away, *refs):
+    given, (acc, *kept), (pays, *scratch) = refs[:5], refs[5:11], refs[11:]
+    pays[0] = own[...]
+    pays[1] = away[...]
     for source, target in zip(given, kept):
         target[...] = source[...]
     acc[...] = jnp.zeros_like(acc)
@@ -334,9 +336,7 @@
     add_deposits(pays, acc, *scratch, skip_own=skip_own)
 
 
-def spread_kernel(own, far, both, out):
-    both[0] = own[...]
-    both[1] = far[...]
+def spread_kernel(own, far, out):
     for y in range(N_Y):
         out[y, 0] = own[...]
         out[y, 1] = far[...]
@@ -536,6 +536,12 @@
     for k in range(3):
         fluid[k] = jnp.where(mine, kept[k], swapped[k])
     press[...] = jnp.where(mine, kept[3], swapped[3])
+
+
+def join_kernel(first, second, out):
+    for k in range(5):
+        out[k, 0:1, :] = first[k : k + 1, :]
+        out[k, 1:2, :] = second[k : k + 1, :]
 
 
 def per_device(
@@ -586,9 +592,9 @@
     )
     pay_far = swap(pay, "z")
     coded_far = swap(coded, "z")
-    pay_pair, pays = call(
+    (pays,) = call(
         spread_kernel,
-        [((N_Z, PAY_ROWS, 128), BF16), ((N_Y, N_Z, PAY_ROWS, 128), BF16)],
+        [((N_Y, N_Z, PAY_ROWS, 128), BF16)],
         [pay, pay_far],
     )
     pays = lax.all_to_all(pays, "y", 0, 0)
@@ -610,8 +616,8 @@
             ((ROWS, 128), I32),
             ((1, TILES), I32),
         ],
-        [pay_pair, keep, parcel_vel, rate, cell, tiles],
-        scratch=deposit_scratch,
+        [pay, pay_far, keep, parcel_vel, rate, cell, tiles],
+        scratch=[pltpu.VMEM((N_Z, PAY_ROWS, 128), BF16)] + deposit_scratch,
         flops=1 << 36,
     )
     (sums,) = call(
@@ -678,8 +684,8 @@
         scratch=[pltpu.SMEM((1, TILES), I32), pltpu.SemaphoreType.DMA((1,))],
         flops=1 << 31,
     )
-    arrivals = jnp.stack([arrive0, arrive1], axis=1).transpose(1, 0, 2)
-    return fluid_next, pressure_next, parcel_next, arrivals
+    (arrivals,) = call(join_kernel, [((5, 2, MIG), F32)], [arrive0, arrive1])
+    return fluid_next, pressure_next, parcel_next, arrivals.transpose(1, 0, 2)
 
 
 def solution(mesh):

time: 99.7 us -> 102 us (1.023)
  waiting for transfers between devices: 11.9 us -> 15.3 us
  Pallas kernels: 17.7 us -> 19 us
    ppermute x1, waiting for transfers between devices: 0.01 us -> 2.73 us  [per_device(): arrive1 = lax.ppermute(out1, ALL, leave_route(1))]
    pallas_call x12 -> x13, Pallas kernels: 17.7 us -> 19 us  [call(): pl.pallas_call(kernel, out_shape=[jax.ShapeDtypeStruct(shape, dtype) for...]
    ppermute x6, starting transfers between devices: 36.4 us -> 35.4 us  [swap(): return lax.ppermute(values, axis, [(0, 1), (1, 0)])]
  transfers between devices with their start and end apart: 12 -> 12, of which waited for: 3 -> 4; matrix products, arithmetic and copies ran while one was open for 0% -> 0% of each run, Pallas kernels for 14% -> 15%
where the time goes in v8:
time: 102 us
  starting transfers between devices  58.8 us (58%)
  Pallas kernels  19 us (19%)
  waiting for transfers between devices  15.3 us (15%)
  blocking collectives  6.44 us (6%)
  between operations  1.53 us (2%)
    ppermute x6, starting transfers between devices, swap(): return lax.ppermute(values, axis, [(0, 1), (1, 0)])  35.4 us
    pallas_call x13, Pallas kernels, call(): pl.pallas_call(kernel, out_shape=[jax.ShapeDtypeStruct(shape, dtype) for...  19 us
    ppermute x6, waiting for transfers between devices, swap(): return lax.ppermute(values, axis, [(0, 1), (1, 0)])  9.56 us
    ppermute x1, starting transfers between devices, per_device(): arrive0 = lax.ppermute(out0, ALL, leave_route(-1))  6.48 us
    all_gather x1, blocking collectives, per_device(): from_c = lax.all_gather(flux_c, 'c', axis=0)  6.44 us
    all_to_all x1, starting transfers between devices, per_device(): fields = lax.all_to_all(fields, 'y', 0, 0)  5.43 us
    all_to_all x1, starting transfers between devices, per_device(): pays = lax.all_to_all(pays, 'y', 0, 0)  4.33 us
    ppermute x1, starting transfers between devices, per_device(): edge = lax.ppermute(edge, ALL, route)  3.34 us
  transfers between devices with their start and end apart: 12, of which 4 were waited for; matrix products, arithmetic and copies ran while one was open for 0% of the time, Pallas kernels for 15%

profile of v8, /device:TPU:1, one launch (start us, length us, event | category | flops | bytes accessed | tf_op | source)
XLA Modules:
  0.0 101.7 jit_solution(1622219929242849125)
XLA Ops:
  1.3 1.7 %shard_map.129.own = bf16[400,128]{1,0:T(8,128)(2,1)} custom-call(f32[3,8192]{1,0:T(4,128)} %refs_1_.1, f32[64,128]{1,0:T(8,128)} %bitcast.24, f32[64,128]{1,0:T(8,128)} %bitcast.14, s32[64,128]{1,0:T(8,128)} %bitcast.17, s32[1,32]{1,0:T(1,128)} %bitcast.20, s32[1,1]{1,0:T(1,128)} %bitcast.10.refs_5_), custom_call_target="tpu_custom_call" | custom-call | bytes 1048576 | tf_op jit(solution)/shard_map/pallas_call | solution.py:83
  3.0 16.3 %collective-permute-start = (bf16[400,128]{1,0:T(8,128)(2,1)}, bf16[400,128]{1,0:T(8,128)(2,1)S(1)}, u32[]{:S(2)}, u32[]{:S(2)}) collective-permute-start(bf16[400,128]{1,0:T(8,128)(2,1)} %shard_map.129.own), channel_id=1, source_target_pairs={{0,2},{2,0},{1,3},{3,1},{4,6},{6,4},{5,7},{7,5},{8,10},{10,8},{9,1... | collective-permute-start | bytes 307208 | tf_op jit(solution)/shard_map/ppermute | solution.py:75
  19.3 2.4 %shard_map.131 = (f32[9,16,256]{2,1,0:T(8,128)}, f32[64,128]{1,0:T(8,128)}, s16[14,16,256]{2,1,0:T(8,128)(2,1)}) custom-call(f32[3,8192]{1,0:T(4,128)} %refs_1_.1, f32[64,128]{1,0:T(8,128)} %bitcast.25, f32[64,128]{1,0:T(8,128)} %bitcast.15, s32[64,128]{1,0:T(8,128)} %bitcast.18, s32[1,32]{1,0:T(1,128)} %bitcast.21, s32[1,1]{1,0:T(1,128)} %bitcast.11.refs_5_, ...), custom_call_target="tpu_custom_call" | custom-call | bytes 1048576 | tf_op jit(solution)/shard_map/pallas_call | solution.py:83
  21.7 1.9 %collective-permute-start.2 = (s16[14,16,256]{2,1,0:T(8,128)(2,1)}, s16[14,16,256]{2,1,0:T(8,128)(2,1)S(1)}, u32[]{:S(2)}, u32[]{:S(2)}) collective-permute-start(s16[14,16,256]{2,1,0:T(8,128)(2,1)} %get-tuple-element.31), channel_id=1, source_target_pairs={{0,2},{2,0},{1,3},{3,1},{4,6},{6,4},{5,7},{7,5},{8,10},{10,8},{9,1... | collective-permute-start | bytes 344072 | tf_op jit(solution)/shard_map/ppermute | solution.py:75
  24.6 4.3 %all-to-all-start = ((bf16[4,2,400,128]{3,2,1,0:T(8,128)(2,1)}), bf16[4,2,400,128]{3,2,1,0:T(8,128)(2,1)S(1)}, u32[]{:S(2)}, u32[]{:S(2)}) async-start(bf16[4,2,400,128]{3,2,1,0:T(8,128)(2,1)} %shard_map.130), calls=%async_computation | async-start | bytes 1638400 | tf_op jit(solution)/shard_map/all_to_all | solution.py:600
  30.9 9.3 %collective-permute-done.2.coded = s16[14,16,256]{2,1,0:T(8,128)(2,1)S(1)} collective-permute-done((s16[14,16,256]{2,1,0:T(8,128)(2,1)}, s16[14,16,256]{2,1,0:T(8,128)(2,1)S(1)}, u32[]{:S(2)}, u32[]{:S(2)}) %collective-permute-start.2) | collective-permute-done | bytes 114720 | tf_op jit(solution)/shard_map/ppermute | solution.py:75
  40.2 2.5 %collective-permute-start.3 = (f32[9,16,256]{2,1,0:T(8,128)S(1)}, f32[9,16,256]{2,1,0:T(8,128)S(1)}, u32[]{:S(2)}, u32[]{:S(2)}) collective-permute-start(f32[9,16,256]{2,1,0:T(8,128)S(1)} %get-tuple-element.33), channel_id=1, source_target_pairs={{0,1},{1,0},{2,3},{3,2},{4,5},{5,4},{6,7},{7,6},{8,9},{9,8},{10,11... | collective-permute-start | bytes 442376 | tf_op jit(solution)/shard_map/ppermute | solution.py:75
  42.7 3.3 %collective-permute-start.4 = (f32[4,16,256]{2,1,0:T(8,128)S(1)}, f32[4,16,256]{2,1,0:T(8,128)S(1)}, u32[]{:S(2)}, u32[]{:S(2)}) collective-permute-start(f32[4,16,256]{2,1,0:T(8,128)S(1)} %get-tuple-element.34), channel_id=1, source_target_pairs={{1,4},{4,1},{3,6},{6,3},{5,8},{8,5},{7,10},{10,7},{9,12},{12,9},{1... | collective-permute-start | bytes 196616 | tf_op jit(solution)/shard_map/ppermute | solution.py:638
  46.1 5.4 %collective-permute-start.1 = (bf16[4,2,400,128]{3,2,1,0:T(8,128)(2,1)S(1)}, bf16[4,2,400,128]{3,2,1,0:T(8,128)(2,1)S(1)}, u32[]{:S(2)}, u32[]{:S(2)}) collective-permute-start(bf16[4,2,400,128]{3,2,1,0:T(8,128)(2,1)S(1)} %all-to-all-done), channel_id=1, source_target_pairs={{0,1},{1,0},{2,3},{3,2},{4,5},{5,4},{6,7},{7,6},{8,9},{9,8},{10,11... | collective-permute-start | bytes 2457608 | tf_op jit(solution)/shard_map/ppermute | solution.py:75
  51.5 2.2 %shard_map.133.before = f32[9,80,128]{2,1,0:T(8,128)S(1)} custom-call(bf16[8,400,128]{2,1,0:T(8,128)(2,1)S(1)} %bitcast.13, f32[9,80,128]{2,1,0:T(8,128)S(1)} %get-tuple-element.29.before), custom_call_target="tpu_custom_call" | custom-call | flops 68719476736 | bytes 1048576 | tf_op jit(solution)/shard_map/pallas_call | solution.py:83
  53.7 2.5 %shard_map.134.acc = f32[9,80,128]{2,1,0:T(8,128)S(1)} custom-call(bf16[8,400,128]{2,1,0:T(8,128)(2,1)S(1)} %bitcast.23, f32[9,80,128]{2,1,0:T(8,128)S(1)} %shard_map.133.before), custom_call_target="tpu_custom_call" | custom-call | flops 68719476736 | bytes 1048576 | tf_op jit(solution)/shard_map/pallas_call | solution.py:83
  56.6 1.9 %collective-permute-start.5 = (f32[12,16,256]{2,1,0:T(8,128)S(1)}, f32[12,16,256]{2,1,0:T(8,128)S(1)}, u32[]{:S(2)}, u32[]{:S(2)}) collective-permute-start(f32[12,16,256]{2,1,0:T(8,128)S(1)} %get-tuple-element.37), channel_id=1, source_target_pairs={{1,4},{4,1},{3,6},{6,3},{5,8},{8,5},{7,10},{10,7},{9,12},{12,9},{1... | collective-permute-start | bytes 589832 | tf_op jit(solution)/shard_map/ppermute | solution.py:652
  58.5 6.4 %all-gather = f32[18,16,256]{2,1,0:T(8,128)S(1)} all-gather(f32[9,16,256]{2,1,0:T(8,128)S(1)} %get-tuple-element.38), channel_id=2, replica_groups=mesh['blk'=32,'y'=4,'z'=2,'c'=2] {'c'}, dimensions={0}, use_global_device_ids=true | all-gather | bytes 442368 | tf_op jit(solution)/shard_map/all_gather | solution.py:653
  65.0 1.3 %shard_map.137 = (bf16[4,8,64,128]{3,2,1,0:T(8,128)(2,1)}, f32[4,2,16,256]{3,2,1,0:T(8,128)S(1)}, f32[4,2,16,256]{3,2,1,0:T(8,128)S(1)}) custom-call(f32[3,4,16,256]{3,2,1,0:T(8,128)S(1)} %get-tuple-element.35.u_in, f32[4,16,256]{2,1,0:T(8,128)S(1)} %get-tuple-element.36.por_in, f32[9,16,256]{2,1,0:T(8,128)S(1)} %copy-done, ...), custom_call_target="tpu_custom_call" | custom-call | bytes 1048576 | tf_op jit(solution)/shard_map/pallas_call | solution.py:83
  66.3 5.4 %all-to-all-start.1 = ((bf16[4,8,64,128]{3,2,1,0:T(8,128)(2,1)}), bf16[4,8,64,128]{3,2,1,0:T(8,128)(2,1)S(1)}, u32[]{:S(2)}, u32[]{:S(2)}) async-start(bf16[4,8,64,128]{3,2,1,0:T(8,128)(2,1)} %get-tuple-element.39), calls=%async_computation.1 | async-start | bytes 1048576 | tf_op jit(solution)/shard_map/all_to_all | solution.py:664
  71.7 4.1 %collective-permute-start.7 = (f32[4,2,16,256]{3,2,1,0:T(8,128)S(1)}, f32[4,2,16,256]{3,2,1,0:T(8,128)S(1)}, u32[]{:S(2)}, u32[]{:S(2)}) collective-permute-start(f32[4,2,16,256]{3,2,1,0:T(8,128)S(1)} %get-tuple-element.46), channel_id=1, source_target_pairs={{0,1},{1,0},{2,3},{3,2},{4,5},{5,4},{6,7},{7,6},{8,9},{9,8},{10,11... | collective-permute-start | bytes 393224 | tf_op jit(solution)/shard_map/ppermute | solution.py:75
  75.8 3.0 %all-to-all-done.1.near = bf16[4,8,64,128]{3,2,1,0:T(8,128)(2,1)S(1)} async-done(((bf16[4,8,64,128]{3,2,1,0:T(8,128)(2,1)}), bf16[4,8,64,128]{3,2,1,0:T(8,128)(2,1)S(1)}, u32[]{:S(2)}, u32[]{:S(2)}) %all-to-all-start.1) | async-done | bytes 524320 | tf_op jit(solution)/shard_map/all_to_all | solution.py:664
  78.8 5.2 %collective-permute-start.6 = (bf16[4,8,64,128]{3,2,1,0:T(8,128)(2,1)S(1)}, bf16[4,8,64,128]{3,2,1,0:T(8,128)(2,1)S(1)}, u32[]{:S(2)}, u32[]{:S(2)}) collective-permute-start(bf16[4,8,64,128]{3,2,1,0:T(8,128)(2,1)S(1)} %all-to-all-done.1.near), channel_id=1, source_target_pairs={{0,1},{1,0},{2,3},{3,2},{4,5},{5,4},{6,7},{7,6},{8,9},{9,8},{10,11... | collective-permute-start | bytes 1572872 | tf_op jit(solution)/shard_map/ppermute | solution.py:75
  84.1 1.3 %shard_map.139.half = f32[64,512]{1,0:T(8,128)S(1)} custom-call(bf16[4,8,64,128]{3,2,1,0:T(8,128)(2,1)S(1)} %all-to-all-done.1.near, f32[9,16,256]{2,1,0:T(8,128)S(1)} %copy-done, f32[9,16,256]{2,1,0:T(8,128)S(1)} %get-tuple-element.32.far), custom_call_target="tpu_custom_call" | custom-call | flops 68719476736 | bytes 1048576 | tf_op jit(solution)/shard_map/pallas_call | solution.py:83
  85.6 1.3 %shard_map.140 = (f32[5,256]{1,0:T(8,128)S(1)}, f32[5,256]{1,0:T(8,128)S(1)}) custom-call(bf16[4,8,64,128]{3,2,1,0:T(8,128)(2,1)S(1)} %collective-permute-done.6.other, f32[9,16,256]{2,1,0:T(8,128)S(1)} %copy-done, f32[9,16,256]{2,1,0:T(8,128)S(1)} %get-tuple-element.32.far, f32[64,512]{1,0:T(8,128)S(1)} %shard_map.139.half), custom_call_target="tpu_custom_call" | custom-call | bytes 1048576 | tf_op jit(solution)/shard_map/pallas_call | solution.py:83
  86.9 6.5 %collective-permute-start.8 = (f32[5,256]{1,0:T(8,128)S(1)}, f32[5,256]{1,0:T(8,128)S(1)}, u32[]{:S(2)}, u32[]{:S(2)}) collective-permute-start(f32[5,256]{1,0:T(8,128)S(1)} %get-tuple-element.50), channel_id=1, source_target_pairs={{2,496},{3,497},{0,498},{1,499},{6,500},{7,501},{4,502},{5,503},{1... | collective-permute-start | bytes 15368 | tf_op jit(solution)/shard_map/ppermute | solution.py:678
  93.4 1.9 %collective-permute-start.9 = (f32[5,256]{1,0:T(8,128)S(1)}, f32[5,256]{1,0:T(8,128)S(1)}, u32[]{:S(2)}, u32[]{:S(2)}) collective-permute-start(f32[5,256]{1,0:T(8,128)S(1)} %get-tuple-element.51), channel_id=1, source_target_pairs={{0,16},{1,17},{2,18},{3,19},{4,20},{5,21},{6,22},{7,23},{8,24},{9,... | collective-permute-start | bytes 15368 | tf_op jit(solution)/shard_map/ppermute | solution.py:679
  95.3 3.0 %shard_map.138 = (f32[3,8192]{1,0:T(4,128)}, f32[3,2,16,256]{3,2,1,0:T(8,128)}, f32[2,16,256]{2,1,0:T(8,128)}) custom-call(bf16[4,8,64,128]{3,2,1,0:T(8,128)(2,1)S(1)} %all-to-all-done.1.near, bf16[4,8,64,128]{3,2,1,0:T(8,128)(2,1)S(1)} %collective-permute-done.6.other, s32[1,32]{1,0:T(1,128)S(1)} %get-tuple-element.40.tiles_in, ...), custom_call_target="tpu_custom_call" | custom-call | flops 2147483648 | bytes 1048576 | tf_op jit(solution)/shard_map/pallas_call | solution.py:83
  98.4 2.7 %collective-permute-done.9.second = f32[5,256]{1,0:T(8,128)S(1)} collective-permute-done((f32[5,256]{1,0:T(8,128)S(1)}, f32[5,256]{1,0:T(8,128)S(1)}, u32[]{:S(2)}, u32[]{:S(2)}) %collective-permute-start.9) | collective-permute-done | bytes 5152 | tf_op jit(solution)/shard_map/ppermute | solution.py:679
  (28 shorter events, 4.2 us)
Async XLA Ops:
  3.0 20.6 %collective-permute-start = (bf16[400,128]{1,0:T(8,128)(2,1)}, bf16[400,128]{1,0:T(8,128)(2,1)S(1)}, u32[]{:S(2)}, u32[]{:S(2)}) collective-permute-start(bf16[400,128]{1,0:T(8,128)(2,1)} %shard_map.129.own), channel_id=1, source_target_pairs={{0,2},{2,0},{1,3},{3,1},{4,6},{6,4},{5,7},{7,5},{8,10},{10,8},{9,1... | collective-permute-start | bytes 307208 | tf_op jit(solution)/shard_map/ppermute | solution.py:75
  19.3 4.3 %copy-start.2 = (bf16[400,128]{1,0:T(8,128)(2,1)S(1)}, bf16[400,128]{1,0:T(8,128)(2,1)}, u32[]{:S(2)}) copy-start(bf16[400,128]{1,0:T(8,128)(2,1)} %shard_map.129.own) | copy-start | bytes 307204
  21.7 18.5 %collective-permute-start.2 = (s16[14,16,256]{2,1,0:T(8,128)(2,1)}, s16[14,16,256]{2,1,0:T(8,128)(2,1)S(1)}, u32[]{:S(2)}, u32[]{:S(2)}) collective-permute-start(s16[14,16,256]{2,1,0:T(8,128)(2,1)} %get-tuple-element.31), channel_id=1, source_target_pairs={{0,2},{2,0},{1,3},{3,1},{4,6},{6,4},{5,7},{7,5},{8,10},{10,8},{9,1... | collective-permute-start | bytes 344072 | tf_op jit(solution)/shard_map/ppermute | solution.py:75
  24.6 4.3 %copy-start.1 = (f32[3,8192]{1,0:T(4,128)S(1)}, f32[3,8192]{1,0:T(4,128)}, u32[]{:S(2)}) copy-start(f32[3,8192]{1,0:T(4,128)} %refs_1_.1) | copy-start | bytes 294916
  24.6 4.3 %copy-start.3 = (f32[8192]{0:T(1024)S(1)}, f32[8192]{0:T(1024)}, u32[]{:S(2)}) copy-start(f32[8192]{0:T(1024)} %param.14) | copy-start | bytes 98308
  24.6 4.3 %copy-start.4 = (s32[8192]{0:T(1024)S(1)}, s32[8192]{0:T(1024)}, u32[]{:S(2)}) copy-start(s32[8192]{0:T(1024)} %param.15) | copy-start | bytes 98308
  24.6 4.4 %copy-start.6 = (f32[64,128]{1,0:T(8,128)S(1)}, f32[64,128]{1,0:T(8,128)}, u32[]{:S(2)}) copy-start(f32[64,128]{1,0:T(8,128)} %get-tuple-element.28.refs_0_) | copy-start | bytes 98308
  24.6 21.4 %all-to-all-start = ((bf16[4,2,400,128]{3,2,1,0:T(8,128)(2,1)}), bf16[4,2,400,128]{3,2,1,0:T(8,128)(2,1)S(1)}, u32[]{:S(2)}, u32[]{:S(2)}) async-start(bf16[4,2,400,128]{3,2,1,0:T(8,128)(2,1)} %shard_map.130), calls=%async_computation | async-start | bytes 1638400 | tf_op jit(solution)/shard_map/all_to_all | solution.py:600
  29.0 0.7 copy-start.5
  29.6 10.5 %copy-start = (f32[9,16,256]{2,1,0:T(8,128)S(1)}, f32[9,16,256]{2,1,0:T(8,128)}, u32[]{:S(2)}) copy-start(f32[9,16,256]{2,1,0:T(8,128)} %get-tuple-element.30.own) | copy-start | bytes 442372
  40.2 16.0 %collective-permute-start.3 = (f32[9,16,256]{2,1,0:T(8,128)S(1)}, f32[9,16,256]{2,1,0:T(8,128)S(1)}, u32[]{:S(2)}, u32[]{:S(2)}) collective-permute-start(f32[9,16,256]{2,1,0:T(8,128)S(1)} %get-tuple-element.33), channel_id=1, source_target_pairs={{0,1},{1,0},{2,3},{3,2},{4,5},{5,4},{6,7},{7,6},{8,9},{9,8},{10,11... | collective-permute-start | bytes 442376 | tf_op jit(solution)/shard_map/ppermute | solution.py:75
  42.7 13.5 %collective-permute-start.4 = (f32[4,16,256]{2,1,0:T(8,128)S(1)}, f32[4,16,256]{2,1,0:T(8,128)S(1)}, u32[]{:S(2)}, u32[]{:S(2)}) collective-permute-start(f32[4,16,256]{2,1,0:T(8,128)S(1)} %get-tuple-element.34), channel_id=1, source_target_pairs={{1,4},{4,1},{3,6},{6,3},{5,8},{8,5},{7,10},{10,7},{9,12},{12,9},{1... | collective-permute-start | bytes 196616 | tf_op jit(solution)/shard_map/ppermute | solution.py:638
  46.1 7.6 %collective-permute-start.1 = (bf16[4,2,400,128]{3,2,1,0:T(8,128)(2,1)S(1)}, bf16[4,2,400,128]{3,2,1,0:T(8,128)(2,1)S(1)}, u32[]{:S(2)}, u32[]{:S(2)}) collective-permute-start(bf16[4,2,400,128]{3,2,1,0:T(8,128)(2,1)S(1)} %all-to-all-done), channel_id=1, source_target_pairs={{0,1},{1,0},{2,3},{3,2},{4,5},{5,4},{6,7},{7,6},{8,9},{9,8},{10,11... | collective-permute-start | bytes 2457608 | tf_op jit(solution)/shard_map/ppermute | solution.py:75
  56.6 8.4 %collective-permute-start.5 = (f32[12,16,256]{2,1,0:T(8,128)S(1)}, f32[12,16,256]{2,1,0:T(8,128)S(1)}, u32[]{:S(2)}, u32[]{:S(2)}) collective-permute-start(f32[12,16,256]{2,1,0:T(8,128)S(1)} %get-tuple-element.37), channel_id=1, source_target_pairs={{1,4},{4,1},{3,6},{6,3},{5,8},{8,5},{7,10},{10,7},{9,12},{12,9},{1... | collective-permute-start | bytes 589832 | tf_op jit(solution)/shard_map/ppermute | solution.py:652
  66.3 12.5 %all-to-all-start.1 = ((bf16[4,8,64,128]{3,2,1,0:T(8,128)(2,1)}), bf16[4,8,64,128]{3,2,1,0:T(8,128)(2,1)S(1)}, u32[]{:S(2)}, u32[]{:S(2)}) async-start(bf16[4,8,64,128]{3,2,1,0:T(8,128)(2,1)} %get-tuple-element.39), calls=%async_computation.1 | async-start | bytes 1048576 | tf_op jit(solution)/shard_map/all_to_all | solution.py:664
  71.7 23.6 %collective-permute-start.7 = (f32[4,2,16,256]{3,2,1,0:T(8,128)S(1)}, f32[4,2,16,256]{3,2,1,0:T(8,128)S(1)}, u32[]{:S(2)}, u32[]{:S(2)}) collective-permute-start(f32[4,2,16,256]{3,2,1,0:T(8,128)S(1)} %get-tuple-element.46), channel_id=1, source_target_pairs={{0,1},{1,0},{2,3},{3,2},{4,5},{5,4},{6,7},{7,6},{8,9},{9,8},{10,11... | collective-permute-start | bytes 393224 | tf_op jit(solution)/shard_map/ppermute | solution.py:75
  78.8 6.8 %collective-permute-start.6 = (bf16[4,8,64,128]{3,2,1,0:T(8,128)(2,1)S(1)}, bf16[4,8,64,128]{3,2,1,0:T(8,128)(2,1)S(1)}, u32[]{:S(2)}, u32[]{:S(2)}) collective-permute-start(bf16[4,8,64,128]{3,2,1,0:T(8,128)(2,1)S(1)} %all-to-all-done.1.near), channel_id=1, source_target_pairs={{0,1},{1,0},{2,3},{3,2},{4,5},{5,4},{6,7},{7,6},{8,9},{9,8},{10,11... | collective-permute-start | bytes 1572872 | tf_op jit(solution)/shard_map/ppermute | solution.py:75
  86.9 11.5 %collective-permute-start.8 = (f32[5,256]{1,0:T(8,128)S(1)}, f32[5,256]{1,0:T(8,128)S(1)}, u32[]{:S(2)}, u32[]{:S(2)}) collective-permute-start(f32[5,256]{1,0:T(8,128)S(1)} %get-tuple-element.50), channel_id=1, source_target_pairs={{2,496},{3,497},{0,498},{1,499},{6,500},{7,501},{4,502},{5,503},{1... | collective-permute-start | bytes 15368 | tf_op jit(solution)/shard_map/ppermute | solution.py:678
  93.4 7.7 %collective-permute-start.9 = (f32[5,256]{1,0:T(8,128)S(1)}, f32[5,256]{1,0:T(8,128)S(1)}, u32[]{:S(2)}, u32[]{:S(2)}) collective-permute-start(f32[5,256]{1,0:T(8,128)S(1)} %get-tuple-element.51), channel_id=1, source_target_pairs={{0,16},{1,17},{2,18},{3,19},{4,20},{5,21},{6,22},{7,23},{8,24},{9,... | collective-permute-start | bytes 15368 | tf_op jit(solution)/shard_map/ppermute | solution.py:679
